TPU v7x, 32 devices: a whole 2x2x4 slice. The times are simulated.
32 devices in a mesh: replica: 4 (over z), fsdp: 8 (over y, x, core).
Axes of the slice: x: 2, y: 2, z: 4, core: 2. Of those that a mesh axis runs over, the one named last changes fastest.
Arguments:
- hidden_states: bfloat16 [32768, 4096], P(('replica', 'fsdp')), may hold values from -6 to 6
- cotangent: bfloat16 [32768, 1024], P(('replica', 'fsdp')), may hold values from -0.0625 to 0.0625
- key_weight: bfloat16 [4, 4096, 1024], P('replica', 'fsdp'), may hold values from -0.09375 to 0.09375
- local_fragments: bfloat16 [4, 2, 4, 4096, 1024], P('replica', None, None, 'fsdp'), may hold values from -6 to 6
- global_fragments: float32 [2, 4, 4096, 1024], P(None, None, 'fsdp', 'replica'), may hold values from -6 to 6
- momentum: float32 [2, 4, 4096, 1024], P(None, None, 'fsdp', 'replica'), may hold values from -3 to 3
- fragment_index: int32 [1], replicated, may hold values from 0 to 4095
Outputs:
- projected: bfloat16 [32768, 1024], P(('replica', 'fsdp'))
- weight_grad: float32 [4, 4096, 1024], P('replica', 'fsdp')
- new_global: float32 [2, 4, 4096, 1024], P(None, None, 'fsdp', 'replica')
- new_momentum: float32 [2, 4, 4096, 1024], P(None, None, 'fsdp', 'replica')
- synced: bfloat16 [4, 4096, 1024], P(None, 'fsdp')
All inputs are finite; a program needn't handle non-finite values.
Results may differ from a plain program's by a relative error of at most 0.0095.
Values may be sent and summed in bfloat16 or wider, within the bound.
No kernel may reach another device: no remote copies, remote signals or barrier semaphores. Data moves between devices by JAX's collectives and lax.ppermute only.
A program may use at most 192 MiB of HBM per device.

v0:
```python
import jax
import jax.numpy as jnp
from jax import lax
from jax.sharding import PartitionSpec as P

FRAGS = 2


def shards(
    hidden_states,
    cotangent,
    key_weight,
    local_fragments,
    global_fragments,
    momentum,
    fragment_index,
):
    weight_rows = key_weight[0]
    columns = hidden_states
    projected = jnp.dot(
        columns,
        lax.all_gather(weight_rows, "fsdp", axis=0, tiled=True),
        preferred_element_type=jnp.float32,
    ).astype(jnp.bfloat16)
    columns = hidden_states
    weight_grad = lax.psum_scatter(
        lax.dot_general(
            columns, cotangent, (((0,), (0,)), ((), ())), preferred_element_type=jnp.float32
        ),
        "fsdp",
        scatter_dimension=0,
        tiled=True,
    )[None]
    chosen = fragment_index[0] % FRAGS
    replicas = lax.axis_size("replica")
    own_replica = lax.axis_index("replica")
    local_chosen = lax.dynamic_index_in_dim(local_fragments[0], chosen, 0, keepdims=False).astype(
        jnp.float32
    )
    width = global_fragments.shape[3]
    summed = lax.psum(local_chosen.astype(jnp.bfloat16), "replica").astype(jnp.float32)
    summed = lax.dynamic_slice_in_dim(summed, own_replica * width, width, 2)
    mean_local = summed / replicas
    global_chosen = lax.dynamic_index_in_dim(global_fragments, chosen, 0, keepdims=False)
    moment_chosen = lax.dynamic_index_in_dim(momentum, chosen, 0, keepdims=False)
    pseudo = global_chosen - mean_local
    moment_next = 0.9 * moment_chosen + pseudo
    global_next = global_chosen - 0.7 * (pseudo + 0.9 * moment_next)
    new_momentum = lax.dynamic_update_index_in_dim(momentum, moment_next, chosen, 0)
    new_global = lax.dynamic_update_index_in_dim(global_fragments, global_next, chosen, 0)
    synced = lax.all_gather(global_next.astype(jnp.bfloat16), "replica", axis=2, tiled=True)
    return (projected, weight_grad, new_global, new_momentum, synced)


def solution(mesh):
    placed = (
        P(("replica", "fsdp"), None),
        P(("replica", "fsdp"), None),
        P("replica", "fsdp", None),
        P("replica", None, None, "fsdp", None),
        P(None, None, "fsdp", "replica"),
        P(None, None, "fsdp", "replica"),
        P(),
    )
    return jax.shard_map(
        shards,
        mesh=mesh,
        in_specs=placed,
        out_specs=(
            P(("replica", "fsdp"), None),
            P("replica", "fsdp", None),
            P(None, None, "fsdp", "replica"),
            P(None, None, "fsdp", "replica"),
            P(None, "fsdp", None),
        ),
        check_vma=False,
    )
```

profile of v0, /device:TPU:0, one launch (start us, length us, event | category | flops | bytes accessed | tf_op | source)
XLA Modules:
  0.0 448.9 jit_solution(1912092872447370985)
XLA Ops:
  7.2 0.0 copy-start
  7.2 0.0 all-reduce.2.cloned.1.call-start
  7.2 0.0 copy-start.3
  7.2 4.7 %copy.20 = f32[2,4,512,256]{3,2,1,0:T(8,128)} copy(f32[2,4,512,256]{3,2,1,0:T(8,128)} %param.12) | data formatting | bytes 8388608
  11.9 0.0 copy-done.3
  11.9 2.0 copy.19
  14.6 4.6 %dynamic-slice_bitcast_fusion = bf16[4,512,1024]{2,1,0:T(8,128)(2,1)} fusion(bf16[1,2,4,512,1024]{4,3,2,1,0:T(8,128)(2,1)} %param.10, s32[]{:T(128)S(6)} %select_n.21), kind=kLoop, calls=%fused_computation.2 | loop fusion | bytes 8388612 | tf_op jit(solution)/shard_map/jit(dynamic_index_in_dim)/squeeze | solution.py:37
  19.2 0.0 all-reduce.2.cloned.1.call-update
  19.2 0.0 all-gather.4.cloned.1.call-start
  19.3 157.8 %all-reduce.2.cloned.1.call-done = bf16[4,512,1024]{2,1,0:T(8,128)(2,1)} async-done(((bf16[4,512,1024]{2,1,0:T(8,128)(2,1)}), bf16[4,512,1024]{2,1,0:T(8,128)(2,1)}) %all-reduce.2.cloned.1.call-update) | async-done | bytes 4194320 | tf_op jit(solution)/shard_map/psum | solution.py:41
  177.1 5.6 %fusion.5 = (bf16[4,512,256]{2,1,0:T(8,128)(2,1)}, f32[4,512,256]{2,1,0:T(8,128)}, f32[4,512,256]{2,1,0:T(8,128)}) fusion(bf16[4,512,1024]{2,1,0:T(8,128)(2,1)} %all-reduce.2.cloned.1.call-done, s32[]{:T(128)S(6)} %select_n.22, f32[2,4,512,256]{3,2,1,0:T(8,128)} %copy.19, s32[]{:T(128)S(6)} %select_n.21, f32[2,4,512,256]{3,2,1,0:T(8,128)} %copy.20), kind=kLoop, calls=%fused_computation.9 | loop fusion | flops 5242880 | bytes 10485768 | tf_op jit(solution)/shard_map/convert_element_type | solution.py:51
  182.7 0.0 all-gather.4.cloned.1.call-update
  182.7 0.0 all-gather.6.cloned.1.call-start
  182.8 0.7 all-gather.6.cloned.1.call-update
  183.5 0.0 reduce-scatter.2.cloned.1.call-start
  183.5 0.0 copy-done
  183.5 14.6 %fusion.6 = f32[4096,1024]{1,0:T(8,128)} fusion(bf16[1024,4096]{1,0:T(8,128)(2,1)} %param.7, bf16[1024,1024]{1,0:T(8,128)(2,1)S(1)} %copy-done), kind=kOutput, calls=%fused_computation.10 | convolution fusion | flops 8589934592 | bytes 27262976 | tf_op jit(solution)/shard_map/dot_general | solution.py:27
  198.1 0.0 copy-start.2
  198.1 0.0 reduce-scatter.2.cloned.1.call-update
  198.1 1.6 copy-done.2
  199.7 3.9 bitcast_dynamic-update-slice_fusion
  203.6 58.9 %all-gather.4.cloned.1.call-done = bf16[4,512,1024]{2,1,0:T(8,128)(2,1)} async-done(((bf16[4,512,256]{2,1,0:T(8,128)(2,1)}), bf16[4,512,1024]{2,1,0:T(8,128)(2,1)}) %all-gather.4.cloned.1.call-update) | async-done | bytes 4194320 | tf_op jit(solution)/shard_map/all_gather | solution.py:51
  262.5 54.7 %all-gather.6.cloned.1.call-done = bf16[1,4096,1024]{2,1,0:T(8,128)(2,1)} async-done(((bf16[1,512,1024]{2,1,0:T(8,128)(2,1)}), bf16[1,4096,1024]{2,1,0:T(8,128)(2,1)}) %all-gather.6.cloned.1.call-update) | async-done | bytes 8388624 | tf_op jit(solution)/shard_map/all_gather | solution.py:22
  317.1 14.6 %fusion.2 = bf16[1024,1024]{1,0:T(8,128)(2,1)} fusion(bf16[1024,4096]{1,0:T(8,128)(2,1)} %param.7, bf16[1,4096,1024]{2,1,0:T(8,128)(2,1)} %all-gather.6.cloned.1.call-done), kind=kOutput, calls=%fused_computation.8 | convolution fusion | flops 8590983168 | bytes 18874368 | tf_op jit(solution)/shard_map/dot_general | solution.py:20
  331.7 105.8 %reduce-scatter.2.cloned.1.call-done = f32[512,1024]{1,0:T(8,128)} async-done(((f32[4096,1024]{1,0:T(8,128)}), f32[512,1024]{1,0:T(8,128)}) %reduce-scatter.2.cloned.1.call-update) | async-done | bytes 2097168 | tf_op jit(solution)/shard_map/reduce_scatter | solution.py:26
  437.6 0.0 copy-start.1
  437.6 4.8 %copy.21 = bf16[4,512,1024]{2,1,0:T(8,128)(2,1)} copy(bf16[4,512,1024]{2,1,0:T(8,128)(2,1)} %all-gather.4.cloned.1.call-done) | data formatting | bytes 8388608
  442.4 0.0 copy-done.1
Async XLA Ops:
  7.2 176.4 %copy-start = (bf16[1024,1024]{1,0:T(8,128)(2,1)S(1)}, bf16[1024,1024]{1,0:T(8,128)(2,1)}, u32[]{:S(2)}) copy-start(bf16[1024,1024]{1,0:T(8,128)(2,1)} %param.8) | copy-start | bytes 6291460
  7.2 169.9 %all-reduce.2.cloned.1.call-start = ((), (), s32[]{:S(2)}) async-start(), calls=%async_computation.2 | async-start | bytes 8388608 | tf_op jit(solution)/shard_map/psum | solution.py:41
  7.2 4.7 %copy-start.3 = (f32[2,4,512,256]{3,2,1,0:T(8,128)S(1)}, f32[2,4,512,256]{3,2,1,0:T(8,128)}, u32[]{:S(2)}) copy-start(f32[2,4,512,256]{3,2,1,0:T(8,128)} %param.11) | copy-start | bytes 12582916
  19.2 243.2 %all-gather.4.cloned.1.call-start = ((), (), s32[]{:S(2)}) async-start(), calls=%async_computation.3 | async-start | bytes 5242880 | tf_op jit(solution)/shard_map/all_gather | solution.py:51
  182.7 134.4 %all-gather.6.cloned.1.call-start = ((), (), s32[]{:S(2)}) async-start(), calls=%async_computation.4 | async-start | bytes 9437184 | tf_op jit(solution)/shard_map/all_gather | solution.py:22
  183.5 254.1 %reduce-scatter.2.cloned.1.call-start = ((), (), s32[]{:S(2)}) async-start(), calls=%async_computation.1 | async-start | bytes 18874368 | tf_op jit(solution)/shard_map/reduce_scatter | solution.py:26
  198.1 1.6 copy-start.2
  437.6 4.8 %copy-start.1 = (bf16[1024,1024]{1,0:T(8,128)(2,1)S(1)}, bf16[1024,1024]{1,0:T(8,128)(2,1)}, u32[]{:S(2)}) copy-start(bf16[1024,1024]{1,0:T(8,128)(2,1)} %param.8) | copy-start | bytes 6291460
Sparse Core Ops, SparseCore 0:
  19.4 157.6 all-reduce.1
  182.9 79.5 all-gather.3
  264.5 52.5 all-gather.5
  321.5 115.9 reduce-scatter.1
where the time goes:
time: 449 us
  waiting for transfers between devices  378 us (84%)
  matrix products  29.2 us (7%)
  local copies, waits for them, and re-layouts  21.6 us (5%)
  between operations  14.5 us (3%)
  other arithmetic  5.63 us (1%)
    psum x1, waiting for transfers between devices, shards(): lax.psum(local_chosen.astype(jnp.bfloat16), 'replica').astype(jnp.float32)  158 us
    reduce_scatter x1, waiting for transfers between devices, shards(): lax.psum_scatter(lax.dot_general(columns, cotangent, (((0,), (0,)), ((),...  106 us
    all_gather x1, waiting for transfers between devices, shards(): lax.all_gather(global_next.astype(jnp.bfloat16), 'replica', axis=2, tiled...  58.9 us
    all_gather x1, waiting for transfers between devices, shards(): lax.all_gather(weight_rows, 'fsdp', axis=0, tiled=True)  54.7 us
    dot_general x1, matrix products, shards(): jnp.dot(columns, lax.all_gather(weight_rows, 'fsdp', axis=0, tiled=True),...  14.6 us
    dot_general x1, matrix products, shards(): lax.dot_general(columns, cotangent, (((0,), (0,)), ((), ())), preferred_e...  14.6 us
    unnamed x11, local copies, waits for them, and re-layouts  13 us
  transfers between devices with their start and end apart: 4, of which 4 were waited for; matrix products, arithmetic and copies ran while one was open for 7% of the time, Pallas kernels for 0%

commit v1 on v0

v1 whole, which is shorter than its diff:
```python
import functools

import jax
import jax.numpy as jnp
from jax import lax
from jax.experimental import pallas as pl
from jax.experimental.pallas import tpu as pltpu
from jax.sharding import PartitionSpec as P

FRAGS = 2
PIECES = 10
STEPS = 1
DELAY = 2
PROJECT_BLOCKS = 4
MEAN_PART = 1.33
GLOBAL_PART = -0.33
MOMENT_PART = -0.567
F32 = jnp.float32
BF16 = jnp.bfloat16
ANY = pl.BlockSpec(memory_space=pl.ANY)
CONTRACT_ROWS = (((0,), (0,)), ((), ()))
CHOSEN, REPLICA, FSDP = 0, 1, 2
VMEM = 16 << 20
LONG = 1 << 30


def in_hbm(x):
    return pltpu.with_memory_space_constraint(x, pltpu.HBM)


class Chain:
    def __init__(self, scalars):
        self.scalars, self.token = scalars, None


def call(body, name, chain, operands, in_specs, out_shape, out_specs, grid, aliases=None, copies=(), cost=0):
    n_in, n_out, n = len(operands), len(out_shape), len(copies)
    aliases = dict(aliases or {})
    operands, in_specs = list(operands), list(in_specs)
    out_shape, out_specs = list(out_shape), list(out_specs)
    unread = []
    for k, (array, in_spec, space, shape, out_spec, into) in enumerate(copies):
        operands.append(array)
        in_specs.append(in_spec)
        out_shape.append(space(shape, array.dtype))
        out_specs.append(out_spec)
        if into is not None:
            aliases[1 + n_in + n + len(unread)] = n_out + k
            unread.append(into)
    if chain.token is not None:
        unread.append(chain.token)
    operands += unread
    out_shape.append(jax.ShapeDtypeStruct((8, 128), F32))

    def kernel(s, *refs):
        outs = refs[len(operands) :]
        body(s, *refs[:n_in], *outs[:n_out])
        for source, target in zip(refs[n_in : n_in + n], outs[n_out:]):
            target[...] = source[...].reshape(target.shape)

    *results, chain.token = pl.pallas_call(
        kernel,
        out_shape=out_shape,
        grid_spec=pltpu.PrefetchScalarGridSpec(
            num_scalar_prefetch=1,
            grid=grid,
            in_specs=in_specs + [ANY] * len(unread),
            out_specs=out_specs + [ANY],
        ),
        input_output_aliases=aliases,
        compiler_params=pltpu.CompilerParams(vmem_limit_bytes=VMEM),
        cost_estimate=pl.CostEstimate(flops=0, bytes_accessed=cost, transcendentals=0),
        name=name,
    )(chain.scalars, *operands)
    return results


class Fsdp:
    def __init__(self, hidden_states, cotangent, weight, chain):
        self.states, self.cotans = in_hbm(hidden_states), in_hbm(cotangent)
        self.tokens, self.model = hidden_states.shape
        self.keys = cotangent.shape[1]
        self.devices = lax.axis_size("fsdp")
        self.rows = self.model // self.devices
        self.chain = chain
        self.whole = pl.BlockSpec((self.tokens, self.keys), lambda i, s: (0, 0))
        self.weight = in_hbm(lax.all_gather(weight, "fsdp", axis=0, tiled=True))
        self.sums = None

    def project(self, part):
        block, depth = self.tokens // PROJECT_BLOCKS, self.model // 4
        first, final = part == 0, part == 3
        rows = pl.BlockSpec((block, self.keys), lambda i, s: (i, 0))
        operands = [self.states, self.weight]
        in_specs = [
            pl.BlockSpec((block, depth), lambda i, s: (i, part)),
            pl.BlockSpec((depth, self.keys), lambda i, s: (part, 0)),
        ]
        aliases = {}
        if not first:
            operands.append(self.total)
            in_specs.append(rows)
            aliases = {} if final else {3: 0}

        def body(s, states, weight, *refs):
            total = jnp.dot(states[...], weight[...], preferred_element_type=F32)
            if not first:
                total = total + refs[0][...]
            refs[-1][...] = total.astype(refs[-1].dtype)

        (self.total,) = call(
            body, f"project_{part}", self.chain, operands, in_specs,
            [pltpu.HBM((self.tokens, self.keys), BF16) if final else pltpu.VMEM((self.tokens, self.keys), F32)], [rows],
            (PROJECT_BLOCKS,), aliases,
        )

    def grad(self, first, n, copies=()):
        def body(s, states, cotans, *refs):
            refs[-1][0] = lax.dot_general(
                states[...], cotans[...], CONTRACT_ROWS, preferred_element_type=F32
            ).astype(BF16)

        operands = [self.states, self.cotans]
        in_specs = [pl.BlockSpec((self.tokens, self.rows), lambda i, s: (0, first + i)), self.whole]
        aliases = {}
        if self.sums is not None:
            operands.append(self.sums)
            in_specs.append(ANY)
            aliases = {3: 0}
        self.sums, *copied = call(
            body, f"grad_{first}", self.chain, operands, in_specs,
            [pltpu.HBM((self.devices, self.rows, self.keys), BF16)],
            [pl.BlockSpec((1, self.rows, self.keys), lambda i, s: (first + i, 0, 0))],
            (n,), aliases, copies=copies,
        )
        return copied

    def scatter(self):
        self.sums = lax.psum_scatter(
            self.sums.reshape(self.model, self.keys), "fsdp", scatter_dimension=0, tiled=True
        )

    def widen(self):
        def body(s, x, out):
            out[...] = x[...].astype(F32)

        each = pl.BlockSpec((self.rows // 2, self.keys), lambda i, s: (i, 0))
        (out,) = call(
            body, "widen", self.chain, [self.sums], [each], [pltpu.HBM((self.rows, self.keys), F32)], [each], (2,)
        )
        return out


def own_term(g, m, replicas):
    return (GLOBAL_PART * g + MOMENT_PART * m) * (replicas / MEAN_PART)


def by_replica(replicas, s, body):
    for z in range(replicas):
        pl.when(s[REPLICA] == z)(functools.partial(body, z))


def way(z, side):
    return (z - 1 + side) % 2


def hops_of(z, replicas):
    return z - 1, replicas - 2 - z


def first_body(replicas, s, l, g, m, out):
    width = g.shape[2]

    def body(z):
        if 0 < z < replicas - 1:
            return
        columns = slice(z * width, (z + 1) * width)
        out[...] = l[0]
        out[:, columns] = (l[0, :, columns].astype(F32) + own_term(g[0], m[0], replicas)).astype(BF16)

    by_replica(replicas, s, body)


def round_body(replicas, old_of, ways, outs, keep, s, *refs):
    refs = list(refs)
    take = lambda n: [refs.pop(0) for _ in range(n)]
    came = take(2)
    old = dict(zip(old_of, take(len(old_of))))
    sources = take(3), take(3)
    width = sources[0][1].shape[2]
    kept = take(3) if outs else ()
    targets = take(ways)
    results = take(3) if outs else ()

    def body(z):
        columns = slice(z * width, (z + 1) * width)
        hops = hops_of(z, replicas)
        for side in (0, 1):
            target = way(z, 1 - side)
            if hops[1 - side] < 0 or target >= ways:
                continue
            l, g, m = sources[side]
            out = targets[target]
            if hops[side] < 0:
                out[...] = l[0]
                mine = l[0, :, columns].astype(F32)
            else:
                total = came[way(z, side)][...].astype(F32) + l[0].astype(F32)
                out[...] = total.astype(BF16)
                mine = total[:, columns]
            out[:, columns] = (mine + own_term(g[0], m[0], replicas)).astype(BF16)
        if not outs:
            return
        reach = max(hops)
        if reach in keep:
            for ref, before in zip(results, kept):
                ref[...] = before[...]
            return
        l, g, m = sources[0 if hops[0] == reach else 1]
        total = l[0].astype(F32)
        for side in (0, 1):
            if hops[side] >= 0:
                path = way(z, side)
                total = total + old.get((path, reach - hops[side]), came[path])[...].astype(F32)
        synced, new_g, new_m = results
        synced[...] = (total * (MEAN_PART / replicas)).astype(BF16)
        mean = total[:, columns] / replicas
        pseudo = g[0] - mean
        moment = 0.9 * m[0] + pseudo
        after = g[0] - 0.7 * (pseudo + 0.9 * moment)
        synced[:, columns] = after.astype(BF16)
        new_g[0] = after
        new_m[0] = moment

    by_replica(replicas, s, body)


class Line:
    def __init__(self, local_fragments, global_fragments, momentum, chain):
        self.replicas = lax.axis_size("replica")
        frags, layers, rows, keys = local_fragments.shape
        self.given = global_fragments.shape
        self.layers, self.rows, self.keys = layers, rows, keys
        self.width = global_fragments.shape[3]
        self.total = layers * rows
        unit = 16 * STEPS
        self.chunk = -(-self.total // (unit * PIECES)) * unit
        self.block = self.chunk // STEPS
        self.pieces = -(-self.total // self.chunk)
        self.local = in_hbm(local_fragments.reshape(frags, self.total, keys))
        self.outer = in_hbm(global_fragments.reshape(frags, self.total, self.width))
        self.moment = in_hbm(momentum.reshape(frags, self.total, self.width))
        self.last = self.pieces - 1 + DELAY * (self.replicas - 2)
        self.chain = chain
        self.sources, self.staged = [self.local, self.outer, self.moment], False
        self.staged_sources, self.idled = [None] * 3, set()
        self.piece = pl.BlockSpec((self.block, keys), lambda i, s: (i, 0))
        self.piece_shape = pltpu.VMEM((self.chunk, keys), BF16)
        self.state = None
        self.ready, self.came = [], []

    def pairs(self, t, path):
        n = self.replicas
        return [
            pair
            for z in range(n - 1)
            if z % 2 == path
            for pair, hop in (((z, z + 1), z), ((z + 1, z), n - 2 - z))
            if 0 <= t - DELAY * hop < self.pieces
        ]

    def ways(self, t):
        if t > self.last:
            return 0
        return 2 if self.pairs(t, 1) else 1

    def row(self, place, i):
        start = jnp.minimum(jnp.clip(place, 0, self.pieces - 1) * self.chunk, self.total - self.chunk)
        return pl.multiple_of(start + i * self.block, 16)

    def at(self, width, place, frag=lambda s: s[CHOSEN]):
        size = (pl.Element(1), pl.Element(self.block), pl.Element(width))
        return pl.BlockSpec(size, lambda i, s: (frag(s), self.row(place(s[REPLICA]), i), 0))

    def first(self, t):
        specs = [self.at(n, lambda z: t) for n in (self.keys, self.width, self.width)]
        self.ready.append(
            call(
                functools.partial(first_body, self.replicas), "first_sends", self.chain,
                [self.local, self.outer, self.moment], specs, [self.piece_shape], [self.piece], (STEPS,),
            )
        )

    def stage(self, k, steps):
        array = self.sources[k]
        size = (1, array.shape[1] // steps, array.shape[2])
        source = pl.BlockSpec(size, lambda i, s: (s[CHOSEN], i, 0))
        target = pl.BlockSpec(size, lambda i, s: (0, i, 0))
        return array, source, pltpu.VMEM, (1,) + array.shape[1:], target, None

    def finish_idle(self, k, copied):
        if copied:
            self.state[k] = copied[0]
            self.idled.add(k)

    def idle(self, k, steps):
        array, state = (self.outer, self.moment)[k - 1], self.state[k]
        spec = pl.BlockSpec((1, array.shape[1] // steps, array.shape[2]), lambda i, s: (1 - s[CHOSEN], i, 0))
        return array, spec, pltpu.HBM, array.shape, spec, state

    def send(self, t):
        came = [lax.ppermute(x, "replica", self.pairs(t, path)) for path, x in enumerate(self.ready[t])]
        self.came.append((came + came)[:2])

    def round(self, t):
        n = self.replicas
        outs = t >= DELAY * min(max(hops_of(z, n)) for z in range(n))
        keep = {r for r in (max(hops_of(z, n)) for z in range(n)) if t > self.pieces - 1 + DELAY * r}
        users = {}
        for z in range(n):
            hops = hops_of(z, n)
            for side in (0, 1):
                behind = max(hops) - hops[side]
                if outs and hops[side] >= 0 and behind and t >= DELAY * behind:
                    users.setdefault((way(z, side), behind), []).append(z)
        old = [self.came[t - DELAY * behind][path] for path, behind in users]
        old_specs = [
            pl.BlockSpec(
                (self.block, self.keys),
                lambda i, s, zs=zs: (i * sum((s[REPLICA] == z).astype(jnp.int32) for z in zs), 0),
            )
            for zs in users.values()
        ]
        to_right = lambda z: t + DELAY - DELAY * z
        to_left = lambda z: t + DELAY - DELAY * (n - 1 - z)
        frag = (lambda s: 0) if self.staged else (lambda s: s[CHOSEN])
        specs = [self.at(w, place, frag) for place in (to_right, to_left) for w in (self.keys, self.width, self.width)]
        in_specs = [self.piece, self.piece] + old_specs + specs
        operands = list(self.came[t]) + old + self.sources * 2
        ways = self.ways(t + DELAY)
        out_shape, out_specs, aliases = [self.piece_shape] * ways, [self.piece] * ways, {}
        if outs:
            place = lambda z: t - DELAY * jnp.maximum(z - 1, n - 2 - z)
            flat = pl.BlockSpec(
                (pl.Element(self.block), pl.Element(self.keys)), lambda i, s: (self.row(place(s[REPLICA]), i), 0)
            )
            state_specs = [flat] + [self.at(self.width, place)] * 2
            if self.state is None:
                operands += [self.came[t][0]] * 3
                in_specs += [ANY] * 3
            else:
                aliases = {1 + len(operands) + k: ways + k for k in range(3)}
                operands += self.state
                in_specs += state_specs if keep else [ANY] * 3
            out_shape += [
                pltpu.HBM((self.total, self.keys), BF16),
                pltpu.HBM(self.outer.shape, F32),
                pltpu.HBM(self.moment.shape, F32),
            ]
            out_specs += state_specs
        if not out_shape:
            return
        results = call(
            functools.partial(round_body, n, list(users), ways, outs, keep), f"round_{t}", self.chain, operands, in_specs,
            out_shape, out_specs, (STEPS,), aliases, cost=LONG if t == self.last else 0,
        )
        self.ready.append(results[:ways])
        if outs:
            self.state = list(results[ways:])

    def result(self):
        for k in (1, 2):
            if k not in self.idled:
                copies = [self.idle(k, 4)]
                self.finish_idle(k, call(lambda s: None, "idle", self.chain, [], [], [], [], (4,), copies=copies))
        synced, new_global, new_momentum = self.state
        return (
            synced.reshape(self.layers, self.rows, self.keys),
            new_global.reshape(self.given),
            new_momentum.reshape(self.given),
        )


def shards(
    hidden_states,
    cotangent,
    key_weight,
    local_fragments,
    global_fragments,
    momentum,
    fragment_index,
):
    chosen = fragment_index[0] % FRAGS
    place = [lax.axis_index("replica"), lax.axis_index("fsdp")]
    chain = Chain(jnp.stack([chosen] + place).astype(jnp.int32))
    line = Line(local_fragments[0], global_fragments, momentum, chain)
    fsdp = Fsdp(hidden_states, cotangent, key_weight[0], chain)
    eighth = fsdp.devices // 8

    def grad(first, n, stage=(), idle=None):
        steps = n * eighth
        copies = [line.stage(k, steps) for k in stage]
        if idle and line.state:
            copies = [line.idle(idle, steps)]
        copied = fsdp.grad(first * eighth, steps, copies)
        for k, array in zip(stage, copied):
            line.staged_sources[k] = array
        if idle:
            line.finish_idle(idle, copied)

    def work(t):
        if t == 0:
            grad(0, 2, stage=(0,))
        elif t == 1:
            grad(2, 2, stage=(1, 2))
            line.sources, line.staged = line.staged_sources, True
        elif t == 2:
            grad(4, 2, idle=1)
        elif t == 3:
            grad(6, 2, idle=2)
            fsdp.scatter()
        elif 6 <= t < 10:
            fsdp.project(t - 6)

    for t in range(DELAY):
        line.first(t)
    for t in range(line.last + 1):
        line.send(t)
        line.round(t)
        work(t)
    synced, new_global, new_momentum = line.result()
    weight_grad = fsdp.widen()
    return (fsdp.total, weight_grad[None], new_global, new_momentum, synced)


def solution(mesh):
    placed = (
        P(("replica", "fsdp"), None),
        P(("replica", "fsdp"), None),
        P("replica", "fsdp", None),
        P("replica", None, None, "fsdp", None),
        P(None, None, "fsdp", "replica"),
        P(None, None, "fsdp", "replica"),
        P(),
    )
    return jax.shard_map(
        shards,
        mesh=mesh,
        in_specs=placed,
        out_specs=(
            P(("replica", "fsdp"), None),
            P("replica", "fsdp", None),
            P(None, None, "fsdp", "replica"),
            P(None, None, "fsdp", "replica"),
            P(None, "fsdp", None),
        ),
        check_vma=False,
    )
```

time: 449 us -> 189 us (0.42)
  waiting for transfers between devices: 378 us -> 31.5 us
  Pallas kernels: 0 us -> 88.9 us
  starting transfers between devices: 0.16 us -> 46.1 us
  matrix products: 29.2 us -> 0 us
  local copies, waits for them, and re-layouts: 21.6 us -> 5.83 us
  other arithmetic: 5.63 us -> 0.08 us
    psum x1 -> x0, waiting for transfers between devices: 158 us -> none  [shards(): lax.psum(local_chosen.astype(jnp.bfloat16), 'replica').astype(jnp.float32)]
    all_gather x2 -> x1, waiting for transfers between devices: 114 us -> 0.01 us  [__init__(): self.weight = in_hbm(lax.all_gather(weight, 'fsdp', axis=0, tiled=True))]
    reduce_scatter x1, waiting for transfers between devices: 106 us -> 0.01 us  [scatter(): lax.psum_scatter(self.sums.reshape(self.model, self.keys), 'fsdp', scatte...]
    pallas_call x0 -> x25, Pallas kernels: none -> 88.9 us  [call(): pl.pallas_call(kernel, out_shape=out_shape, grid_spec=pltpu.PrefetchScala...]
    ppermute x0 -> x24, starting transfers between devices: none -> 46 us  [send(): lax.ppermute(x, 'replica', self.pairs(t, path))]
    ppermute x0 -> x24, waiting for transfers between devices: none -> 30.8 us  [send(): lax.ppermute(x, 'replica', self.pairs(t, path))]
    dot_general x2 -> x0, matrix products: 29.2 us -> none  [the longest x1 14.6 us: shards(): jnp.dot(columns, lax.all_gather(weight_rows, 'fsdp', axis=0, tiled=True),...]
    unnamed x11 -> x20, local copies, waits for them, and re-layouts: 13 us -> 5.83 us
  transfers between devices with their start and end apart: 4 -> 26, of which waited for: 4 -> 6; matrix products, arithmetic and copies ran while one was open for 7% -> 0% of each run, Pallas kernels for 0% -> 46%
where the time goes in v1:
time: 189 us; the launch traced here: 187 us
  Pallas kernels  88.9 us (47%)
  starting transfers between devices  46.1 us (24%)
  waiting for transfers between devices  31.5 us (17%)
  between operations  15 us (8%)
  local copies, waits for them, and re-layouts  5.83 us (3%)
    pallas_call x25, Pallas kernels, call(): pl.pallas_call(kernel, out_shape=out_shape, grid_spec=pltpu.PrefetchScala...  88.9 us
    ppermute x24, starting transfers between devices, send(): lax.ppermute(x, 'replica', self.pairs(t, path))  46 us
    ppermute x24, waiting for transfers between devices, send(): lax.ppermute(x, 'replica', self.pairs(t, path))  30.8 us
    unnamed x20, local copies, waits for them, and re-layouts  5.83 us
  transfers between devices with their start and end apart: 26, of which 6 were waited for; matrix products, arithmetic and copies ran while one was open for 0% of the time, Pallas kernels for 46%

profile of v1, /device:TPU:0, one launch (start us, length us, event | category | flops | bytes accessed | tf_op | source)
XLA Modules:
  0.0 187.4 jit_solution(2743928477309504346)
XLA Ops:
  10.5 4.9 %collective-permute-start = (bf16[208,1024]{1,0:T(8,128)(2,1)S(1)}, bf16[208,1024]{1,0:T(8,128)(2,1)S(1)}, u32[]{:S(2)}, u32[]{:S(2)}) collective-permute-start(bf16[208,1024]{1,0:T(8,128)(2,1)S(1)} %get-tuple-element.103), channel_id=1, source_target_pairs={{0,8},{24,16},{1,9},{25,17},{2,10},{26,18},{3,11},{27,19},{4,12},{... | collective-permute-start | bytes 1277960 | tf_op jit(solution)/shard_map/ppermute | solution.py:312
  18.5 7.1 %collective-permute-done.refs_0_.refs_1_.refs_2_ = bf16[208,1024]{1,0:T(8,128)(2,1)S(1)} collective-permute-done((bf16[208,1024]{1,0:T(8,128)(2,1)S(1)}, bf16[208,1024]{1,0:T(8,128)(2,1)S(1)}, u32[]{:S(2)}, u32[]{:S(2)}) %collective-permute-start) | collective-permute-done | bytes 426016 | tf_op jit(solution)/shard_map/ppermute | solution.py:312
  25.5 2.1 %round_0.1 = (bf16[208,1024]{1,0:T(8,128)(2,1)S(1)}, bf16[208,1024]{1,0:T(8,128)(2,1)S(1)}, f32[8,128]{1,0:T(8,128)S(1)}) custom-call(s32[3]{0:T(128)S(1)} %pad_add_fusion.s, bf16[208,1024]{1,0:T(8,128)(2,1)S(1)} %collective-permute-done.refs_0_.refs_1_.refs_2_, bf16[208,1024]{1,0:T(8,128)(2,1)S(1)} %collective-permute-done.refs_0_.refs_1_.refs_2_, ...), custom_call_target="tpu_custom_call" | custom-call | tf_op jit(solution)/shard_map/round_0/pallas_call | solution.py:61
  27.6 4.7 %collective-permute-start.1 = (bf16[208,1024]{1,0:T(8,128)(2,1)S(1)}, bf16[208,1024]{1,0:T(8,128)(2,1)S(1)}, u32[]{:S(2)}, u32[]{:S(2)}) collective-permute-start(bf16[208,1024]{1,0:T(8,128)(2,1)S(1)} %get-tuple-element.106), channel_id=1, source_target_pairs={{0,8},{24,16},{1,9},{25,17},{2,10},{26,18},{3,11},{27,19},{4,12},{... | collective-permute-start | bytes 1277960 | tf_op jit(solution)/shard_map/ppermute | solution.py:312
  33.0 7.0 %grad_0.1 = (bf16[8,512,1024]{2,1,0:T(8,128)(2,1)}, bf16[1,2048,1024]{2,1,0:T(8,128)(2,1)S(1)}, f32[8,128]{1,0:T(8,128)S(1)}) custom-call(s32[3]{0:T(128)S(1)} %pad_add_fusion.s, bf16[1024,4096]{1,0:T(8,128)(2,1)} %refs_0_.15, bf16[1024,1024]{1,0:T(8,128)(2,1)} %refs_1_.7, bf16[2,2048,1024]{2,1,0:T(8,128)(2,1)} %bitcast.23, ...), custom_call_target="tpu_custom_call" | custom-call | tf_op jit(solution)/shard_map/grad_0/pallas_call | solution.py:61
  40.0 3.4 %round_1.1 = (bf16[208,1024]{1,0:T(8,128)(2,1)S(1)}, bf16[208,1024]{1,0:T(8,128)(2,1)S(1)}, f32[8,128]{1,0:T(8,128)S(1)}) custom-call(s32[3]{0:T(128)S(1)} %pad_add_fusion.s, bf16[208,1024]{1,0:T(8,128)(2,1)S(1)} %collective-permute-done.3.refs_0_.refs_1_.refs_2_, bf16[208,1024]{1,0:T(8,128)(2,1)S(1)} %collective-permute-done.3.refs_0_.refs_1_.refs_2_, ...), custom_call_target="tpu_custom_call" | custom-call | tf_op jit(solution)/shard_map/round_1/pallas_call | solution.py:61
  43.3 4.3 %collective-permute-start.6 = (bf16[208,1024]{1,0:T(8,128)(2,1)S(1)}, bf16[208,1024]{1,0:T(8,128)(2,1)S(1)}, u32[]{:S(2)}, u32[]{:S(2)}) collective-permute-start(bf16[208,1024]{1,0:T(8,128)(2,1)S(1)} %get-tuple-element.119), channel_id=1, source_target_pairs={{0,8},{24,16},{1,9},{25,17},{2,10},{26,18},{3,11},{27,19},{4,12},{... | collective-permute-start | bytes 1277960 | tf_op jit(solution)/shard_map/ppermute | solution.py:312
  48.3 7.4 %grad_2.1 = (bf16[8,512,1024]{2,1,0:T(8,128)(2,1)}, f32[1,2048,256]{2,1,0:T(8,128)S(1)}, f32[1,2048,256]{2,1,0:T(8,128)S(1)}, f32[8,128]{1,0:T(8,128)S(1)}) custom-call(s32[3]{0:T(128)S(1)} %pad_add_fusion.s, bf16[1024,4096]{1,0:T(8,128)(2,1)} %refs_0_.15, bf16[1024,1024]{1,0:T(8,128)(2,1)} %refs_1_.7, ...), custom_call_target="tpu_custom_call", output_to_operand_aliasing={{0}: (3, {})} | custom-call | tf_op jit(solution)/shard_map/grad_2/pallas_call | solution.py:61
  57.5 6.7 %grad_4.1 = (bf16[8,512,1024]{2,1,0:T(8,128)(2,1)}, f32[2,2048,256]{2,1,0:T(8,128)}, f32[8,128]{1,0:T(8,128)S(1)}) custom-call(s32[3]{0:T(128)S(1)} %pad_add_fusion.s, bf16[1024,4096]{1,0:T(8,128)(2,1)} %refs_0_.15, bf16[1024,1024]{1,0:T(8,128)(2,1)} %refs_1_.7, ...), custom_call_target="tpu_custom_call", output_to_operand_aliasing={{0}: (3, {}), {1}: (5, {})} | custom-call | tf_op jit(solution)/shard_map/grad_4/pallas_call | solution.py:61
  64.3 2.0 %round_3.1 = (bf16[208,1024]{1,0:T(8,128)(2,1)}, bf16[208,1024]{1,0:T(8,128)(2,1)}, bf16[2048,1024]{1,0:T(8,128)(2,1)}, f32[2,2048,256]{2,1,0:T(8,128)}, f32[2,2048,256]{2,1,0:T(8,128)}, /*index=5*/f32[8,128]{1,0:T(8,128)S(1)}) custom-call(s32[3]{0:T(128)S(1)} %pad_add_fusion.s, ...), custom_call_target="tpu_custom_call", output_to_operand_aliasing={{2}: (10, {}), {3}: (11, {}), {4}: (12, {})} | custom-call | tf_op jit(solution)/shard_map/round_3/pallas_call | solution.py:61
  66.3 6.8 %grad_6.1 = (bf16[8,512,1024]{2,1,0:T(8,128)(2,1)}, f32[2,2048,256]{2,1,0:T(8,128)}, f32[8,128]{1,0:T(8,128)S(1)}) custom-call(s32[3]{0:T(128)S(1)} %pad_add_fusion.s, bf16[1024,4096]{1,0:T(8,128)(2,1)} %refs_0_.15, bf16[1024,1024]{1,0:T(8,128)(2,1)} %refs_1_.7, ...), custom_call_target="tpu_custom_call", output_to_operand_aliasing={{0}: (3, {}), {1}: (5, {})} | custom-call | tf_op jit(solution)/shard_map/grad_6/pallas_call | solution.py:61
  75.5 2.9 %collective-permute-start.10 = (bf16[208,1024]{1,0:T(8,128)(2,1)}, bf16[208,1024]{1,0:T(8,128)(2,1)S(1)}, u32[]{:S(2)}, u32[]{:S(2)}) collective-permute-start(bf16[208,1024]{1,0:T(8,128)(2,1)} %get-tuple-element.137), channel_id=1, source_target_pairs={{0,8},{8,0},{16,24},{24,16},{1,9},{9,1},{17,25},{25,17},{2,10},{10... | collective-permute-start | bytes 1277960 | tf_op jit(solution)/shard_map/ppermute | solution.py:312
  79.1 7.0 %collective-permute-done.4.refs_0_.refs_2_ = bf16[208,1024]{1,0:T(8,128)(2,1)S(1)} collective-permute-done((bf16[208,1024]{1,0:T(8,128)(2,1)}, bf16[208,1024]{1,0:T(8,128)(2,1)S(1)}, u32[]{:S(2)}, u32[]{:S(2)}) %collective-permute-start.4) | collective-permute-done | bytes 426016 | tf_op jit(solution)/shard_map/ppermute | solution.py:312
  86.1 2.9 %copy-done.1 = bf16[1,2048,1024]{2,1,0:T(8,128)(2,1)S(1)} copy-done((bf16[1,2048,1024]{2,1,0:T(8,128)(2,1)S(1)}, bf16[1,2048,1024]{2,1,0:T(8,128)(2,1)}, u32[]{:S(2)}) %copy-start.1) | copy-done | bytes 4194328
  92.6 3.6 %collective-permute-start.8 = (bf16[208,1024]{1,0:T(8,128)(2,1)S(1)}, bf16[208,1024]{1,0:T(8,128)(2,1)S(1)}, u32[]{:S(2)}, u32[]{:S(2)}) collective-permute-start(bf16[208,1024]{1,0:T(8,128)(2,1)S(1)} %get-tuple-element.135), channel_id=1, source_target_pairs={{0,8},{8,0},{16,24},{24,16},{1,9},{9,1},{17,25},{25,17},{2,10},{10... | collective-permute-start | bytes 1277960 | tf_op jit(solution)/shard_map/ppermute | solution.py:312
  96.9 2.0 %round_5.1 = (bf16[208,1024]{1,0:T(8,128)(2,1)}, bf16[208,1024]{1,0:T(8,128)(2,1)}, bf16[2048,1024]{1,0:T(8,128)(2,1)}, f32[2,2048,256]{2,1,0:T(8,128)}, f32[2,2048,256]{2,1,0:T(8,128)}, /*index=5*/f32[8,128]{1,0:T(8,128)S(1)}) custom-call(s32[3]{0:T(128)S(1)} %pad_add_fusion.s, ...), custom_call_target="tpu_custom_call", output_to_operand_aliasing={{2}: (10, {}), {3}: (11, {}), {4}: (12, {})} | custom-call | tf_op jit(solution)/shard_map/round_5/pallas_call | solution.py:61
  98.9 2.8 %collective-permute-start.12 = (bf16[208,1024]{1,0:T(8,128)(2,1)}, bf16[208,1024]{1,0:T(8,128)(2,1)S(1)}, u32[]{:S(2)}, u32[]{:S(2)}) collective-permute-start(bf16[208,1024]{1,0:T(8,128)(2,1)} %get-tuple-element.149), channel_id=1, source_target_pairs={{0,8},{8,0},{16,24},{24,16},{1,9},{9,1},{17,25},{25,17},{2,10},{10... | collective-permute-start | bytes 1277960 | tf_op jit(solution)/shard_map/ppermute | solution.py:312
  103.1 3.8 %collective-permute-done.8.refs_0_.refs_2_ = bf16[208,1024]{1,0:T(8,128)(2,1)S(1)} collective-permute-done((bf16[208,1024]{1,0:T(8,128)(2,1)S(1)}, bf16[208,1024]{1,0:T(8,128)(2,1)S(1)}, u32[]{:S(2)}, u32[]{:S(2)}) %collective-permute-start.8) | collective-permute-done | bytes 426016 | tf_op jit(solution)/shard_map/ppermute | solution.py:312
  106.9 2.0 %round_6.1 = (bf16[208,1024]{1,0:T(8,128)(2,1)}, bf16[208,1024]{1,0:T(8,128)(2,1)}, bf16[2048,1024]{1,0:T(8,128)(2,1)}, f32[2,2048,256]{2,1,0:T(8,128)}, f32[2,2048,256]{2,1,0:T(8,128)}, /*index=5*/f32[8,128]{1,0:T(8,128)S(1)}) custom-call(s32[3]{0:T(128)S(1)} %pad_add_fusion.s, ...), custom_call_target="tpu_custom_call", output_to_operand_aliasing={{2}: (10, {}), {3}: (11, {}), {4}: (12, {})} | custom-call | tf_op jit(solution)/shard_map/round_6/pallas_call | solution.py:61
  108.9 4.0 %collective-permute-start.14 = (bf16[208,1024]{1,0:T(8,128)(2,1)}, bf16[208,1024]{1,0:T(8,128)(2,1)S(1)}, u32[]{:S(2)}, u32[]{:S(2)}) collective-permute-start(bf16[208,1024]{1,0:T(8,128)(2,1)} %get-tuple-element.157), channel_id=1, source_target_pairs={{0,8},{8,0},{16,24},{24,16},{1,9},{9,1},{17,25},{25,17},{2,10},{10... | collective-permute-start | bytes 1277960 | tf_op jit(solution)/shard_map/ppermute | solution.py:312
  114.3 5.9 %project_0.1 = (f32[1024,1024]{1,0:T(8,128)S(1)}, f32[8,128]{1,0:T(8,128)S(1)}) custom-call(s32[3]{0:T(128)S(1)} %pad_add_fusion.s, bf16[1024,4096]{1,0:T(8,128)(2,1)} %refs_0_.15, bf16[4096,1024]{1,0:T(8,128)(2,1)} %bitcast.42, f32[8,128]{1,0:T(8,128)S(1)} %get-tuple-element.147.refs_2_), custom_call_target="tpu_custom_call" | custom-call | tf_op jit(solution)/shard_map/project_0/pallas_call | solution.py:61
  120.3 2.7 %round_7.1 = (bf16[208,1024]{1,0:T(8,128)(2,1)S(1)}, bf16[208,1024]{1,0:T(8,128)(2,1)S(1)}, bf16[2048,1024]{1,0:T(8,128)(2,1)}, f32[2,2048,256]{2,1,0:T(8,128)},...) custom-call(s32[3]{0:T(128)S(1)} %pad_add_fusion.s, ...), custom_call_target="tpu_custom_call", output_to_operand_aliasing={{2}: (10, {}), {3}: (11, {}), {4}: (12, {})} | custom-call | tf_op jit(solution)/shard_map/round_7/pallas_call | solution.py:61
  123.0 2.4 %collective-permute-start.16 = (bf16[208,1024]{1,0:T(8,128)(2,1)S(1)}, bf16[208,1024]{1,0:T(8,128)(2,1)S(1)}, u32[]{:S(2)}, u32[]{:S(2)}) collective-permute-start(bf16[208,1024]{1,0:T(8,128)(2,1)S(1)} %get-tuple-element.165), channel_id=1, source_target_pairs={{0,8},{8,0},{16,24},{24,16},{1,9},{9,1},{17,25},{25,17},{2,10},{10... | collective-permute-start | bytes 1277960 | tf_op jit(solution)/shard_map/ppermute | solution.py:312
  126.1 5.7 %project_1.1 = (f32[1024,1024]{1,0:T(8,128)S(1)}, f32[8,128]{1,0:T(8,128)S(1)}) custom-call(s32[3]{0:T(128)S(1)} %pad_add_fusion.s, bf16[1024,4096]{1,0:T(8,128)(2,1)} %refs_0_.15, bf16[4096,1024]{1,0:T(8,128)(2,1)} %bitcast.43, f32[1024,1024]{1,0:T(8,128)S(1)} %get-tuple-element.148.refs_2_, ...), custom_call_target="tpu_custom_call", output_to_operand_aliasing={{0}: (3, {})} | custom-call | tf_op jit(solution)/shard_map/project_1/pallas_call | solution.py:61
  131.8 2.7 %round_8.1 = (bf16[208,1024]{1,0:T(8,128)(2,1)S(1)}, bf16[208,1024]{1,0:T(8,128)(2,1)S(1)}, bf16[2048,1024]{1,0:T(8,128)(2,1)}, f32[2,2048,256]{2,1,0:T(8,128)},...) custom-call(s32[3]{0:T(128)S(1)} %pad_add_fusion.s, ...), custom_call_target="tpu_custom_call", output_to_operand_aliasing={{2}: (10, {}), {3}: (11, {}), {4}: (12, {})} | custom-call | tf_op jit(solution)/shard_map/round_8/pallas_call | solution.py:61
  136.6 5.6 %project_2.1 = (f32[1024,1024]{1,0:T(8,128)S(1)}, f32[8,128]{1,0:T(8,128)S(1)}) custom-call(s32[3]{0:T(128)S(1)} %pad_add_fusion.s, bf16[1024,4096]{1,0:T(8,128)(2,1)} %refs_0_.15, bf16[4096,1024]{1,0:T(8,128)(2,1)} %bitcast.44, f32[1024,1024]{1,0:T(8,128)S(1)} %get-tuple-element.156.refs_2_, ...), custom_call_target="tpu_custom_call", output_to_operand_aliasing={{0}: (3, {})} | custom-call | tf_op jit(solution)/shard_map/project_2/pallas_call | solution.py:61
  145.9 6.6 %project_3.1 = (bf16[1024,1024]{1,0:T(8,128)(2,1)}, f32[8,128]{1,0:T(8,128)S(1)}) custom-call(s32[3]{0:T(128)S(1)} %pad_add_fusion.s, bf16[1024,4096]{1,0:T(8,128)(2,1)} %refs_0_.15, bf16[4096,1024]{1,0:T(8,128)(2,1)} %bitcast.45, f32[1024,1024]{1,0:T(8,128)S(1)} %get-tuple-element.164.refs_2_, f32[8,128]{1,0:T(8,128)S(1)} %get-tuple-element.171.refs_3_), custom_call_target="tpu_custom_call" | custom-call | tf_op jit(solution)/shard_map/project_3/pallas_call | solution.py:61
  152.5 2.0 %round_10.1 = (bf16[208,1024]{1,0:T(8,128)(2,1)S(1)}, bf16[2048,1024]{1,0:T(8,128)(2,1)}, f32[2,2048,256]{2,1,0:T(8,128)}, f32[2,2048,256]{2,1,0:T(8,128)}, f32[8,128]{1,0:T(8,128)S(1)}) custom-call(s32[3]{0:T(128)S(1)} %pad_add_fusion.s, ...), custom_call_target="tpu_custom_call", output_to_operand_aliasing={{1}: (10, {}), {2}: (11, {}), {3}: (12, {})} | custom-call | tf_op jit(solution)/shard_map/round_10/pallas_call | solution.py:61
  155.8 5.2 %collective-permute-done.18.refs_0_.refs_2_ = bf16[208,1024]{1,0:T(8,128)(2,1)S(1)} collective-permute-done((bf16[208,1024]{1,0:T(8,128)(2,1)S(1)}, bf16[208,1024]{1,0:T(8,128)(2,1)S(1)}, u32[]{:S(2)}, u32[]{:S(2)}) %collective-permute-start.18) | collective-permute-done | bytes 426016 | tf_op jit(solution)/shard_map/ppermute | solution.py:312
  164.0 6.0 %collective-permute-done.23.refs_0_.refs_1_ = bf16[208,1024]{1,0:T(8,128)(2,1)S(1)} collective-permute-done((bf16[208,1024]{1,0:T(8,128)(2,1)S(1)}, bf16[208,1024]{1,0:T(8,128)(2,1)S(1)}, u32[]{:S(2)}, u32[]{:S(2)}) %collective-permute-start.23) | collective-permute-done | bytes 426016 | tf_op jit(solution)/shard_map/ppermute | solution.py:312
  170.0 2.8 %round_12.1 = (bf16[2048,1024]{1,0:T(8,128)(2,1)}, f32[2,2048,256]{2,1,0:T(8,128)}, f32[2,2048,256]{2,1,0:T(8,128)}, f32[8,128]{1,0:T(8,128)S(1)}) custom-call(s32[3]{0:T(128)S(1)} %pad_add_fusion.s, bf16[208,1024]{1,0:T(8,128)(2,1)S(1)} %collective-permute-done.23.refs_0_.refs_1_, ...), custom_call_target="tpu_custom_call", output_to_operand_aliasing={{0}: (10, {}), {1}: (11, {}), {2}: (12, {})} | custom-call | tf_op jit(solution)/shard_map/round_12/pallas_call | solution.py:61
  174.6 2.8 %round_13.1 = (bf16[2048,1024]{1,0:T(8,128)(2,1)}, f32[2,2048,256]{2,1,0:T(8,128)}, f32[2,2048,256]{2,1,0:T(8,128)}, f32[8,128]{1,0:T(8,128)S(1)}) custom-call(s32[3]{0:T(128)S(1)} %pad_add_fusion.s, bf16[208,1024]{1,0:T(8,128)(2,1)S(1)} %collective-permute-done.22.refs_0_.refs_1_, ...), custom_call_target="tpu_custom_call", output_to_operand_aliasing={{0}: (10, {}), {1}: (11, {}), {2}: (12, {})} | custom-call | bytes 1073741824 | tf_op jit(solution)/shard_map/round_13/pallas_call | solution.py:61
  (68 shorter events, 34.7 us)
Async XLA Ops:
  7.2 107.2 %all-gather.3.cloned.1.call-start = ((), (), s32[]{:S(2)}) async-start(), calls=%async_computation.2 | async-start | bytes 9437184 | tf_op jit(solution)/shard_map/all_gather | solution.py:87
  7.9 169.5 %reduce-scatter.2.cloned.1.call-start = ((), (), s32[]{:S(2)}) async-start(), calls=%async_computation.1 | async-start | bytes 9437184 | tf_op jit(solution)/shard_map/reduce_scatter | solution.py:139
  10.5 15.0 %collective-permute-start = (bf16[208,1024]{1,0:T(8,128)(2,1)S(1)}, bf16[208,1024]{1,0:T(8,128)(2,1)S(1)}, u32[]{:S(2)}, u32[]{:S(2)}) collective-permute-start(bf16[208,1024]{1,0:T(8,128)(2,1)S(1)} %get-tuple-element.103), channel_id=1, source_target_pairs={{0,8},{24,16},{1,9},{25,17},{2,10},{26,18},{3,11},{27,19},{4,12},{... | collective-permute-start | bytes 1277960 | tf_op jit(solution)/shard_map/ppermute | solution.py:312
  17.2 22.8 %collective-permute-start.3 = (bf16[208,1024]{1,0:T(8,128)(2,1)S(1)}, bf16[208,1024]{1,0:T(8,128)(2,1)S(1)}, u32[]{:S(2)}, u32[]{:S(2)}) collective-permute-start(bf16[208,1024]{1,0:T(8,128)(2,1)S(1)} %get-tuple-element.111), channel_id=1, source_target_pairs={{0,8},{24,16},{1,9},{25,17},{2,10},{26,18},{3,11},{27,19},{4,12},{... | collective-permute-start | bytes 1277960 | tf_op jit(solution)/shard_map/ppermute | solution.py:312
  27.6 28.1 %collective-permute-start.1 = (bf16[208,1024]{1,0:T(8,128)(2,1)S(1)}, bf16[208,1024]{1,0:T(8,128)(2,1)S(1)}, u32[]{:S(2)}, u32[]{:S(2)}) collective-permute-start(bf16[208,1024]{1,0:T(8,128)(2,1)S(1)} %get-tuple-element.106), channel_id=1, source_target_pairs={{0,8},{24,16},{1,9},{25,17},{2,10},{26,18},{3,11},{27,19},{4,12},{... | collective-permute-start | bytes 1277960 | tf_op jit(solution)/shard_map/ppermute | solution.py:312
  32.3 23.5 %collective-permute-start.2 = (bf16[208,1024]{1,0:T(8,128)(2,1)S(1)}, bf16[208,1024]{1,0:T(8,128)(2,1)S(1)}, u32[]{:S(2)}, u32[]{:S(2)}) collective-permute-start(bf16[208,1024]{1,0:T(8,128)(2,1)S(1)} %get-tuple-element.107), channel_id=1, source_target_pairs={{8,16},{16,8},{9,17},{17,9},{10,18},{18,10},{11,19},{19,11},{12,20... | collective-permute-start | bytes 1277960 | tf_op jit(solution)/shard_map/ppermute | solution.py:312
  39.9 24.3 %copy-start = (bf16[1,2048,1024]{2,1,0:T(8,128)(2,1)}, bf16[1,2048,1024]{2,1,0:T(8,128)(2,1)S(1)}, u32[]{:S(2)}) copy-start(bf16[1,2048,1024]{2,1,0:T(8,128)(2,1)S(1)} %get-tuple-element.109.refs_3_.refs_6_) | copy-start | bytes 12582916
  43.3 20.9 %collective-permute-start.6 = (bf16[208,1024]{1,0:T(8,128)(2,1)S(1)}, bf16[208,1024]{1,0:T(8,128)(2,1)S(1)}, u32[]{:S(2)}, u32[]{:S(2)}) collective-permute-start(bf16[208,1024]{1,0:T(8,128)(2,1)S(1)} %get-tuple-element.119), channel_id=1, source_target_pairs={{0,8},{24,16},{1,9},{25,17},{2,10},{26,18},{3,11},{27,19},{4,12},{... | collective-permute-start | bytes 1277960 | tf_op jit(solution)/shard_map/ppermute | solution.py:312
  47.6 16.6 %collective-permute-start.7 = (bf16[208,1024]{1,0:T(8,128)(2,1)S(1)}, bf16[208,1024]{1,0:T(8,128)(2,1)S(1)}, u32[]{:S(2)}, u32[]{:S(2)}) collective-permute-start(bf16[208,1024]{1,0:T(8,128)(2,1)S(1)} %get-tuple-element.120), channel_id=1, source_target_pairs={{8,16},{16,8},{9,17},{17,9},{10,18},{18,10},{11,19},{19,11},{12,20... | collective-permute-start | bytes 1277960 | tf_op jit(solution)/shard_map/ppermute | solution.py:312
  55.7 8.5 %copy-start.3 = (f32[1,2048,256]{2,1,0:T(8,128)}, f32[1,2048,256]{2,1,0:T(8,128)S(1)}, u32[]{:S(2)}) copy-start(f32[1,2048,256]{2,1,0:T(8,128)S(1)} %get-tuple-element.115.refs_5_.refs_8_) | copy-start | bytes 6291460
  57.5 6.7 %copy-start.9 = (bf16[208,1024]{1,0:T(8,128)(2,1)}, bf16[208,1024]{1,0:T(8,128)(2,1)S(1)}, u32[]{:S(2)}) copy-start(bf16[208,1024]{1,0:T(8,128)(2,1)S(1)} %get-tuple-element.117) | copy-start | bytes 1277956
  73.1 13.0 %collective-permute-start.4 = (bf16[208,1024]{1,0:T(8,128)(2,1)}, bf16[208,1024]{1,0:T(8,128)(2,1)S(1)}, u32[]{:S(2)}, u32[]{:S(2)}) collective-permute-start(bf16[208,1024]{1,0:T(8,128)(2,1)} %copy-done.9), channel_id=1, source_target_pairs={{0,8},{8,0},{16,24},{24,16},{1,9},{9,1},{17,25},{25,17},{2,10},{10... | collective-permute-start | bytes 1277960 | tf_op jit(solution)/shard_map/ppermute | solution.py:312
  74.8 11.3 %collective-permute-start.5 = (bf16[208,1024]{1,0:T(8,128)(2,1)S(1)}, bf16[208,1024]{1,0:T(8,128)(2,1)S(1)}, u32[]{:S(2)}, u32[]{:S(2)}) collective-permute-start(bf16[208,1024]{1,0:T(8,128)(2,1)S(1)} %get-tuple-element.118), channel_id=1, source_target_pairs={{8,16},{16,8},{9,17},{17,9},{10,18},{18,10},{11,19},{19,11},{12,20... | collective-permute-start | bytes 1277960 | tf_op jit(solution)/shard_map/ppermute | solution.py:312
  75.5 21.3 %collective-permute-start.10 = (bf16[208,1024]{1,0:T(8,128)(2,1)}, bf16[208,1024]{1,0:T(8,128)(2,1)S(1)}, u32[]{:S(2)}, u32[]{:S(2)}) collective-permute-start(bf16[208,1024]{1,0:T(8,128)(2,1)} %get-tuple-element.137), channel_id=1, source_target_pairs={{0,8},{8,0},{16,24},{24,16},{1,9},{9,1},{17,25},{25,17},{2,10},{10... | collective-permute-start | bytes 1277960 | tf_op jit(solution)/shard_map/ppermute | solution.py:312
  78.4 18.5 %collective-permute-start.11 = (bf16[208,1024]{1,0:T(8,128)(2,1)}, bf16[208,1024]{1,0:T(8,128)(2,1)S(1)}, u32[]{:S(2)}, u32[]{:S(2)}) collective-permute-start(bf16[208,1024]{1,0:T(8,128)(2,1)} %get-tuple-element.138), channel_id=1, source_target_pairs={{8,16},{16,8},{9,17},{17,9},{10,18},{18,10},{11,19},{19,11},{12,20... | collective-permute-start | bytes 1277960 | tf_op jit(solution)/shard_map/ppermute | solution.py:312
  92.6 14.3 %collective-permute-start.8 = (bf16[208,1024]{1,0:T(8,128)(2,1)S(1)}, bf16[208,1024]{1,0:T(8,128)(2,1)S(1)}, u32[]{:S(2)}, u32[]{:S(2)}) collective-permute-start(bf16[208,1024]{1,0:T(8,128)(2,1)S(1)} %get-tuple-element.135), channel_id=1, source_target_pairs={{0,8},{8,0},{16,24},{24,16},{1,9},{9,1},{17,25},{25,17},{2,10},{10... | collective-permute-start | bytes 1277960 | tf_op jit(solution)/shard_map/ppermute | solution.py:312
  96.2 10.7 %collective-permute-start.9 = (bf16[208,1024]{1,0:T(8,128)(2,1)S(1)}, bf16[208,1024]{1,0:T(8,128)(2,1)S(1)}, u32[]{:S(2)}, u32[]{:S(2)}) collective-permute-start(bf16[208,1024]{1,0:T(8,128)(2,1)S(1)} %get-tuple-element.136), channel_id=1, source_target_pairs={{8,16},{16,8},{9,17},{17,9},{10,18},{18,10},{11,19},{19,11},{12,20... | collective-permute-start | bytes 1277960 | tf_op jit(solution)/shard_map/ppermute | solution.py:312
  98.9 21.3 %collective-permute-start.12 = (bf16[208,1024]{1,0:T(8,128)(2,1)}, bf16[208,1024]{1,0:T(8,128)(2,1)S(1)}, u32[]{:S(2)}, u32[]{:S(2)}) collective-permute-start(bf16[208,1024]{1,0:T(8,128)(2,1)} %get-tuple-element.149), channel_id=1, source_target_pairs={{0,8},{8,0},{16,24},{24,16},{1,9},{9,1},{17,25},{25,17},{2,10},{10... | collective-permute-start | bytes 1277960 | tf_op jit(solution)/shard_map/ppermute | solution.py:312
  101.7 18.5 %collective-permute-start.13 = (bf16[208,1024]{1,0:T(8,128)(2,1)}, bf16[208,1024]{1,0:T(8,128)(2,1)}, u32[]{:S(2)}, u32[]{:S(2)}) collective-permute-start(bf16[208,1024]{1,0:T(8,128)(2,1)} %get-tuple-element.150), channel_id=1, source_target_pairs={{8,16},{16,8},{9,17},{17,9},{10,18},{18,10},{11,19},{19,11},{12,20... | collective-permute-start | bytes 1277960 | tf_op jit(solution)/shard_map/ppermute | solution.py:312
  108.9 22.9 %collective-permute-start.14 = (bf16[208,1024]{1,0:T(8,128)(2,1)}, bf16[208,1024]{1,0:T(8,128)(2,1)S(1)}, u32[]{:S(2)}, u32[]{:S(2)}) collective-permute-start(bf16[208,1024]{1,0:T(8,128)(2,1)} %get-tuple-element.157), channel_id=1, source_target_pairs={{0,8},{8,0},{16,24},{24,16},{1,9},{9,1},{17,25},{25,17},{2,10},{10... | collective-permute-start | bytes 1277960 | tf_op jit(solution)/shard_map/ppermute | solution.py:312
  112.9 19.0 %collective-permute-start.15 = (bf16[208,1024]{1,0:T(8,128)(2,1)}, bf16[208,1024]{1,0:T(8,128)(2,1)}, u32[]{:S(2)}, u32[]{:S(2)}) collective-permute-start(bf16[208,1024]{1,0:T(8,128)(2,1)} %get-tuple-element.158), channel_id=1, source_target_pairs={{8,16},{16,8},{9,17},{17,9},{10,18},{18,10},{11,19},{19,11},{12,20... | collective-permute-start | bytes 1277960 | tf_op jit(solution)/shard_map/ppermute | solution.py:312
  114.3 5.9 %copy-start.2 = (bf16[1,2048,1024]{2,1,0:T(8,128)(2,1)S(1)}, bf16[1,2048,1024]{2,1,0:T(8,128)(2,1)}, u32[]{:S(2)}) copy-start(bf16[1,2048,1024]{2,1,0:T(8,128)(2,1)} %copy-done) | copy-start | bytes 12582916
  114.3 5.9 %copy-start.5 = (f32[1,2048,256]{2,1,0:T(8,128)S(1)}, f32[1,2048,256]{2,1,0:T(8,128)}, u32[]{:S(2)}) copy-start(f32[1,2048,256]{2,1,0:T(8,128)} %copy-done.3) | copy-start | bytes 6291460
  114.3 5.9 %copy-start.7 = (bf16[208,1024]{1,0:T(8,128)(2,1)S(1)}, bf16[208,1024]{1,0:T(8,128)(2,1)}, u32[]{:S(2)}) copy-start(bf16[208,1024]{1,0:T(8,128)(2,1)} %copy-done.6) | copy-start | bytes 1277956
  123.0 19.1 %collective-permute-start.16 = (bf16[208,1024]{1,0:T(8,128)(2,1)S(1)}, bf16[208,1024]{1,0:T(8,128)(2,1)S(1)}, u32[]{:S(2)}, u32[]{:S(2)}) collective-permute-start(bf16[208,1024]{1,0:T(8,128)(2,1)S(1)} %get-tuple-element.165), channel_id=1, source_target_pairs={{0,8},{8,0},{16,24},{24,16},{1,9},{9,1},{17,25},{25,17},{2,10},{10... | collective-permute-start | bytes 1277960 | tf_op jit(solution)/shard_map/ppermute | solution.py:312
  125.5 16.7 %collective-permute-start.17 = (bf16[208,1024]{1,0:T(8,128)(2,1)S(1)}, bf16[208,1024]{1,0:T(8,128)(2,1)S(1)}, u32[]{:S(2)}, u32[]{:S(2)}) collective-permute-start(bf16[208,1024]{1,0:T(8,128)(2,1)S(1)} %get-tuple-element.166), channel_id=1, source_target_pairs={{8,16},{16,8},{9,17},{17,9},{10,18},{18,10},{11,19},{19,11},{12,20... | collective-permute-start | bytes 1277960 | tf_op jit(solution)/shard_map/ppermute | solution.py:312
  134.6 17.9 %collective-permute-start.20 = (bf16[208,1024]{1,0:T(8,128)(2,1)S(1)}, bf16[208,1024]{1,0:T(8,128)(2,1)S(1)}, u32[]{:S(2)}, u32[]{:S(2)}) collective-permute-start(bf16[208,1024]{1,0:T(8,128)(2,1)S(1)} %get-tuple-element.176), channel_id=1, source_target_pairs={{8,0},{16,24},{9,1},{17,25},{10,2},{18,26},{11,3},{19,27},{12,4},{... | collective-permute-start | bytes 1277960 | tf_op jit(solution)/shard_map/ppermute | solution.py:312
  135.9 16.7 %collective-permute-start.21 = (bf16[208,1024]{1,0:T(8,128)(2,1)S(1)}, bf16[208,1024]{1,0:T(8,128)(2,1)S(1)}, u32[]{:S(2)}, u32[]{:S(2)}) collective-permute-start(bf16[208,1024]{1,0:T(8,128)(2,1)S(1)} %get-tuple-element.177), channel_id=1, source_target_pairs={{8,16},{16,8},{9,17},{17,9},{10,18},{18,10},{11,19},{19,11},{12,20... | collective-permute-start | bytes 1277960 | tf_op jit(solution)/shard_map/ppermute | solution.py:312
  143.9 17.1 %collective-permute-start.18 = (bf16[208,1024]{1,0:T(8,128)(2,1)S(1)}, bf16[208,1024]{1,0:T(8,128)(2,1)S(1)}, u32[]{:S(2)}, u32[]{:S(2)}) collective-permute-start(bf16[208,1024]{1,0:T(8,128)(2,1)S(1)} %get-tuple-element.174), channel_id=1, source_target_pairs={{8,0},{16,24},{9,1},{17,25},{10,2},{18,26},{11,3},{19,27},{12,4},{... | collective-permute-start | bytes 1277960 | tf_op jit(solution)/shard_map/ppermute | solution.py:312
  145.2 15.8 %collective-permute-start.19 = (bf16[208,1024]{1,0:T(8,128)(2,1)S(1)}, bf16[208,1024]{1,0:T(8,128)(2,1)S(1)}, u32[]{:S(2)}, u32[]{:S(2)}) collective-permute-start(bf16[208,1024]{1,0:T(8,128)(2,1)S(1)} %get-tuple-element.175), channel_id=1, source_target_pairs={{8,16},{16,8},{9,17},{17,9},{10,18},{18,10},{11,19},{19,11},{12,20... | collective-permute-start | bytes 1277960 | tf_op jit(solution)/shard_map/ppermute | solution.py:312
  154.5 15.5 %collective-permute-start.23 = (bf16[208,1024]{1,0:T(8,128)(2,1)S(1)}, bf16[208,1024]{1,0:T(8,128)(2,1)S(1)}, u32[]{:S(2)}, u32[]{:S(2)}) collective-permute-start(bf16[208,1024]{1,0:T(8,128)(2,1)S(1)} %get-tuple-element.187), channel_id=1, source_target_pairs={{8,0},{16,24},{9,1},{17,25},{10,2},{18,26},{11,3},{19,27},{12,4},{... | collective-permute-start | bytes 1277960 | tf_op jit(solution)/shard_map/ppermute | solution.py:312
  162.7 11.8 %collective-permute-start.22 = (bf16[208,1024]{1,0:T(8,128)(2,1)S(1)}, bf16[208,1024]{1,0:T(8,128)(2,1)S(1)}, u32[]{:S(2)}, u32[]{:S(2)}) collective-permute-start(bf16[208,1024]{1,0:T(8,128)(2,1)S(1)} %get-tuple-element.186), channel_id=1, source_target_pairs={{8,0},{16,24},{9,1},{17,25},{10,2},{18,26},{11,3},{19,27},{12,4},{... | collective-permute-start | bytes 1277960 | tf_op jit(solution)/shard_map/ppermute | solution.py:312
  (4 other events, 7.8 us)
Sparse Core Ops, SparseCore 0:
  9.9 57.0 all-gather.2
  73.2 71.6 reduce-scatter.1

commit v2 on v1

--- a/solution.py
+++ b/solution.py
@@ -8,10 +8,13 @@
 from jax.sharding import PartitionSpec as P
 
 FRAGS = 2
-PIECES = 10
+PIECES = 8
 STEPS = 1
 DELAY = 2
 PROJECT_BLOCKS = 4
+GRADS = ((0, 2, (0,), -1), (2, 3, (1, 2), 0), (5, 3, (), 2))
+IDLE_BEFORE = 1
+PROJECT_ROUNDS = (5, 8)
 MEAN_PART = 1.33
 GLOBAL_PART = -0.33
 MOMENT_PART = -0.567
@@ -20,8 +23,14 @@
 ANY = pl.BlockSpec(memory_space=pl.ANY)
 CONTRACT_ROWS = (((0,), (0,)), ((), ()))
 CHOSEN, REPLICA, FSDP = 0, 1, 2
-VMEM = 16 << 20
-LONG = 1 << 30
+VMEM = 18 << 20
+VMEM_R = 10 << 20
+VMEM_P = 16 << 20
+LONG = 112 * 10**9
+
+
+def in_vmem(x):
+    return pltpu.with_memory_space_constraint(x, pltpu.VMEM)
 
 
 def in_hbm(x):
@@ -33,7 +42,7 @@
         self.scalars, self.token = scalars, None
 
 
-def call(body, name, chain, operands, in_specs, out_shape, out_specs, grid, aliases=None, copies=(), cost=0):
+def call(body, name, chain, operands, in_specs, out_shape, out_specs, grid, aliases=None, copies=(), cost=0, vmem=VMEM):
     n_in, n_out, n = len(operands), len(out_shape), len(copies)
     aliases = dict(aliases or {})
     operands, in_specs = list(operands), list(in_specs)
@@ -68,8 +77,8 @@
             out_specs=out_specs + [ANY],
         ),
         input_output_aliases=aliases,
-        compiler_params=pltpu.CompilerParams(vmem_limit_bytes=VMEM),
-        cost_estimate=pl.CostEstimate(flops=0, bytes_accessed=cost, transcendentals=0),
+        compiler_params=pltpu.CompilerParams(vmem_limit_bytes=vmem),
+        cost_estimate=pl.CostEstimate(flops=cost, bytes_accessed=0, transcendentals=0),
         name=name,
     )(chain.scalars, *operands)
     return results
@@ -83,18 +92,18 @@
         self.devices = lax.axis_size("fsdp")
         self.rows = self.model // self.devices
         self.chain = chain
-        self.whole = pl.BlockSpec((self.tokens, self.keys), lambda i, s: (0, 0))
+        self.whole = pl.BlockSpec((self.tokens, self.keys), lambda i, s: (0, 0), pipeline_mode=pl.Buffered(1))
         self.weight = in_hbm(lax.all_gather(weight, "fsdp", axis=0, tiled=True))
         self.sums = None
 
-    def project(self, part):
-        block, depth = self.tokens // PROJECT_BLOCKS, self.model // 4
-        first, final = part == 0, part == 3
+    def project(self, part, parts):
+        block, depth = self.tokens // PROJECT_BLOCKS, self.model // parts
+        first, final = part == 0, part == parts - 1
         rows = pl.BlockSpec((block, self.keys), lambda i, s: (i, 0))
         operands = [self.states, self.weight]
         in_specs = [
             pl.BlockSpec((block, depth), lambda i, s: (i, part)),
-            pl.BlockSpec((depth, self.keys), lambda i, s: (part, 0)),
+            pl.BlockSpec((depth, self.keys), lambda i, s: (part, 0), pipeline_mode=pl.Buffered(1)),
         ]
         aliases = {}
         if not first:
@@ -111,7 +120,7 @@
         (self.total,) = call(
             body, f"project_{part}", self.chain, operands, in_specs,
             [pltpu.HBM((self.tokens, self.keys), BF16) if final else pltpu.VMEM((self.tokens, self.keys), F32)], [rows],
-            (PROJECT_BLOCKS,), aliases,
+            (PROJECT_BLOCKS,), aliases, vmem=VMEM_P,
         )
 
     def grad(self, first, n, copies=()):
@@ -146,7 +155,7 @@
 
         each = pl.BlockSpec((self.rows // 2, self.keys), lambda i, s: (i, 0))
         (out,) = call(
-            body, "widen", self.chain, [self.sums], [each], [pltpu.HBM((self.rows, self.keys), F32)], [each], (2,)
+            body, "widen", self.chain, [in_hbm(self.sums)], [each], [pltpu.HBM((self.rows, self.keys), F32)], [each], (2,)
         )
         return out
 
@@ -253,7 +262,7 @@
         self.last = self.pieces - 1 + DELAY * (self.replicas - 2)
         self.chain = chain
         self.sources, self.staged = [self.local, self.outer, self.moment], False
-        self.staged_sources, self.idled = [None] * 3, set()
+        self.staged_sources = [None] * 3
         self.piece = pl.BlockSpec((self.block, keys), lambda i, s: (i, 0))
         self.piece_shape = pltpu.VMEM((self.chunk, keys), BF16)
         self.state = None
@@ -293,20 +302,21 @@
 
     def stage(self, k, steps):
         array = self.sources[k]
+        steps = 2 ** (steps.bit_length() - 1)
+        last = steps - 1
         size = (1, array.shape[1] // steps, array.shape[2])
-        source = pl.BlockSpec(size, lambda i, s: (s[CHOSEN], i, 0))
-        target = pl.BlockSpec(size, lambda i, s: (0, i, 0))
+        source = pl.BlockSpec(size, lambda i, s: (s[CHOSEN], jnp.minimum(i, last), 0))
+        target = pl.BlockSpec(size, lambda i, s: (0, jnp.minimum(i, last), 0))
         return array, source, pltpu.VMEM, (1,) + array.shape[1:], target, None
-
-    def finish_idle(self, k, copied):
-        if copied:
-            self.state[k] = copied[0]
-            self.idled.add(k)
 
     def idle(self, k, steps):
         array, state = (self.outer, self.moment)[k - 1], self.state[k]
         spec = pl.BlockSpec((1, array.shape[1] // steps, array.shape[2]), lambda i, s: (1 - s[CHOSEN], i, 0))
         return array, spec, pltpu.HBM, array.shape, spec, state
+
+    def idle_all(self):
+        copies = [self.idle(k, 4) for k in (1, 2)]
+        self.state[1:] = call(lambda s: None, "idle", self.chain, [], [], [], [], (4,), copies=copies)
 
     def send(self, t):
         came = [lax.ppermute(x, "replica", self.pairs(t, path)) for path, x in enumerate(self.ready[t])]
@@ -362,17 +372,13 @@
             return
         results = call(
             functools.partial(round_body, n, list(users), ways, outs, keep), f"round_{t}", self.chain, operands, in_specs,
-            out_shape, out_specs, (STEPS,), aliases, cost=LONG if t == self.last else 0,
+            out_shape, out_specs, (STEPS,), aliases, cost=LONG if t == self.last else 0, vmem=VMEM_R,
         )
         self.ready.append(results[:ways])
         if outs:
             self.state = list(results[ways:])
 
     def result(self):
-        for k in (1, 2):
-            if k not in self.idled:
-                copies = [self.idle(k, 4)]
-                self.finish_idle(k, call(lambda s: None, "idle", self.chain, [], [], [], [], (4,), copies=copies))
         synced, new_global, new_momentum = self.state
         return (
             synced.reshape(self.layers, self.rows, self.keys),
@@ -397,33 +403,28 @@
     fsdp = Fsdp(hidden_states, cotangent, key_weight[0], chain)
     eighth = fsdp.devices // 8
 
-    def grad(first, n, stage=(), idle=None):
+    def grad(first, n, stage):
         steps = n * eighth
-        copies = [line.stage(k, steps) for k in stage]
-        if idle and line.state:
-            copies = [line.idle(idle, steps)]
-        copied = fsdp.grad(first * eighth, steps, copies)
+        copied = fsdp.grad(first * eighth, steps, [line.stage(k, steps) for k in stage])
         for k, array in zip(stage, copied):
             line.staged_sources[k] = array
-        if idle:
-            line.finish_idle(idle, copied)
 
     def work(t):
-        if t == 0:
-            grad(0, 2, stage=(0,))
-        elif t == 1:
-            grad(2, 2, stage=(1, 2))
-            line.sources, line.staged = line.staged_sources, True
-        elif t == 2:
-            grad(4, 2, idle=1)
-        elif t == 3:
-            grad(6, 2, idle=2)
-            fsdp.scatter()
-        elif 6 <= t < 10:
-            fsdp.project(t - 6)
+        for first, n, stage, then in GRADS:
+            if t == then:
+                grad(first, n, stage)
+                if None not in line.staged_sources and not line.staged:
+                    line.sources, line.staged = [in_vmem(x) for x in line.staged_sources], True
+                if first + n == 8:
+                    fsdp.scatter()
+        if t in PROJECT_ROUNDS:
+            fsdp.project(PROJECT_ROUNDS.index(t), len(PROJECT_ROUNDS))
+        if t == line.last - IDLE_BEFORE:
+            line.idle_all()
 
     for t in range(DELAY):
         line.first(t)
+    work(-1)
     for t in range(line.last + 1):
         line.send(t)
         line.round(t)

time: 189 us -> 165 us (0.87)
  waiting for transfers between devices: 31.5 us -> 19.9 us
  starting transfers between devices: 46.1 us -> 39.2 us
  Pallas kernels: 88.9 us -> 85.4 us
    ppermute x24 -> x20, waiting for transfers between devices: 30.8 us -> 19.2 us  [send(): lax.ppermute(x, 'replica', self.pairs(t, path))]
    ppermute x24 -> x20, starting transfers between devices: 46 us -> 39.1 us  [send(): lax.ppermute(x, 'replica', self.pairs(t, path))]
    pallas_call x25 -> x21, Pallas kernels: 88.9 us -> 85.4 us  [call(): pl.pallas_call(kernel, out_shape=out_shape, grid_spec=pltpu.PrefetchScala...]
    unnamed x20 -> x16, local copies, waits for them, and re-layouts: 5.83 us -> 4.18 us
  transfers between devices with their start and end apart: 26 -> 22, of which waited for: 6 -> 4; matrix products, arithmetic and copies ran while one was open for 0% -> 0% of each run, Pallas kernels for 46% -> 50%
where the time goes in v2:
time: 165 us; the launch traced here: 164 us
  Pallas kernels  85.4 us (52%)
  starting transfers between devices  39.2 us (24%)
  waiting for transfers between devices  19.9 us (12%)
  between operations  14.9 us (9%)
  local copies, waits for them, and re-layouts  4.18 us (3%)
    pallas_call x21, Pallas kernels, call(): pl.pallas_call(kernel, out_shape=out_shape, grid_spec=pltpu.PrefetchScala...  85.4 us
    ppermute x20, starting transfers between devices, send(): lax.ppermute(x, 'replica', self.pairs(t, path))  39.1 us
    ppermute x20, waiting for transfers between devices, send(): lax.ppermute(x, 'replica', self.pairs(t, path))  19.2 us
    unnamed x16, local copies, waits for them, and re-layouts  4.18 us
  transfers between devices with their start and end apart: 22, of which 4 were waited for; matrix products, arithmetic and copies ran while one was open for 0% of the time, Pallas kernels for 50%

profile of v2, /device:TPU:0, one launch (start us, length us, event | category | flops | bytes accessed | tf_op | source)
XLA Modules:
  0.0 163.7 jit_solution(16074728626500663007)
XLA Ops:
  8.7 1.8 %first_sends.2 = (bf16[256,1024]{1,0:T(8,128)(2,1)S(1)}, f32[8,128]{1,0:T(8,128)S(1)}) custom-call(s32[3]{0:T(128)S(1)} %pad_add_fusion.s, bf16[2,2048,1024]{2,1,0:T(8,128)(2,1)} %bitcast.19, f32[2,2048,256]{2,1,0:T(8,128)} %bitcast.24, f32[2,2048,256]{2,1,0:T(8,128)} %bitcast.30), custom_call_target="tpu_custom_call" | custom-call | tf_op jit(solution)/shard_map/first_sends/pallas_call | solution.py:70
  10.5 4.9 %collective-permute-start.1 = (bf16[256,1024]{1,0:T(8,128)(2,1)S(1)}, bf16[256,1024]{1,0:T(8,128)(2,1)S(1)}, u32[]{:S(2)}, u32[]{:S(2)}) collective-permute-start(bf16[256,1024]{1,0:T(8,128)(2,1)S(1)} %get-tuple-element.91), channel_id=1, source_target_pairs={{0,8},{24,16},{1,9},{25,17},{2,10},{26,18},{3,11},{27,19},{4,12},{... | collective-permute-start | bytes 1572872 | tf_op jit(solution)/shard_map/ppermute | solution.py:322
  15.4 1.8 %first_sends.3 = (bf16[256,1024]{1,0:T(8,128)(2,1)S(1)}, f32[8,128]{1,0:T(8,128)S(1)}) custom-call(s32[3]{0:T(128)S(1)} %pad_add_fusion.s, bf16[2,2048,1024]{2,1,0:T(8,128)(2,1)} %bitcast.20, f32[2,2048,256]{2,1,0:T(8,128)} %bitcast.25, f32[2,2048,256]{2,1,0:T(8,128)} %bitcast.31, f32[8,128]{1,0:T(8,128)S(1)} %get-tuple-element.86.refs_3_), custom_call_target="tpu_custom_call" | custom-call | tf_op jit(solution)/shard_map/first_sends/pallas_call | solution.py:70
  18.5 7.4 %grad_0.1 = (bf16[8,512,1024]{2,1,0:T(8,128)(2,1)}, bf16[1,2048,1024]{2,1,0:T(8,128)(2,1)S(1)}, f32[8,128]{1,0:T(8,128)S(1)}) custom-call(s32[3]{0:T(128)S(1)} %pad_add_fusion.s, bf16[1024,4096]{1,0:T(8,128)(2,1)} %refs_0_.9, bf16[1024,1024]{1,0:T(8,128)(2,1)} %refs_1_.5, bf16[2,2048,1024]{2,1,0:T(8,128)(2,1)} %bitcast.21, ...), custom_call_target="tpu_custom_call" | custom-call | tf_op jit(solution)/shard_map/grad_0/pallas_call | solution.py:70
  27.6 2.2 %round_0.1 = (bf16[256,1024]{1,0:T(8,128)(2,1)S(1)}, bf16[256,1024]{1,0:T(8,128)(2,1)S(1)}, f32[8,128]{1,0:T(8,128)S(1)}) custom-call(s32[3]{0:T(128)S(1)} %pad_add_fusion.s, bf16[256,1024]{1,0:T(8,128)(2,1)S(1)} %collective-permute-done.1.refs_0_.refs_1_.refs_2_, bf16[256,1024]{1,0:T(8,128)(2,1)S(1)} %collective-permute-done.1.refs_0_.refs_1_.refs_2_, ...), custom_call_target="tpu_custom_call" | custom-call | tf_op jit(solution)/shard_map/round_0/pallas_call | solution.py:70
  29.8 4.7 %collective-permute-start.4 = (bf16[256,1024]{1,0:T(8,128)(2,1)S(1)}, bf16[256,1024]{1,0:T(8,128)(2,1)S(1)}, u32[]{:S(2)}, u32[]{:S(2)}) collective-permute-start(bf16[256,1024]{1,0:T(8,128)(2,1)S(1)} %get-tuple-element.99), channel_id=1, source_target_pairs={{0,8},{24,16},{1,9},{25,17},{2,10},{26,18},{3,11},{27,19},{4,12},{... | collective-permute-start | bytes 1572872 | tf_op jit(solution)/shard_map/ppermute | solution.py:322
  35.3 9.1 %grad_2.1 = (bf16[8,512,1024]{2,1,0:T(8,128)(2,1)}, f32[1,2048,256]{2,1,0:T(8,128)S(1)}, f32[1,2048,256]{2,1,0:T(8,128)S(1)}, f32[8,128]{1,0:T(8,128)S(1)}) custom-call(s32[3]{0:T(128)S(1)} %pad_add_fusion.s, bf16[1024,4096]{1,0:T(8,128)(2,1)} %refs_0_.9, bf16[1024,1024]{1,0:T(8,128)(2,1)} %refs_1_.5, ...), custom_call_target="tpu_custom_call", output_to_operand_aliasing={{0}: (3, {})} | custom-call | tf_op jit(solution)/shard_map/grad_2/pallas_call | solution.py:70
  45.0 4.3 %collective-permute-start.2 = (bf16[256,1024]{1,0:T(8,128)(2,1)S(1)}, bf16[256,1024]{1,0:T(8,128)(2,1)S(1)}, u32[]{:S(2)}, u32[]{:S(2)}) collective-permute-start(bf16[256,1024]{1,0:T(8,128)(2,1)S(1)} %get-tuple-element.97), channel_id=1, source_target_pairs={{0,8},{24,16},{1,9},{25,17},{2,10},{26,18},{3,11},{27,19},{4,12},{... | collective-permute-start | bytes 1572872 | tf_op jit(solution)/shard_map/ppermute | solution.py:322
  50.1 2.2 %round_2.1 = (bf16[256,1024]{1,0:T(8,128)(2,1)}, bf16[256,1024]{1,0:T(8,128)(2,1)}, bf16[2048,1024]{1,0:T(8,128)(2,1)}, f32[2,2048,256]{2,1,0:T(8,128)}, f32[2,2048,256]{2,1,0:T(8,128)}, /*index=5*/f32[8,128]{1,0:T(8,128)S(1)}) custom-call(s32[3]{0:T(128)S(1)} %pad_add_fusion.s, ...), custom_call_target="tpu_custom_call" | custom-call | tf_op jit(solution)/shard_map/round_2/pallas_call | solution.py:70
  52.3 2.8 %collective-permute-start.8 = (bf16[256,1024]{1,0:T(8,128)(2,1)}, bf16[256,1024]{1,0:T(8,128)(2,1)S(1)}, u32[]{:S(2)}, u32[]{:S(2)}) collective-permute-start(bf16[256,1024]{1,0:T(8,128)(2,1)} %get-tuple-element.110), channel_id=1, source_target_pairs={{0,8},{8,0},{16,24},{24,16},{1,9},{9,1},{17,25},{25,17},{2,10},{10... | collective-permute-start | bytes 1572872 | tf_op jit(solution)/shard_map/ppermute | solution.py:322
  56.6 7.7 %grad_5.1 = (bf16[8,512,1024]{2,1,0:T(8,128)(2,1)}, f32[8,128]{1,0:T(8,128)S(1)}) custom-call(s32[3]{0:T(128)S(1)} %pad_add_fusion.s, bf16[1024,4096]{1,0:T(8,128)(2,1)} %refs_0_.9, bf16[1024,1024]{1,0:T(8,128)(2,1)} %refs_1_.5, bf16[8,512,1024]{2,1,0:T(8,128)(2,1)} %get-tuple-element.105.refs_2_, ...), custom_call_target="tpu_custom_call", output_to_operand_aliasing={{0}: (3, {})} | custom-call | tf_op jit(solution)/shard_map/grad_5/pallas_call | solution.py:70
  64.3 2.2 %round_3.1 = (bf16[256,1024]{1,0:T(8,128)(2,1)}, bf16[256,1024]{1,0:T(8,128)(2,1)}, bf16[2048,1024]{1,0:T(8,128)(2,1)}, f32[2,2048,256]{2,1,0:T(8,128)}, f32[2,2048,256]{2,1,0:T(8,128)}, /*index=5*/f32[8,128]{1,0:T(8,128)S(1)}) custom-call(s32[3]{0:T(128)S(1)} %pad_add_fusion.s, ...), custom_call_target="tpu_custom_call", output_to_operand_aliasing={{2}: (10, {}), {3}: (11, {}), {4}: (12, {})} | custom-call | tf_op jit(solution)/shard_map/round_3/pallas_call | solution.py:70
  66.5 2.4 %collective-permute-start.6 = (bf16[256,1024]{1,0:T(8,128)(2,1)}, bf16[256,1024]{1,0:T(8,128)(2,1)}, u32[]{:S(2)}, u32[]{:S(2)}) collective-permute-start(bf16[256,1024]{1,0:T(8,128)(2,1)} %get-tuple-element.108), channel_id=1, source_target_pairs={{0,8},{8,0},{16,24},{24,16},{1,9},{9,1},{17,25},{25,17},{2,10},{10... | collective-permute-start | bytes 1572872 | tf_op jit(solution)/shard_map/ppermute | solution.py:322
  70.4 2.7 %collective-permute-done.8.refs_0_.refs_2_ = bf16[256,1024]{1,0:T(8,128)(2,1)S(1)} collective-permute-done((bf16[256,1024]{1,0:T(8,128)(2,1)}, bf16[256,1024]{1,0:T(8,128)(2,1)S(1)}, u32[]{:S(2)}, u32[]{:S(2)}) %collective-permute-start.8) | collective-permute-done | bytes 524320 | tf_op jit(solution)/shard_map/ppermute | solution.py:322
  73.1 2.2 %copy-done.1 = bf16[1,2048,1024]{2,1,0:T(8,128)(2,1)S(1)} copy-done((bf16[1,2048,1024]{2,1,0:T(8,128)(2,1)S(1)}, bf16[1,2048,1024]{2,1,0:T(8,128)(2,1)}, u32[]{:S(2)}) %copy-start.1) | copy-done | bytes 4194328
  75.3 2.0 %copy-done.4 = f32[1,2048,256]{2,1,0:T(8,128)S(1)} copy-done((f32[1,2048,256]{2,1,0:T(8,128)S(1)}, f32[1,2048,256]{2,1,0:T(8,128)}, u32[]{:S(2)}) %copy-start.4) | copy-done | bytes 2097176
  77.2 3.5 %round_4.1 = (bf16[256,1024]{1,0:T(8,128)(2,1)}, bf16[256,1024]{1,0:T(8,128)(2,1)}, bf16[2048,1024]{1,0:T(8,128)(2,1)}, f32[2,2048,256]{2,1,0:T(8,128)}, f32[2,2048,256]{2,1,0:T(8,128)}, /*index=5*/f32[8,128]{1,0:T(8,128)S(1)}) custom-call(s32[3]{0:T(128)S(1)} %pad_add_fusion.s, ...), custom_call_target="tpu_custom_call", output_to_operand_aliasing={{2}: (10, {}), {3}: (11, {}), {4}: (12, {})} | custom-call | tf_op jit(solution)/shard_map/round_4/pallas_call | solution.py:70
  80.7 2.5 %collective-permute-start.10 = (bf16[256,1024]{1,0:T(8,128)(2,1)}, bf16[256,1024]{1,0:T(8,128)(2,1)}, u32[]{:S(2)}, u32[]{:S(2)}) collective-permute-start(bf16[256,1024]{1,0:T(8,128)(2,1)} %get-tuple-element.122), channel_id=1, source_target_pairs={{0,8},{8,0},{16,24},{24,16},{1,9},{9,1},{17,25},{25,17},{2,10},{10... | collective-permute-start | bytes 1572872 | tf_op jit(solution)/shard_map/ppermute | solution.py:322
  84.7 3.5 %round_5.1 = (bf16[256,1024]{1,0:T(8,128)(2,1)}, bf16[256,1024]{1,0:T(8,128)(2,1)}, bf16[2048,1024]{1,0:T(8,128)(2,1)}, f32[2,2048,256]{2,1,0:T(8,128)}, f32[2,2048,256]{2,1,0:T(8,128)}, /*index=5*/f32[8,128]{1,0:T(8,128)S(1)}) custom-call(s32[3]{0:T(128)S(1)} %pad_add_fusion.s, ...), custom_call_target="tpu_custom_call", output_to_operand_aliasing={{2}: (10, {}), {3}: (11, {}), {4}: (12, {})} | custom-call | tf_op jit(solution)/shard_map/round_5/pallas_call | solution.py:70
  88.2 2.5 %collective-permute-start.14 = (bf16[256,1024]{1,0:T(8,128)(2,1)}, bf16[256,1024]{1,0:T(8,128)(2,1)S(1)}, u32[]{:S(2)}, u32[]{:S(2)}) collective-permute-start(bf16[256,1024]{1,0:T(8,128)(2,1)} %get-tuple-element.130), channel_id=1, source_target_pairs={{0,8},{8,0},{16,24},{24,16},{1,9},{9,1},{17,25},{25,17},{2,10},{10... | collective-permute-start | bytes 1572872 | tf_op jit(solution)/shard_map/ppermute | solution.py:322
  92.1 8.4 %project_0.1 = (f32[1024,1024]{1,0:T(8,128)S(1)}, f32[8,128]{1,0:T(8,128)S(1)}) custom-call(s32[3]{0:T(128)S(1)} %pad_add_fusion.s, bf16[1024,4096]{1,0:T(8,128)(2,1)} %refs_0_.9, bf16[4096,1024]{1,0:T(8,128)(2,1)} %bitcast.37, f32[8,128]{1,0:T(8,128)S(1)} %get-tuple-element.120.refs_2_), custom_call_target="tpu_custom_call" | custom-call | tf_op jit(solution)/shard_map/project_0/pallas_call | solution.py:70
  100.5 3.1 %round_6.1 = (bf16[256,1024]{1,0:T(8,128)(2,1)S(1)}, bf16[256,1024]{1,0:T(8,128)(2,1)S(1)}, bf16[2048,1024]{1,0:T(8,128)(2,1)}, f32[2,2048,256]{2,1,0:T(8,128)},...) custom-call(s32[3]{0:T(128)S(1)} %pad_add_fusion.s, ...), custom_call_target="tpu_custom_call", output_to_operand_aliasing={{2}: (10, {}), {3}: (11, {}), {4}: (12, {})} | custom-call | tf_op jit(solution)/shard_map/round_6/pallas_call | solution.py:70
  105.6 3.1 %round_7.1 = (bf16[256,1024]{1,0:T(8,128)(2,1)S(1)}, bf16[256,1024]{1,0:T(8,128)(2,1)S(1)}, bf16[2048,1024]{1,0:T(8,128)(2,1)}, f32[2,2048,256]{2,1,0:T(8,128)},...) custom-call(s32[3]{0:T(128)S(1)} %pad_add_fusion.s, ...), custom_call_target="tpu_custom_call", output_to_operand_aliasing={{2}: (10, {}), {3}: (11, {}), {4}: (12, {})} | custom-call | tf_op jit(solution)/shard_map/round_7/pallas_call | solution.py:70
  110.7 9.6 %collective-permute-done.12.refs_0_.refs_2_ = bf16[256,1024]{1,0:T(8,128)(2,1)S(1)} collective-permute-done((bf16[256,1024]{1,0:T(8,128)(2,1)S(1)}, bf16[256,1024]{1,0:T(8,128)(2,1)S(1)}, u32[]{:S(2)}, u32[]{:S(2)}) %collective-permute-start.12) | collective-permute-done | bytes 524320 | tf_op jit(solution)/shard_map/ppermute | solution.py:322
  120.2 2.9 %round_8.1 = (bf16[256,1024]{1,0:T(8,128)(2,1)S(1)}, bf16[2048,1024]{1,0:T(8,128)(2,1)}, f32[2,2048,256]{2,1,0:T(8,128)}, f32[2,2048,256]{2,1,0:T(8,128)}, f32[8,128]{1,0:T(8,128)S(1)}) custom-call(s32[3]{0:T(128)S(1)} %pad_add_fusion.s, ...), custom_call_target="tpu_custom_call", output_to_operand_aliasing={{1}: (10, {}), {2}: (11, {}), {3}: (12, {})} | custom-call | tf_op jit(solution)/shard_map/round_8/pallas_call | solution.py:70
  124.4 9.7 %project_1.1 = (bf16[1024,1024]{1,0:T(8,128)(2,1)}, f32[8,128]{1,0:T(8,128)S(1)}) custom-call(s32[3]{0:T(128)S(1)} %pad_add_fusion.s, bf16[1024,4096]{1,0:T(8,128)(2,1)} %refs_0_.9, bf16[4096,1024]{1,0:T(8,128)(2,1)} %bitcast.38, f32[1024,1024]{1,0:T(8,128)S(1)} %get-tuple-element.121.refs_2_, f32[8,128]{1,0:T(8,128)S(1)} %get-tuple-element.140.refs_3_), custom_call_target="tpu_custom_call" | custom-call | tf_op jit(solution)/shard_map/project_1/pallas_call | solution.py:70
  134.1 2.1 %round_9.1 = (bf16[256,1024]{1,0:T(8,128)(2,1)S(1)}, bf16[2048,1024]{1,0:T(8,128)(2,1)}, f32[2,2048,256]{2,1,0:T(8,128)}, f32[2,2048,256]{2,1,0:T(8,128)}, f32[8,128]{1,0:T(8,128)S(1)}) custom-call(s32[3]{0:T(128)S(1)} %pad_add_fusion.s, ...), custom_call_target="tpu_custom_call", output_to_operand_aliasing={{1}: (10, {}), {2}: (11, {}), {3}: (12, {})} | custom-call | tf_op jit(solution)/shard_map/round_9/pallas_call | solution.py:70
  137.5 5.2 %collective-permute-done.19.refs_0_.refs_1_ = bf16[256,1024]{1,0:T(8,128)(2,1)S(1)} collective-permute-done((bf16[256,1024]{1,0:T(8,128)(2,1)S(1)}, bf16[256,1024]{1,0:T(8,128)(2,1)S(1)}, u32[]{:S(2)}, u32[]{:S(2)}) %collective-permute-start.19) | collective-permute-done | bytes 524320 | tf_op jit(solution)/shard_map/ppermute | solution.py:322
  142.7 3.0 %round_10.1 = (bf16[2048,1024]{1,0:T(8,128)(2,1)}, f32[2,2048,256]{2,1,0:T(8,128)}, f32[2,2048,256]{2,1,0:T(8,128)}, f32[8,128]{1,0:T(8,128)S(1)}) custom-call(s32[3]{0:T(128)S(1)} %pad_add_fusion.s, bf16[256,1024]{1,0:T(8,128)(2,1)S(1)} %collective-permute-done.19.refs_0_.refs_1_, ...), custom_call_target="tpu_custom_call", output_to_operand_aliasing={{0}: (10, {}), {1}: (11, {}), {2}: (12, {})} | custom-call | tf_op jit(solution)/shard_map/round_10/pallas_call | solution.py:70
  145.7 5.2 %idle.1 = (f32[2,2048,256]{2,1,0:T(8,128)}, f32[2,2048,256]{2,1,0:T(8,128)}, f32[8,128]{1,0:T(8,128)S(1)}) custom-call(s32[3]{0:T(128)S(1)} %pad_add_fusion.s, f32[2,2048,256]{2,1,0:T(8,128)} %bitcast.29, f32[2,2048,256]{2,1,0:T(8,128)} %bitcast.35, f32[2,2048,256]{2,1,0:T(8,128)} %get-tuple-element.156.refs_2_, ...), custom_call_target="tpu_custom_call", output_to_operand_aliasing={{0}: (3, {}), {1}: (4, {})} | custom-call | tf_op jit(solution)/shard_map/idle/pallas_call | solution.py:70
  150.9 3.0 %round_11.1 = (bf16[2048,1024]{1,0:T(8,128)(2,1)}, f32[2,2048,256]{2,1,0:T(8,128)}, f32[2,2048,256]{2,1,0:T(8,128)}, f32[8,128]{1,0:T(8,128)S(1)}) custom-call(s32[3]{0:T(128)S(1)} %pad_add_fusion.s, bf16[256,1024]{1,0:T(8,128)(2,1)S(1)} %collective-permute-done.18.refs_0_.refs_1_, ...), custom_call_target="tpu_custom_call", output_to_operand_aliasing={{0}: (10, {}), {1}: (11, {}), {2}: (12, {})} | custom-call | flops 112000000000 | tf_op jit(solution)/shard_map/round_11/pallas_call | solution.py:70
  153.9 3.0 %widen.1 = (f32[512,1024]{1,0:T(8,128)}, f32[8,128]{1,0:T(8,128)}) custom-call(s32[3]{0:T(128)S(1)} %pad_add_fusion.s, bf16[512,1024]{1,0:T(8,128)(2,1)} %reduce-scatter.2.cloned.1.call-done.refs_0_, f32[8,128]{1,0:T(8,128)S(1)} %get-tuple-element.162.refs_1_), custom_call_target="tpu_custom_call" | custom-call | tf_op jit(solution)/shard_map/widen/pallas_call | solution.py:70
  (52 shorter events, 18.3 us)
Async XLA Ops:
  7.2 84.9 %all-gather.3.cloned.1.call-start = ((), (), s32[]{:S(2)}) async-start(), calls=%async_computation.2 | async-start | bytes 9437184 | tf_op jit(solution)/shard_map/all_gather | solution.py:96
  7.9 146.0 %reduce-scatter.2.cloned.1.call-start = ((), (), s32[]{:S(2)}) async-start(), calls=%async_computation.1 | async-start | bytes 9437184 | tf_op jit(solution)/shard_map/reduce_scatter | solution.py:148
  10.5 17.1 %collective-permute-start.1 = (bf16[256,1024]{1,0:T(8,128)(2,1)S(1)}, bf16[256,1024]{1,0:T(8,128)(2,1)S(1)}, u32[]{:S(2)}, u32[]{:S(2)}) collective-permute-start(bf16[256,1024]{1,0:T(8,128)(2,1)S(1)} %get-tuple-element.91), channel_id=1, source_target_pairs={{0,8},{24,16},{1,9},{25,17},{2,10},{26,18},{3,11},{27,19},{4,12},{... | collective-permute-start | bytes 1572872 | tf_op jit(solution)/shard_map/ppermute | solution.py:322
  17.2 27.2 %collective-permute-start = (bf16[256,1024]{1,0:T(8,128)(2,1)S(1)}, bf16[256,1024]{1,0:T(8,128)(2,1)S(1)}, u32[]{:S(2)}, u32[]{:S(2)}) collective-permute-start(bf16[256,1024]{1,0:T(8,128)(2,1)S(1)} %get-tuple-element.87), channel_id=1, source_target_pairs={{0,8},{24,16},{1,9},{25,17},{2,10},{26,18},{3,11},{27,19},{4,12},{... | collective-permute-start | bytes 1572872 | tf_op jit(solution)/shard_map/ppermute | solution.py:322
  26.0 38.3 %copy-start = (bf16[1,2048,1024]{2,1,0:T(8,128)(2,1)}, bf16[1,2048,1024]{2,1,0:T(8,128)(2,1)S(1)}, u32[]{:S(2)}) copy-start(bf16[1,2048,1024]{2,1,0:T(8,128)(2,1)S(1)} %get-tuple-element.89.refs_2_.refs_5_.refs_3_.refs_6_) | copy-start | bytes 12582916
  29.8 20.3 %collective-permute-start.4 = (bf16[256,1024]{1,0:T(8,128)(2,1)S(1)}, bf16[256,1024]{1,0:T(8,128)(2,1)S(1)}, u32[]{:S(2)}, u32[]{:S(2)}) collective-permute-start(bf16[256,1024]{1,0:T(8,128)(2,1)S(1)} %get-tuple-element.99), channel_id=1, source_target_pairs={{0,8},{24,16},{1,9},{25,17},{2,10},{26,18},{3,11},{27,19},{4,12},{... | collective-permute-start | bytes 1572872 | tf_op jit(solution)/shard_map/ppermute | solution.py:322
  34.6 15.6 %collective-permute-start.5 = (bf16[256,1024]{1,0:T(8,128)(2,1)S(1)}, bf16[256,1024]{1,0:T(8,128)(2,1)S(1)}, u32[]{:S(2)}, u32[]{:S(2)}) collective-permute-start(bf16[256,1024]{1,0:T(8,128)(2,1)S(1)} %get-tuple-element.100), channel_id=1, source_target_pairs={{8,16},{16,8},{9,17},{17,9},{10,18},{18,10},{11,19},{19,11},{12,20... | collective-permute-start | bytes 1572872 | tf_op jit(solution)/shard_map/ppermute | solution.py:322
  44.4 19.9 %copy-start.3 = (f32[1,2048,256]{2,1,0:T(8,128)}, f32[1,2048,256]{2,1,0:T(8,128)S(1)}, u32[]{:S(2)}) copy-start(f32[1,2048,256]{2,1,0:T(8,128)S(1)} %get-tuple-element.95.refs_4_.refs_7_.refs_5_.refs_8_) | copy-start | bytes 6291460
  45.0 19.2 %collective-permute-start.2 = (bf16[256,1024]{1,0:T(8,128)(2,1)S(1)}, bf16[256,1024]{1,0:T(8,128)(2,1)S(1)}, u32[]{:S(2)}, u32[]{:S(2)}) collective-permute-start(bf16[256,1024]{1,0:T(8,128)(2,1)S(1)} %get-tuple-element.97), channel_id=1, source_target_pairs={{0,8},{24,16},{1,9},{25,17},{2,10},{26,18},{3,11},{27,19},{4,12},{... | collective-permute-start | bytes 1572872 | tf_op jit(solution)/shard_map/ppermute | solution.py:322
  49.4 14.9 %collective-permute-start.3 = (bf16[256,1024]{1,0:T(8,128)(2,1)S(1)}, bf16[256,1024]{1,0:T(8,128)(2,1)S(1)}, u32[]{:S(2)}, u32[]{:S(2)}) collective-permute-start(bf16[256,1024]{1,0:T(8,128)(2,1)S(1)} %get-tuple-element.98), channel_id=1, source_target_pairs={{8,16},{16,8},{9,17},{17,9},{10,18},{18,10},{11,19},{19,11},{12,20... | collective-permute-start | bytes 1572872 | tf_op jit(solution)/shard_map/ppermute | solution.py:322
  52.3 20.7 %collective-permute-start.8 = (bf16[256,1024]{1,0:T(8,128)(2,1)}, bf16[256,1024]{1,0:T(8,128)(2,1)S(1)}, u32[]{:S(2)}, u32[]{:S(2)}) collective-permute-start(bf16[256,1024]{1,0:T(8,128)(2,1)} %get-tuple-element.110), channel_id=1, source_target_pairs={{0,8},{8,0},{16,24},{24,16},{1,9},{9,1},{17,25},{25,17},{2,10},{10... | collective-permute-start | bytes 1572872 | tf_op jit(solution)/shard_map/ppermute | solution.py:322
  55.1 17.9 %collective-permute-start.9 = (bf16[256,1024]{1,0:T(8,128)(2,1)}, bf16[256,1024]{1,0:T(8,128)(2,1)}, u32[]{:S(2)}, u32[]{:S(2)}) collective-permute-start(bf16[256,1024]{1,0:T(8,128)(2,1)} %get-tuple-element.111), channel_id=1, source_target_pairs={{8,16},{16,8},{9,17},{17,9},{10,18},{18,10},{11,19},{19,11},{12,20... | collective-permute-start | bytes 1572872 | tf_op jit(solution)/shard_map/ppermute | solution.py:322
  64.3 2.2 %copy-start.6 = (bf16[256,1024]{1,0:T(8,128)(2,1)}, bf16[256,1024]{1,0:T(8,128)(2,1)S(1)}, u32[]{:S(2)}) copy-start(bf16[256,1024]{1,0:T(8,128)(2,1)S(1)} %collective-permute-done.2.refs_0_.refs_2_) | copy-start | bytes 1572868
  66.5 18.2 %collective-permute-start.6 = (bf16[256,1024]{1,0:T(8,128)(2,1)}, bf16[256,1024]{1,0:T(8,128)(2,1)}, u32[]{:S(2)}, u32[]{:S(2)}) collective-permute-start(bf16[256,1024]{1,0:T(8,128)(2,1)} %get-tuple-element.108), channel_id=1, source_target_pairs={{0,8},{8,0},{16,24},{24,16},{1,9},{9,1},{17,25},{25,17},{2,10},{10... | collective-permute-start | bytes 1572872 | tf_op jit(solution)/shard_map/ppermute | solution.py:322
  68.9 15.8 %collective-permute-start.7 = (bf16[256,1024]{1,0:T(8,128)(2,1)}, bf16[256,1024]{1,0:T(8,128)(2,1)}, u32[]{:S(2)}, u32[]{:S(2)}) collective-permute-start(bf16[256,1024]{1,0:T(8,128)(2,1)} %get-tuple-element.109), channel_id=1, source_target_pairs={{8,16},{16,8},{9,17},{17,9},{10,18},{18,10},{11,19},{19,11},{12,20... | collective-permute-start | bytes 1572872 | tf_op jit(solution)/shard_map/ppermute | solution.py:322
  73.1 2.2 %copy-start.1 = (bf16[1,2048,1024]{2,1,0:T(8,128)(2,1)S(1)}, bf16[1,2048,1024]{2,1,0:T(8,128)(2,1)}, u32[]{:S(2)}) copy-start(bf16[1,2048,1024]{2,1,0:T(8,128)(2,1)} %copy-done) | copy-start | bytes 12582916
  75.3 2.0 %copy-start.4 = (f32[1,2048,256]{2,1,0:T(8,128)S(1)}, f32[1,2048,256]{2,1,0:T(8,128)}, u32[]{:S(2)}) copy-start(f32[1,2048,256]{2,1,0:T(8,128)} %copy-done.3) | copy-start | bytes 6291460
  77.2 7.5 %copy-start.7 = (bf16[256,1024]{1,0:T(8,128)(2,1)S(1)}, bf16[256,1024]{1,0:T(8,128)(2,1)}, u32[]{:S(2)}) copy-start(bf16[256,1024]{1,0:T(8,128)(2,1)} %copy-done.6) | copy-start | bytes 1572868
  80.7 19.7 %collective-permute-start.10 = (bf16[256,1024]{1,0:T(8,128)(2,1)}, bf16[256,1024]{1,0:T(8,128)(2,1)}, u32[]{:S(2)}, u32[]{:S(2)}) collective-permute-start(bf16[256,1024]{1,0:T(8,128)(2,1)} %get-tuple-element.122), channel_id=1, source_target_pairs={{0,8},{8,0},{16,24},{24,16},{1,9},{9,1},{17,25},{25,17},{2,10},{10... | collective-permute-start | bytes 1572872 | tf_op jit(solution)/shard_map/ppermute | solution.py:322
  83.2 17.2 %collective-permute-start.11 = (bf16[256,1024]{1,0:T(8,128)(2,1)}, bf16[256,1024]{1,0:T(8,128)(2,1)}, u32[]{:S(2)}, u32[]{:S(2)}) collective-permute-start(bf16[256,1024]{1,0:T(8,128)(2,1)} %get-tuple-element.123), channel_id=1, source_target_pairs={{8,16},{16,8},{9,17},{17,9},{10,18},{18,10},{11,19},{19,11},{12,20... | collective-permute-start | bytes 1572872 | tf_op jit(solution)/shard_map/ppermute | solution.py:322
  88.2 17.4 %collective-permute-start.14 = (bf16[256,1024]{1,0:T(8,128)(2,1)}, bf16[256,1024]{1,0:T(8,128)(2,1)S(1)}, u32[]{:S(2)}, u32[]{:S(2)}) collective-permute-start(bf16[256,1024]{1,0:T(8,128)(2,1)} %get-tuple-element.130), channel_id=1, source_target_pairs={{0,8},{8,0},{16,24},{24,16},{1,9},{9,1},{17,25},{25,17},{2,10},{10... | collective-permute-start | bytes 1572872 | tf_op jit(solution)/shard_map/ppermute | solution.py:322
  90.6 15.0 %collective-permute-start.15 = (bf16[256,1024]{1,0:T(8,128)(2,1)}, bf16[256,1024]{1,0:T(8,128)(2,1)}, u32[]{:S(2)}, u32[]{:S(2)}) collective-permute-start(bf16[256,1024]{1,0:T(8,128)(2,1)} %get-tuple-element.131), channel_id=1, source_target_pairs={{8,16},{16,8},{9,17},{17,9},{10,18},{18,10},{11,19},{19,11},{12,20... | collective-permute-start | bytes 1572872 | tf_op jit(solution)/shard_map/ppermute | solution.py:322
  92.1 8.4 %copy-start.2 = (bf16[1,2048,1024]{2,1,0:T(8,128)(2,1)S(1)}, bf16[1,2048,1024]{2,1,0:T(8,128)(2,1)}, u32[]{:S(2)}) copy-start(bf16[1,2048,1024]{2,1,0:T(8,128)(2,1)} %copy-done) | copy-start | bytes 12582916
  92.1 8.4 %copy-start.5 = (f32[1,2048,256]{2,1,0:T(8,128)S(1)}, f32[1,2048,256]{2,1,0:T(8,128)}, u32[]{:S(2)}) copy-start(f32[1,2048,256]{2,1,0:T(8,128)} %copy-done.3) | copy-start | bytes 6291460
  103.6 16.6 %collective-permute-start.12 = (bf16[256,1024]{1,0:T(8,128)(2,1)S(1)}, bf16[256,1024]{1,0:T(8,128)(2,1)S(1)}, u32[]{:S(2)}, u32[]{:S(2)}) collective-permute-start(bf16[256,1024]{1,0:T(8,128)(2,1)S(1)} %get-tuple-element.128), channel_id=1, source_target_pairs={{8,0},{16,24},{9,1},{17,25},{10,2},{18,26},{11,3},{19,27},{12,4},{... | collective-permute-start | bytes 1572872 | tf_op jit(solution)/shard_map/ppermute | solution.py:322
  104.9 15.4 %collective-permute-start.13 = (bf16[256,1024]{1,0:T(8,128)(2,1)S(1)}, bf16[256,1024]{1,0:T(8,128)(2,1)S(1)}, u32[]{:S(2)}, u32[]{:S(2)}) collective-permute-start(bf16[256,1024]{1,0:T(8,128)(2,1)S(1)} %get-tuple-element.129), channel_id=1, source_target_pairs={{8,16},{16,8},{9,17},{17,9},{10,18},{18,10},{11,19},{19,11},{12,20... | collective-permute-start | bytes 1572872 | tf_op jit(solution)/shard_map/ppermute | solution.py:322
  108.7 25.4 %collective-permute-start.16 = (bf16[256,1024]{1,0:T(8,128)(2,1)S(1)}, bf16[256,1024]{1,0:T(8,128)(2,1)S(1)}, u32[]{:S(2)}, u32[]{:S(2)}) collective-permute-start(bf16[256,1024]{1,0:T(8,128)(2,1)S(1)} %get-tuple-element.143), channel_id=1, source_target_pairs={{8,0},{16,24},{9,1},{17,25},{10,2},{18,26},{11,3},{19,27},{12,4},{... | collective-permute-start | bytes 1572872 | tf_op jit(solution)/shard_map/ppermute | solution.py:322
  110.0 24.2 %collective-permute-start.17 = (bf16[256,1024]{1,0:T(8,128)(2,1)S(1)}, bf16[256,1024]{1,0:T(8,128)(2,1)S(1)}, u32[]{:S(2)}, u32[]{:S(2)}) collective-permute-start(bf16[256,1024]{1,0:T(8,128)(2,1)S(1)} %get-tuple-element.144), channel_id=1, source_target_pairs={{8,16},{16,8},{9,17},{17,9},{10,18},{18,10},{11,19},{19,11},{12,20... | collective-permute-start | bytes 1572872 | tf_op jit(solution)/shard_map/ppermute | solution.py:322
  123.2 19.5 %collective-permute-start.19 = (bf16[256,1024]{1,0:T(8,128)(2,1)S(1)}, bf16[256,1024]{1,0:T(8,128)(2,1)S(1)}, u32[]{:S(2)}, u32[]{:S(2)}) collective-permute-start(bf16[256,1024]{1,0:T(8,128)(2,1)S(1)} %get-tuple-element.150), channel_id=1, source_target_pairs={{8,0},{16,24},{9,1},{17,25},{10,2},{18,26},{11,3},{19,27},{12,4},{... | collective-permute-start | bytes 1572872 | tf_op jit(solution)/shard_map/ppermute | solution.py:322
  136.2 14.7 %collective-permute-start.18 = (bf16[256,1024]{1,0:T(8,128)(2,1)S(1)}, bf16[256,1024]{1,0:T(8,128)(2,1)S(1)}, u32[]{:S(2)}, u32[]{:S(2)}) collective-permute-start(bf16[256,1024]{1,0:T(8,128)(2,1)S(1)} %get-tuple-element.149), channel_id=1, source_target_pairs={{8,0},{16,24},{9,1},{17,25},{10,2},{18,26},{11,3},{19,27},{12,4},{... | collective-permute-start | bytes 1572872 | tf_op jit(solution)/shard_map/ppermute | solution.py:322
Sparse Core Ops, SparseCore 0:
  9.9 57.0 all-gather.2
  70.5 71.2 reduce-scatter.1

commit v3 on v2

--- a/solution.py
+++ b/solution.py
@@ -8,13 +8,13 @@
 from jax.sharding import PartitionSpec as P
 
 FRAGS = 2
-PIECES = 8
+PIECES = 10
 STEPS = 1
 DELAY = 2
 PROJECT_BLOCKS = 4
 GRADS = ((0, 2, (0,), -1), (2, 3, (1, 2), 0), (5, 3, (), 2))
-IDLE_BEFORE = 1
-PROJECT_ROUNDS = (5, 8)
+IDLE_BEFORE = 5
+PROJECT_ROUNDS = (6, 10)
 MEAN_PART = 1.33
 GLOBAL_PART = -0.33
 MOMENT_PART = -0.567
@@ -23,10 +23,10 @@
 ANY = pl.BlockSpec(memory_space=pl.ANY)
 CONTRACT_ROWS = (((0,), (0,)), ((), ()))
 CHOSEN, REPLICA, FSDP = 0, 1, 2
-VMEM = 18 << 20
+VMEM = 14 << 20
 VMEM_R = 10 << 20
 VMEM_P = 16 << 20
-LONG = 112 * 10**9
+LONG = 116 * 10**9
 
 
 def in_vmem(x):

time: 165 us -> 162 us (0.982)
  waiting for transfers between devices: 19.9 us -> 13.7 us
  starting transfers between devices: 39.2 us -> 42.3 us
    ppermute x20 -> x24, waiting for transfers between devices: 19.2 us -> 13 us  [send(): lax.ppermute(x, 'replica', self.pairs(t, path))]
    ppermute x20 -> x24, starting transfers between devices: 39.1 us -> 42.2 us  [send(): lax.ppermute(x, 'replica', self.pairs(t, path))]
    pallas_call x21 -> x23, Pallas kernels: 85.4 us -> 86.1 us  [call(): pl.pallas_call(kernel, out_shape=out_shape, grid_spec=pltpu.PrefetchScala...]
    unnamed x16 -> x20, local copies, waits for them, and re-layouts: 4.18 us -> 3.8 us
  transfers between devices with their start and end apart: 22 -> 26, of which waited for: 4 -> 5; matrix products, arithmetic and copies ran while one was open for 0% -> 0% of each run, Pallas kernels for 50% -> 52%
where the time goes in v3:
time: 162 us; the launch traced here: 161 us
  Pallas kernels  86.1 us (53%)
  starting transfers between devices  42.3 us (26%)
  between operations  15 us (9%)
  waiting for transfers between devices  13.7 us (8%)
  local copies, waits for them, and re-layouts  3.8 us (2%)
    pallas_call x23, Pallas kernels, call(): pl.pallas_call(kernel, out_shape=out_shape, grid_spec=pltpu.PrefetchScala...  86.1 us
    ppermute x24, starting transfers between devices, send(): lax.ppermute(x, 'replica', self.pairs(t, path))  42.2 us
    ppermute x24, waiting for transfers between devices, send(): lax.ppermute(x, 'replica', self.pairs(t, path))  13 us
    unnamed x20, local copies, waits for them, and re-layouts  3.8 us
  transfers between devices with their start and end apart: 26, of which 5 were waited for; matrix products, arithmetic and copies ran while one was open for 0% of the time, Pallas kernels for 52%

profile of v3, /device:TPU:0, one launch (start us, length us, event | category | flops | bytes accessed | tf_op | source)
XLA Modules:
  0.0 161.0 jit_solution(4435939029016560413)
XLA Ops:
  8.7 1.8 %first_sends.2 = (bf16[208,1024]{1,0:T(8,128)(2,1)S(1)}, f32[8,128]{1,0:T(8,128)S(1)}) custom-call(s32[3]{0:T(128)S(1)} %pad_add_fusion.s, bf16[2,2048,1024]{2,1,0:T(8,128)(2,1)} %bitcast.19, f32[2,2048,256]{2,1,0:T(8,128)} %bitcast.24, f32[2,2048,256]{2,1,0:T(8,128)} %bitcast.30), custom_call_target="tpu_custom_call" | custom-call | tf_op jit(solution)/shard_map/first_sends/pallas_call | solution.py:70
  10.5 4.9 %collective-permute-start = (bf16[208,1024]{1,0:T(8,128)(2,1)S(1)}, bf16[208,1024]{1,0:T(8,128)(2,1)S(1)}, u32[]{:S(2)}, u32[]{:S(2)}) collective-permute-start(bf16[208,1024]{1,0:T(8,128)(2,1)S(1)} %get-tuple-element.98), channel_id=1, source_target_pairs={{0,8},{24,16},{1,9},{25,17},{2,10},{26,18},{3,11},{27,19},{4,12},{... | collective-permute-start | bytes 1277960 | tf_op jit(solution)/shard_map/ppermute | solution.py:322
  15.4 1.8 %first_sends.3 = (bf16[208,1024]{1,0:T(8,128)(2,1)S(1)}, f32[8,128]{1,0:T(8,128)S(1)}) custom-call(s32[3]{0:T(128)S(1)} %pad_add_fusion.s, bf16[2,2048,1024]{2,1,0:T(8,128)(2,1)} %bitcast.20, f32[2,2048,256]{2,1,0:T(8,128)} %bitcast.25, f32[2,2048,256]{2,1,0:T(8,128)} %bitcast.31, f32[8,128]{1,0:T(8,128)S(1)} %get-tuple-element.99.refs_3_), custom_call_target="tpu_custom_call" | custom-call | tf_op jit(solution)/shard_map/first_sends/pallas_call | solution.py:70
  18.5 7.4 %grad_0.1 = (bf16[8,512,1024]{2,1,0:T(8,128)(2,1)}, bf16[1,2048,1024]{2,1,0:T(8,128)(2,1)S(1)}, f32[8,128]{1,0:T(8,128)S(1)}) custom-call(s32[3]{0:T(128)S(1)} %pad_add_fusion.s, bf16[1024,4096]{1,0:T(8,128)(2,1)} %refs_0_.9, bf16[1024,1024]{1,0:T(8,128)(2,1)} %refs_1_.5, bf16[2,2048,1024]{2,1,0:T(8,128)(2,1)} %bitcast.21, ...), custom_call_target="tpu_custom_call" | custom-call | tf_op jit(solution)/shard_map/grad_0/pallas_call | solution.py:70
  25.9 3.0 %round_0.1 = (bf16[208,1024]{1,0:T(8,128)(2,1)S(1)}, bf16[208,1024]{1,0:T(8,128)(2,1)S(1)}, f32[8,128]{1,0:T(8,128)S(1)}) custom-call(s32[3]{0:T(128)S(1)} %pad_add_fusion.s, bf16[208,1024]{1,0:T(8,128)(2,1)S(1)} %collective-permute-done.refs_0_.refs_1_.refs_2_, bf16[208,1024]{1,0:T(8,128)(2,1)S(1)} %collective-permute-done.refs_0_.refs_1_.refs_2_, ...), custom_call_target="tpu_custom_call" | custom-call | tf_op jit(solution)/shard_map/round_0/pallas_call | solution.py:70
  28.9 3.3 %collective-permute-start.1 = (bf16[208,1024]{1,0:T(8,128)(2,1)S(1)}, bf16[208,1024]{1,0:T(8,128)(2,1)S(1)}, u32[]{:S(2)}, u32[]{:S(2)}) collective-permute-start(bf16[208,1024]{1,0:T(8,128)(2,1)S(1)} %get-tuple-element.102), channel_id=1, source_target_pairs={{0,8},{24,16},{1,9},{25,17},{2,10},{26,18},{3,11},{27,19},{4,12},{... | collective-permute-start | bytes 1277960 | tf_op jit(solution)/shard_map/ppermute | solution.py:322
  33.0 8.9 %grad_2.1 = (bf16[8,512,1024]{2,1,0:T(8,128)(2,1)}, f32[1,2048,256]{2,1,0:T(8,128)S(1)}, f32[1,2048,256]{2,1,0:T(8,128)S(1)}, f32[8,128]{1,0:T(8,128)S(1)}) custom-call(s32[3]{0:T(128)S(1)} %pad_add_fusion.s, bf16[1024,4096]{1,0:T(8,128)(2,1)} %refs_0_.9, bf16[1024,1024]{1,0:T(8,128)(2,1)} %refs_1_.5, ...), custom_call_target="tpu_custom_call", output_to_operand_aliasing={{0}: (3, {})} | custom-call | tf_op jit(solution)/shard_map/grad_2/pallas_call | solution.py:70
  42.5 4.3 %collective-permute-start.6 = (bf16[208,1024]{1,0:T(8,128)(2,1)S(1)}, bf16[208,1024]{1,0:T(8,128)(2,1)S(1)}, u32[]{:S(2)}, u32[]{:S(2)}) collective-permute-start(bf16[208,1024]{1,0:T(8,128)(2,1)S(1)} %get-tuple-element.114), channel_id=1, source_target_pairs={{0,8},{24,16},{1,9},{25,17},{2,10},{26,18},{3,11},{27,19},{4,12},{... | collective-permute-start | bytes 1277960 | tf_op jit(solution)/shard_map/ppermute | solution.py:322
  47.5 2.0 %round_2.1 = (bf16[208,1024]{1,0:T(8,128)(2,1)}, bf16[208,1024]{1,0:T(8,128)(2,1)}, bf16[2048,1024]{1,0:T(8,128)(2,1)}, f32[2,2048,256]{2,1,0:T(8,128)}, f32[2,2048,256]{2,1,0:T(8,128)}, /*index=5*/f32[8,128]{1,0:T(8,128)S(1)}) custom-call(s32[3]{0:T(128)S(1)} %pad_add_fusion.s, ...), custom_call_target="tpu_custom_call" | custom-call | tf_op jit(solution)/shard_map/round_2/pallas_call | solution.py:70
  52.3 7.6 %grad_5.1 = (bf16[8,512,1024]{2,1,0:T(8,128)(2,1)}, f32[8,128]{1,0:T(8,128)S(1)}) custom-call(s32[3]{0:T(128)S(1)} %pad_add_fusion.s, bf16[1024,4096]{1,0:T(8,128)(2,1)} %refs_0_.9, bf16[1024,1024]{1,0:T(8,128)(2,1)} %refs_1_.5, bf16[8,512,1024]{2,1,0:T(8,128)(2,1)} %get-tuple-element.119.refs_2_, ...), custom_call_target="tpu_custom_call", output_to_operand_aliasing={{0}: (3, {})} | custom-call | tf_op jit(solution)/shard_map/grad_5/pallas_call | solution.py:70
  60.0 2.0 %round_3.1 = (bf16[208,1024]{1,0:T(8,128)(2,1)}, bf16[208,1024]{1,0:T(8,128)(2,1)}, bf16[2048,1024]{1,0:T(8,128)(2,1)}, f32[2,2048,256]{2,1,0:T(8,128)}, f32[2,2048,256]{2,1,0:T(8,128)}, /*index=5*/f32[8,128]{1,0:T(8,128)S(1)}) custom-call(s32[3]{0:T(128)S(1)} %pad_add_fusion.s, ...), custom_call_target="tpu_custom_call", output_to_operand_aliasing={{2}: (10, {}), {3}: (11, {}), {4}: (12, {})} | custom-call | tf_op jit(solution)/shard_map/round_3/pallas_call | solution.py:70
  62.0 2.4 %collective-permute-start.10 = (bf16[208,1024]{1,0:T(8,128)(2,1)}, bf16[208,1024]{1,0:T(8,128)(2,1)S(1)}, u32[]{:S(2)}, u32[]{:S(2)}) collective-permute-start(bf16[208,1024]{1,0:T(8,128)(2,1)} %get-tuple-element.128), channel_id=1, source_target_pairs={{0,8},{8,0},{16,24},{24,16},{1,9},{9,1},{17,25},{25,17},{2,10},{10... | collective-permute-start | bytes 1277960 | tf_op jit(solution)/shard_map/ppermute | solution.py:322
  65.8 2.2 %copy-done.1 = bf16[1,2048,1024]{2,1,0:T(8,128)(2,1)S(1)} copy-done((bf16[1,2048,1024]{2,1,0:T(8,128)(2,1)S(1)}, bf16[1,2048,1024]{2,1,0:T(8,128)(2,1)}, u32[]{:S(2)}) %copy-start.1) | copy-done | bytes 4194328
  69.6 2.7 %round_4.1 = (bf16[208,1024]{1,0:T(8,128)(2,1)S(1)}, bf16[208,1024]{1,0:T(8,128)(2,1)S(1)}, bf16[2048,1024]{1,0:T(8,128)(2,1)}, f32[2,2048,256]{2,1,0:T(8,128)},...) custom-call(s32[3]{0:T(128)S(1)} %pad_add_fusion.s, ...), custom_call_target="tpu_custom_call", output_to_operand_aliasing={{2}: (10, {}), {3}: (11, {}), {4}: (12, {})} | custom-call | tf_op jit(solution)/shard_map/round_4/pallas_call | solution.py:70
  72.3 2.0 %collective-permute-start.8 = (bf16[208,1024]{1,0:T(8,128)(2,1)S(1)}, bf16[208,1024]{1,0:T(8,128)(2,1)S(1)}, u32[]{:S(2)}, u32[]{:S(2)}) collective-permute-start(bf16[208,1024]{1,0:T(8,128)(2,1)S(1)} %get-tuple-element.126), channel_id=1, source_target_pairs={{0,8},{8,0},{16,24},{24,16},{1,9},{9,1},{17,25},{25,17},{2,10},{10... | collective-permute-start | bytes 1277960 | tf_op jit(solution)/shard_map/ppermute | solution.py:322
  75.0 3.2 %round_5.1 = (bf16[208,1024]{1,0:T(8,128)(2,1)}, bf16[208,1024]{1,0:T(8,128)(2,1)}, bf16[2048,1024]{1,0:T(8,128)(2,1)}, f32[2,2048,256]{2,1,0:T(8,128)}, f32[2,2048,256]{2,1,0:T(8,128)}, /*index=5*/f32[8,128]{1,0:T(8,128)S(1)}) custom-call(s32[3]{0:T(128)S(1)} %pad_add_fusion.s, ...), custom_call_target="tpu_custom_call", output_to_operand_aliasing={{2}: (10, {}), {3}: (11, {}), {4}: (12, {})} | custom-call | tf_op jit(solution)/shard_map/round_5/pallas_call | solution.py:70
  78.3 2.5 %collective-permute-start.14 = (bf16[208,1024]{1,0:T(8,128)(2,1)}, bf16[208,1024]{1,0:T(8,128)(2,1)S(1)}, u32[]{:S(2)}, u32[]{:S(2)}) collective-permute-start(bf16[208,1024]{1,0:T(8,128)(2,1)} %get-tuple-element.142), channel_id=1, source_target_pairs={{0,8},{8,0},{16,24},{24,16},{1,9},{9,1},{17,25},{25,17},{2,10},{10... | collective-permute-start | bytes 1277960 | tf_op jit(solution)/shard_map/ppermute | solution.py:322
  82.2 2.4 %collective-permute-done.8.refs_0_.refs_2_ = bf16[208,1024]{1,0:T(8,128)(2,1)S(1)} collective-permute-done((bf16[208,1024]{1,0:T(8,128)(2,1)S(1)}, bf16[208,1024]{1,0:T(8,128)(2,1)S(1)}, u32[]{:S(2)}, u32[]{:S(2)}) %collective-permute-start.8) | collective-permute-done | bytes 426016 | tf_op jit(solution)/shard_map/ppermute | solution.py:322
  84.6 2.0 %round_6.1 = (bf16[208,1024]{1,0:T(8,128)(2,1)}, bf16[208,1024]{1,0:T(8,128)(2,1)}, bf16[2048,1024]{1,0:T(8,128)(2,1)}, f32[2,2048,256]{2,1,0:T(8,128)}, f32[2,2048,256]{2,1,0:T(8,128)}, /*index=5*/f32[8,128]{1,0:T(8,128)S(1)}) custom-call(s32[3]{0:T(128)S(1)} %pad_add_fusion.s, ...), custom_call_target="tpu_custom_call", output_to_operand_aliasing={{2}: (10, {}), {3}: (11, {}), {4}: (12, {})} | custom-call | tf_op jit(solution)/shard_map/round_6/pallas_call | solution.py:70
  86.6 3.6 %collective-permute-start.12 = (bf16[208,1024]{1,0:T(8,128)(2,1)}, bf16[208,1024]{1,0:T(8,128)(2,1)S(1)}, u32[]{:S(2)}, u32[]{:S(2)}) collective-permute-start(bf16[208,1024]{1,0:T(8,128)(2,1)} %get-tuple-element.140), channel_id=1, source_target_pairs={{0,8},{8,0},{16,24},{24,16},{1,9},{9,1},{17,25},{25,17},{2,10},{10... | collective-permute-start | bytes 1277960 | tf_op jit(solution)/shard_map/ppermute | solution.py:322
  91.6 8.4 %project_0.1 = (f32[1024,1024]{1,0:T(8,128)S(1)}, f32[8,128]{1,0:T(8,128)S(1)}) custom-call(s32[3]{0:T(128)S(1)} %pad_add_fusion.s, bf16[1024,4096]{1,0:T(8,128)(2,1)} %refs_0_.9, bf16[4096,1024]{1,0:T(8,128)(2,1)} %bitcast.37, f32[8,128]{1,0:T(8,128)S(1)} %get-tuple-element.138.refs_2_), custom_call_target="tpu_custom_call" | custom-call | tf_op jit(solution)/shard_map/project_0/pallas_call | solution.py:70
  100.0 2.8 %round_7.1 = (bf16[208,1024]{1,0:T(8,128)(2,1)S(1)}, bf16[208,1024]{1,0:T(8,128)(2,1)S(1)}, bf16[2048,1024]{1,0:T(8,128)(2,1)}, f32[2,2048,256]{2,1,0:T(8,128)},...) custom-call(s32[3]{0:T(128)S(1)} %pad_add_fusion.s, ...), custom_call_target="tpu_custom_call", output_to_operand_aliasing={{2}: (10, {}), {3}: (11, {}), {4}: (12, {})} | custom-call | tf_op jit(solution)/shard_map/round_7/pallas_call | solution.py:70
  105.0 2.8 %round_8.1 = (bf16[208,1024]{1,0:T(8,128)(2,1)S(1)}, bf16[208,1024]{1,0:T(8,128)(2,1)S(1)}, bf16[2048,1024]{1,0:T(8,128)(2,1)}, f32[2,2048,256]{2,1,0:T(8,128)},...) custom-call(s32[3]{0:T(128)S(1)} %pad_add_fusion.s, ...), custom_call_target="tpu_custom_call", output_to_operand_aliasing={{2}: (10, {}), {3}: (11, {}), {4}: (12, {})} | custom-call | tf_op jit(solution)/shard_map/round_8/pallas_call | solution.py:70
  109.7 5.4 %idle.1 = (f32[2,2048,256]{2,1,0:T(8,128)}, f32[2,2048,256]{2,1,0:T(8,128)}, f32[8,128]{1,0:T(8,128)S(1)}) custom-call(s32[3]{0:T(128)S(1)} %pad_add_fusion.s, f32[2,2048,256]{2,1,0:T(8,128)} %bitcast.29, f32[2,2048,256]{2,1,0:T(8,128)} %bitcast.35, f32[2,2048,256]{2,1,0:T(8,128)} %get-tuple-element.157.refs_2_, ...), custom_call_target="tpu_custom_call", output_to_operand_aliasing={{0}: (3, {}), {1}: (4, {})} | custom-call | tf_op jit(solution)/shard_map/idle/pallas_call | solution.py:70
  115.1 1.7 %round_9.1 = (bf16[208,1024]{1,0:T(8,128)(2,1)S(1)}, bf16[208,1024]{1,0:T(8,128)(2,1)S(1)}, bf16[2048,1024]{1,0:T(8,128)(2,1)}, f32[2,2048,256]{2,1,0:T(8,128)},...) custom-call(s32[3]{0:T(128)S(1)} %pad_add_fusion.s, ...), custom_call_target="tpu_custom_call", output_to_operand_aliasing={{2}: (10, {}), {3}: (11, {}), {4}: (12, {})} | custom-call | tf_op jit(solution)/shard_map/round_9/pallas_call | solution.py:70
  118.9 3.2 %collective-permute-done.16.refs_0_.refs_2_ = bf16[208,1024]{1,0:T(8,128)(2,1)S(1)} collective-permute-done((bf16[208,1024]{1,0:T(8,128)(2,1)S(1)}, bf16[208,1024]{1,0:T(8,128)(2,1)S(1)}, u32[]{:S(2)}, u32[]{:S(2)}) %collective-permute-start.16) | collective-permute-done | bytes 426016 | tf_op jit(solution)/shard_map/ppermute | solution.py:322
  125.3 9.8 %project_1.1 = (bf16[1024,1024]{1,0:T(8,128)(2,1)}, f32[8,128]{1,0:T(8,128)S(1)}) custom-call(s32[3]{0:T(128)S(1)} %pad_add_fusion.s, bf16[1024,4096]{1,0:T(8,128)(2,1)} %refs_0_.9, bf16[4096,1024]{1,0:T(8,128)(2,1)} %bitcast.38, f32[1024,1024]{1,0:T(8,128)S(1)} %get-tuple-element.139.refs_2_, f32[8,128]{1,0:T(8,128)S(1)} %get-tuple-element.167.refs_3_), custom_call_target="tpu_custom_call" | custom-call | tf_op jit(solution)/shard_map/project_1/pallas_call | solution.py:70
  135.1 1.8 %round_11.1 = (bf16[208,1024]{1,0:T(8,128)(2,1)S(1)}, bf16[2048,1024]{1,0:T(8,128)(2,1)}, f32[2,2048,256]{2,1,0:T(8,128)}, f32[2,2048,256]{2,1,0:T(8,128)}, f32[8,128]{1,0:T(8,128)S(1)}) custom-call(s32[3]{0:T(128)S(1)} %pad_add_fusion.s, ...), custom_call_target="tpu_custom_call", output_to_operand_aliasing={{1}: (10, {}), {2}: (11, {}), {3}: (12, {})} | custom-call | tf_op jit(solution)/shard_map/round_11/pallas_call | solution.py:70
  139.8 2.8 %round_12.1 = (bf16[2048,1024]{1,0:T(8,128)(2,1)}, f32[2,2048,256]{2,1,0:T(8,128)}, f32[2,2048,256]{2,1,0:T(8,128)}, f32[8,128]{1,0:T(8,128)S(1)}) custom-call(s32[3]{0:T(128)S(1)} %pad_add_fusion.s, bf16[208,1024]{1,0:T(8,128)(2,1)S(1)} %collective-permute-done.23.refs_0_.refs_1_, ...), custom_call_target="tpu_custom_call", output_to_operand_aliasing={{0}: (10, {}), {1}: (11, {}), {2}: (12, {})} | custom-call | tf_op jit(solution)/shard_map/round_12/pallas_call | solution.py:70
  142.6 5.7 %collective-permute-done.22.refs_0_.refs_1_ = bf16[208,1024]{1,0:T(8,128)(2,1)S(1)} collective-permute-done((bf16[208,1024]{1,0:T(8,128)(2,1)S(1)}, bf16[208,1024]{1,0:T(8,128)(2,1)S(1)}, u32[]{:S(2)}, u32[]{:S(2)}) %collective-permute-start.22) | collective-permute-done | bytes 426016 | tf_op jit(solution)/shard_map/ppermute | solution.py:322
  148.3 2.8 %round_13.1 = (bf16[2048,1024]{1,0:T(8,128)(2,1)}, f32[2,2048,256]{2,1,0:T(8,128)}, f32[2,2048,256]{2,1,0:T(8,128)}, f32[8,128]{1,0:T(8,128)S(1)}) custom-call(s32[3]{0:T(128)S(1)} %pad_add_fusion.s, bf16[208,1024]{1,0:T(8,128)(2,1)S(1)} %collective-permute-done.22.refs_0_.refs_1_, ...), custom_call_target="tpu_custom_call", output_to_operand_aliasing={{0}: (10, {}), {1}: (11, {}), {2}: (12, {})} | custom-call | flops 115999997952 | tf_op jit(solution)/shard_map/round_13/pallas_call | solution.py:70
  151.2 3.0 %widen.1 = (f32[512,1024]{1,0:T(8,128)}, f32[8,128]{1,0:T(8,128)}) custom-call(s32[3]{0:T(128)S(1)} %pad_add_fusion.s, bf16[512,1024]{1,0:T(8,128)(2,1)} %reduce-scatter.2.cloned.1.call-done.refs_0_, f32[8,128]{1,0:T(8,128)S(1)} %get-tuple-element.186.refs_1_), custom_call_target="tpu_custom_call" | custom-call | tf_op jit(solution)/shard_map/widen/pallas_call | solution.py:70
  (66 shorter events, 25.8 us)
Async XLA Ops:
  7.2 84.4 %all-gather.3.cloned.1.call-start = ((), (), s32[]{:S(2)}) async-start(), calls=%async_computation.2 | async-start | bytes 9437184 | tf_op jit(solution)/shard_map/all_gather | solution.py:96
  7.9 143.3 %reduce-scatter.2.cloned.1.call-start = ((), (), s32[]{:S(2)}) async-start(), calls=%async_computation.1 | async-start | bytes 9437184 | tf_op jit(solution)/shard_map/reduce_scatter | solution.py:148
  10.5 15.4 %collective-permute-start = (bf16[208,1024]{1,0:T(8,128)(2,1)S(1)}, bf16[208,1024]{1,0:T(8,128)(2,1)S(1)}, u32[]{:S(2)}, u32[]{:S(2)}) collective-permute-start(bf16[208,1024]{1,0:T(8,128)(2,1)S(1)} %get-tuple-element.98), channel_id=1, source_target_pairs={{0,8},{24,16},{1,9},{25,17},{2,10},{26,18},{3,11},{27,19},{4,12},{... | collective-permute-start | bytes 1277960 | tf_op jit(solution)/shard_map/ppermute | solution.py:322
  17.2 24.7 %collective-permute-start.3 = (bf16[208,1024]{1,0:T(8,128)(2,1)S(1)}, bf16[208,1024]{1,0:T(8,128)(2,1)S(1)}, u32[]{:S(2)}, u32[]{:S(2)}) collective-permute-start(bf16[208,1024]{1,0:T(8,128)(2,1)S(1)} %get-tuple-element.109), channel_id=1, source_target_pairs={{0,8},{24,16},{1,9},{25,17},{2,10},{26,18},{3,11},{27,19},{4,12},{... | collective-permute-start | bytes 1277960 | tf_op jit(solution)/shard_map/ppermute | solution.py:322
  25.9 34.0 %copy-start = (bf16[1,2048,1024]{2,1,0:T(8,128)(2,1)}, bf16[1,2048,1024]{2,1,0:T(8,128)(2,1)S(1)}, u32[]{:S(2)}) copy-start(bf16[1,2048,1024]{2,1,0:T(8,128)(2,1)S(1)} %get-tuple-element.104.refs_2_.refs_5_.refs_3_.refs_6_) | copy-start | bytes 12582916
  28.9 18.6 %collective-permute-start.1 = (bf16[208,1024]{1,0:T(8,128)(2,1)S(1)}, bf16[208,1024]{1,0:T(8,128)(2,1)S(1)}, u32[]{:S(2)}, u32[]{:S(2)}) collective-permute-start(bf16[208,1024]{1,0:T(8,128)(2,1)S(1)} %get-tuple-element.102), channel_id=1, source_target_pairs={{0,8},{24,16},{1,9},{25,17},{2,10},{26,18},{3,11},{27,19},{4,12},{... | collective-permute-start | bytes 1277960 | tf_op jit(solution)/shard_map/ppermute | solution.py:322
  32.3 15.2 %collective-permute-start.2 = (bf16[208,1024]{1,0:T(8,128)(2,1)S(1)}, bf16[208,1024]{1,0:T(8,128)(2,1)S(1)}, u32[]{:S(2)}, u32[]{:S(2)}) collective-permute-start(bf16[208,1024]{1,0:T(8,128)(2,1)S(1)} %get-tuple-element.103), channel_id=1, source_target_pairs={{8,16},{16,8},{9,17},{17,9},{10,18},{18,10},{11,19},{19,11},{12,20... | collective-permute-start | bytes 1277960 | tf_op jit(solution)/shard_map/ppermute | solution.py:322
  41.8 18.1 %copy-start.3 = (f32[1,2048,256]{2,1,0:T(8,128)}, f32[1,2048,256]{2,1,0:T(8,128)S(1)}, u32[]{:S(2)}) copy-start(f32[1,2048,256]{2,1,0:T(8,128)S(1)} %get-tuple-element.108.refs_4_.refs_7_.refs_5_.refs_8_) | copy-start | bytes 6291460
  42.5 17.4 %collective-permute-start.6 = (bf16[208,1024]{1,0:T(8,128)(2,1)S(1)}, bf16[208,1024]{1,0:T(8,128)(2,1)S(1)}, u32[]{:S(2)}, u32[]{:S(2)}) collective-permute-start(bf16[208,1024]{1,0:T(8,128)(2,1)S(1)} %get-tuple-element.114), channel_id=1, source_target_pairs={{0,8},{24,16},{1,9},{25,17},{2,10},{26,18},{3,11},{27,19},{4,12},{... | collective-permute-start | bytes 1277960 | tf_op jit(solution)/shard_map/ppermute | solution.py:322
  46.8 13.2 %collective-permute-start.7 = (bf16[208,1024]{1,0:T(8,128)(2,1)S(1)}, bf16[208,1024]{1,0:T(8,128)(2,1)S(1)}, u32[]{:S(2)}, u32[]{:S(2)}) collective-permute-start(bf16[208,1024]{1,0:T(8,128)(2,1)S(1)} %get-tuple-element.115), channel_id=1, source_target_pairs={{8,16},{16,8},{9,17},{17,9},{10,18},{18,10},{11,19},{19,11},{12,20... | collective-permute-start | bytes 1277960 | tf_op jit(solution)/shard_map/ppermute | solution.py:322
  49.5 16.2 %collective-permute-start.4 = (bf16[208,1024]{1,0:T(8,128)(2,1)}, bf16[208,1024]{1,0:T(8,128)(2,1)S(1)}, u32[]{:S(2)}, u32[]{:S(2)}) collective-permute-start(bf16[208,1024]{1,0:T(8,128)(2,1)} %get-tuple-element.112), channel_id=1, source_target_pairs={{0,8},{8,0},{16,24},{24,16},{1,9},{9,1},{17,25},{25,17},{2,10},{10... | collective-permute-start | bytes 1277960 | tf_op jit(solution)/shard_map/ppermute | solution.py:322
  50.9 14.9 %collective-permute-start.5 = (bf16[208,1024]{1,0:T(8,128)(2,1)}, bf16[208,1024]{1,0:T(8,128)(2,1)}, u32[]{:S(2)}, u32[]{:S(2)}) collective-permute-start(bf16[208,1024]{1,0:T(8,128)(2,1)} %get-tuple-element.113), channel_id=1, source_target_pairs={{8,16},{16,8},{9,17},{17,9},{10,18},{18,10},{11,19},{19,11},{12,20... | collective-permute-start | bytes 1277960 | tf_op jit(solution)/shard_map/ppermute | solution.py:322
  62.0 13.0 %collective-permute-start.10 = (bf16[208,1024]{1,0:T(8,128)(2,1)}, bf16[208,1024]{1,0:T(8,128)(2,1)S(1)}, u32[]{:S(2)}, u32[]{:S(2)}) collective-permute-start(bf16[208,1024]{1,0:T(8,128)(2,1)} %get-tuple-element.128), channel_id=1, source_target_pairs={{0,8},{8,0},{16,24},{24,16},{1,9},{9,1},{17,25},{25,17},{2,10},{10... | collective-permute-start | bytes 1277960 | tf_op jit(solution)/shard_map/ppermute | solution.py:322
  64.4 10.7 %collective-permute-start.11 = (bf16[208,1024]{1,0:T(8,128)(2,1)}, bf16[208,1024]{1,0:T(8,128)(2,1)}, u32[]{:S(2)}, u32[]{:S(2)}) collective-permute-start(bf16[208,1024]{1,0:T(8,128)(2,1)} %get-tuple-element.129), channel_id=1, source_target_pairs={{8,16},{16,8},{9,17},{17,9},{10,18},{18,10},{11,19},{19,11},{12,20... | collective-permute-start | bytes 1277960 | tf_op jit(solution)/shard_map/ppermute | solution.py:322
  69.6 5.5 %copy-start.7 = (bf16[208,1024]{1,0:T(8,128)(2,1)S(1)}, bf16[208,1024]{1,0:T(8,128)(2,1)}, u32[]{:S(2)}) copy-start(bf16[208,1024]{1,0:T(8,128)(2,1)} %copy-done.6) | copy-start | bytes 1277956
  72.3 12.3 %collective-permute-start.8 = (bf16[208,1024]{1,0:T(8,128)(2,1)S(1)}, bf16[208,1024]{1,0:T(8,128)(2,1)S(1)}, u32[]{:S(2)}, u32[]{:S(2)}) collective-permute-start(bf16[208,1024]{1,0:T(8,128)(2,1)S(1)} %get-tuple-element.126), channel_id=1, source_target_pairs={{0,8},{8,0},{16,24},{24,16},{1,9},{9,1},{17,25},{25,17},{2,10},{10... | collective-permute-start | bytes 1277960 | tf_op jit(solution)/shard_map/ppermute | solution.py:322
  74.3 10.3 %collective-permute-start.9 = (bf16[208,1024]{1,0:T(8,128)(2,1)S(1)}, bf16[208,1024]{1,0:T(8,128)(2,1)S(1)}, u32[]{:S(2)}, u32[]{:S(2)}) collective-permute-start(bf16[208,1024]{1,0:T(8,128)(2,1)S(1)} %get-tuple-element.127), channel_id=1, source_target_pairs={{8,16},{16,8},{9,17},{17,9},{10,18},{18,10},{11,19},{19,11},{12,20... | collective-permute-start | bytes 1277960 | tf_op jit(solution)/shard_map/ppermute | solution.py:322
  78.3 21.7 %collective-permute-start.14 = (bf16[208,1024]{1,0:T(8,128)(2,1)}, bf16[208,1024]{1,0:T(8,128)(2,1)S(1)}, u32[]{:S(2)}, u32[]{:S(2)}) collective-permute-start(bf16[208,1024]{1,0:T(8,128)(2,1)} %get-tuple-element.142), channel_id=1, source_target_pairs={{0,8},{8,0},{16,24},{24,16},{1,9},{9,1},{17,25},{25,17},{2,10},{10... | collective-permute-start | bytes 1277960 | tf_op jit(solution)/shard_map/ppermute | solution.py:322
  80.8 19.2 %collective-permute-start.15 = (bf16[208,1024]{1,0:T(8,128)(2,1)}, bf16[208,1024]{1,0:T(8,128)(2,1)}, u32[]{:S(2)}, u32[]{:S(2)}) collective-permute-start(bf16[208,1024]{1,0:T(8,128)(2,1)} %get-tuple-element.143), channel_id=1, source_target_pairs={{8,16},{16,8},{9,17},{17,9},{10,18},{18,10},{11,19},{19,11},{12,20... | collective-permute-start | bytes 1277960 | tf_op jit(solution)/shard_map/ppermute | solution.py:322
  86.6 18.3 %collective-permute-start.12 = (bf16[208,1024]{1,0:T(8,128)(2,1)}, bf16[208,1024]{1,0:T(8,128)(2,1)S(1)}, u32[]{:S(2)}, u32[]{:S(2)}) collective-permute-start(bf16[208,1024]{1,0:T(8,128)(2,1)} %get-tuple-element.140), channel_id=1, source_target_pairs={{0,8},{8,0},{16,24},{24,16},{1,9},{9,1},{17,25},{25,17},{2,10},{10... | collective-permute-start | bytes 1277960 | tf_op jit(solution)/shard_map/ppermute | solution.py:322
  90.2 14.8 %collective-permute-start.13 = (bf16[208,1024]{1,0:T(8,128)(2,1)}, bf16[208,1024]{1,0:T(8,128)(2,1)}, u32[]{:S(2)}, u32[]{:S(2)}) collective-permute-start(bf16[208,1024]{1,0:T(8,128)(2,1)} %get-tuple-element.141), channel_id=1, source_target_pairs={{8,16},{16,8},{9,17},{17,9},{10,18},{18,10},{11,19},{19,11},{12,20... | collective-permute-start | bytes 1277960 | tf_op jit(solution)/shard_map/ppermute | solution.py:322
  91.6 8.4 %copy-start.2 = (bf16[1,2048,1024]{2,1,0:T(8,128)(2,1)S(1)}, bf16[1,2048,1024]{2,1,0:T(8,128)(2,1)}, u32[]{:S(2)}) copy-start(bf16[1,2048,1024]{2,1,0:T(8,128)(2,1)} %copy-done) | copy-start | bytes 12582916
  91.6 8.4 %copy-start.5 = (f32[1,2048,256]{2,1,0:T(8,128)S(1)}, f32[1,2048,256]{2,1,0:T(8,128)}, u32[]{:S(2)}) copy-start(f32[1,2048,256]{2,1,0:T(8,128)} %copy-done.3) | copy-start | bytes 6291460
  100.0 5.0 %copy-start.9 = (bf16[208,1024]{1,0:T(8,128)(2,1)S(1)}, bf16[208,1024]{1,0:T(8,128)(2,1)}, u32[]{:S(2)}) copy-start(bf16[208,1024]{1,0:T(8,128)(2,1)} %copy-done.8) | copy-start | bytes 1277956
  102.8 12.3 %collective-permute-start.18 = (bf16[208,1024]{1,0:T(8,128)(2,1)S(1)}, bf16[208,1024]{1,0:T(8,128)(2,1)S(1)}, u32[]{:S(2)}, u32[]{:S(2)}) collective-permute-start(bf16[208,1024]{1,0:T(8,128)(2,1)S(1)} %get-tuple-element.154), channel_id=1, source_target_pairs={{0,8},{8,0},{16,24},{24,16},{1,9},{9,1},{17,25},{25,17},{2,10},{10... | collective-permute-start | bytes 1277960 | tf_op jit(solution)/shard_map/ppermute | solution.py:322
  104.3 10.9 %collective-permute-start.19 = (bf16[208,1024]{1,0:T(8,128)(2,1)S(1)}, bf16[208,1024]{1,0:T(8,128)(2,1)S(1)}, u32[]{:S(2)}, u32[]{:S(2)}) collective-permute-start(bf16[208,1024]{1,0:T(8,128)(2,1)S(1)} %get-tuple-element.155), channel_id=1, source_target_pairs={{8,16},{16,8},{9,17},{17,9},{10,18},{18,10},{11,19},{19,11},{12,20... | collective-permute-start | bytes 1277960 | tf_op jit(solution)/shard_map/ppermute | solution.py:322
  107.7 14.3 %collective-permute-start.16 = (bf16[208,1024]{1,0:T(8,128)(2,1)S(1)}, bf16[208,1024]{1,0:T(8,128)(2,1)S(1)}, u32[]{:S(2)}, u32[]{:S(2)}) collective-permute-start(bf16[208,1024]{1,0:T(8,128)(2,1)S(1)} %get-tuple-element.152), channel_id=1, source_target_pairs={{8,0},{16,24},{9,1},{17,25},{10,2},{18,26},{11,3},{19,27},{12,4},{... | collective-permute-start | bytes 1277960 | tf_op jit(solution)/shard_map/ppermute | solution.py:322
  109.0 13.0 %collective-permute-start.17 = (bf16[208,1024]{1,0:T(8,128)(2,1)S(1)}, bf16[208,1024]{1,0:T(8,128)(2,1)S(1)}, u32[]{:S(2)}, u32[]{:S(2)}) collective-permute-start(bf16[208,1024]{1,0:T(8,128)(2,1)S(1)} %get-tuple-element.153), channel_id=1, source_target_pairs={{8,16},{16,8},{9,17},{17,9},{10,18},{18,10},{11,19},{19,11},{12,20... | collective-permute-start | bytes 1277960 | tf_op jit(solution)/shard_map/ppermute | solution.py:322
  116.9 18.2 %collective-permute-start.20 = (bf16[208,1024]{1,0:T(8,128)(2,1)S(1)}, bf16[208,1024]{1,0:T(8,128)(2,1)S(1)}, u32[]{:S(2)}, u32[]{:S(2)}) collective-permute-start(bf16[208,1024]{1,0:T(8,128)(2,1)S(1)} %get-tuple-element.170), channel_id=1, source_target_pairs={{8,0},{16,24},{9,1},{17,25},{10,2},{18,26},{11,3},{19,27},{12,4},{... | collective-permute-start | bytes 1277960 | tf_op jit(solution)/shard_map/ppermute | solution.py:322
  118.2 17.0 %collective-permute-start.21 = (bf16[208,1024]{1,0:T(8,128)(2,1)S(1)}, bf16[208,1024]{1,0:T(8,128)(2,1)S(1)}, u32[]{:S(2)}, u32[]{:S(2)}) collective-permute-start(bf16[208,1024]{1,0:T(8,128)(2,1)S(1)} %get-tuple-element.171), channel_id=1, source_target_pairs={{8,16},{16,8},{9,17},{17,9},{10,18},{18,10},{11,19},{19,11},{12,20... | collective-permute-start | bytes 1277960 | tf_op jit(solution)/shard_map/ppermute | solution.py:322
  123.8 16.0 %collective-permute-start.23 = (bf16[208,1024]{1,0:T(8,128)(2,1)S(1)}, bf16[208,1024]{1,0:T(8,128)(2,1)S(1)}, u32[]{:S(2)}, u32[]{:S(2)}) collective-permute-start(bf16[208,1024]{1,0:T(8,128)(2,1)S(1)} %get-tuple-element.177), channel_id=1, source_target_pairs={{8,0},{16,24},{9,1},{17,25},{10,2},{18,26},{11,3},{19,27},{12,4},{... | collective-permute-start | bytes 1277960 | tf_op jit(solution)/shard_map/ppermute | solution.py:322
  136.9 11.4 %collective-permute-start.22 = (bf16[208,1024]{1,0:T(8,128)(2,1)S(1)}, bf16[208,1024]{1,0:T(8,128)(2,1)S(1)}, u32[]{:S(2)}, u32[]{:S(2)}) collective-permute-start(bf16[208,1024]{1,0:T(8,128)(2,1)S(1)} %get-tuple-element.176), channel_id=1, source_target_pairs={{8,0},{16,24},{9,1},{17,25},{10,2},{18,26},{11,3},{19,27},{12,4},{... | collective-permute-start | bytes 1277960 | tf_op jit(solution)/shard_map/ppermute | solution.py:322
  (4 other events, 7.8 us)
Sparse Core Ops, SparseCore 0:
  9.9 57.0 all-gather.2
  70.5 71.2 reduce-scatter.1

commit v4 on v3

--- a/solution.py
+++ b/solution.py
@@ -11,7 +11,7 @@
 PIECES = 10
 STEPS = 1
 DELAY = 2
-PROJECT_BLOCKS = 4
+PROJECT_BLOCKS = 2
 GRADS = ((0, 2, (0,), -1), (2, 3, (1, 2), 0), (5, 3, (), 2))
 IDLE_BEFORE = 5
 PROJECT_ROUNDS = (6, 10)
@@ -25,7 +25,7 @@
 CHOSEN, REPLICA, FSDP = 0, 1, 2
 VMEM = 14 << 20
 VMEM_R = 10 << 20
-VMEM_P = 16 << 20
+VMEM_P = 24 << 20
 LONG = 116 * 10**9
 
 

time: 162 us -> 162 us (level)
  no operation moved by 1% of the time
where the time goes in v4:
time: 162 us; the launch traced here: 161 us
  Pallas kernels  86.1 us (53%)
  starting transfers between devices  42.2 us (26%)
  between operations  15 us (9%)
  waiting for transfers between devices  13.6 us (8%)
  local copies, waits for them, and re-layouts  3.8 us (2%)
    pallas_call x23, Pallas kernels, call(): pl.pallas_call(kernel, out_shape=out_shape, grid_spec=pltpu.PrefetchScala...  86.1 us
    ppermute x24, starting transfers between devices, send(): lax.ppermute(x, 'replica', self.pairs(t, path))  42.1 us
    ppermute x24, waiting for transfers between devices, send(): lax.ppermute(x, 'replica', self.pairs(t, path))  12.9 us
    unnamed x20, local copies, waits for them, and re-layouts  3.8 us
  transfers between devices with their start and end apart: 26, of which 5 were waited for; matrix products, arithmetic and copies ran while one was open for 0% of the time, Pallas kernels for 52%

profile of v4, /device:TPU:0, one launch (start us, length us, event | category | flops | bytes accessed | tf_op | source)
XLA Modules:
  0.0 160.8 jit_solution(12313758435227136705)
XLA Ops:
  8.7 1.8 %first_sends.2 = (bf16[208,1024]{1,0:T(8,128)(2,1)S(1)}, f32[8,128]{1,0:T(8,128)S(1)}) custom-call(s32[3]{0:T(128)S(1)} %pad_add_fusion.s, bf16[2,2048,1024]{2,1,0:T(8,128)(2,1)} %bitcast.19, f32[2,2048,256]{2,1,0:T(8,128)} %bitcast.24, f32[2,2048,256]{2,1,0:T(8,128)} %bitcast.30), custom_call_target="tpu_custom_call" | custom-call | tf_op jit(solution)/shard_map/first_sends/pallas_call | solution.py:70
  10.5 4.9 %collective-permute-start = (bf16[208,1024]{1,0:T(8,128)(2,1)S(1)}, bf16[208,1024]{1,0:T(8,128)(2,1)S(1)}, u32[]{:S(2)}, u32[]{:S(2)}) collective-permute-start(bf16[208,1024]{1,0:T(8,128)(2,1)S(1)} %get-tuple-element.98), channel_id=1, source_target_pairs={{0,8},{24,16},{1,9},{25,17},{2,10},{26,18},{3,11},{27,19},{4,12},{... | collective-permute-start | bytes 1277960 | tf_op jit(solution)/shard_map/ppermute | solution.py:322
  15.4 1.8 %first_sends.3 = (bf16[208,1024]{1,0:T(8,128)(2,1)S(1)}, f32[8,128]{1,0:T(8,128)S(1)}) custom-call(s32[3]{0:T(128)S(1)} %pad_add_fusion.s, bf16[2,2048,1024]{2,1,0:T(8,128)(2,1)} %bitcast.20, f32[2,2048,256]{2,1,0:T(8,128)} %bitcast.25, f32[2,2048,256]{2,1,0:T(8,128)} %bitcast.31, f32[8,128]{1,0:T(8,128)S(1)} %get-tuple-element.99.refs_3_), custom_call_target="tpu_custom_call" | custom-call | tf_op jit(solution)/shard_map/first_sends/pallas_call | solution.py:70
  18.5 7.4 %grad_0.1 = (bf16[8,512,1024]{2,1,0:T(8,128)(2,1)}, bf16[1,2048,1024]{2,1,0:T(8,128)(2,1)S(1)}, f32[8,128]{1,0:T(8,128)S(1)}) custom-call(s32[3]{0:T(128)S(1)} %pad_add_fusion.s, bf16[1024,4096]{1,0:T(8,128)(2,1)} %refs_0_.9, bf16[1024,1024]{1,0:T(8,128)(2,1)} %refs_1_.5, bf16[2,2048,1024]{2,1,0:T(8,128)(2,1)} %bitcast.21, ...), custom_call_target="tpu_custom_call" | custom-call | tf_op jit(solution)/shard_map/grad_0/pallas_call | solution.py:70
  25.9 3.0 %round_0.1 = (bf16[208,1024]{1,0:T(8,128)(2,1)S(1)}, bf16[208,1024]{1,0:T(8,128)(2,1)S(1)}, f32[8,128]{1,0:T(8,128)S(1)}) custom-call(s32[3]{0:T(128)S(1)} %pad_add_fusion.s, bf16[208,1024]{1,0:T(8,128)(2,1)S(1)} %collective-permute-done.refs_0_.refs_1_.refs_2_, bf16[208,1024]{1,0:T(8,128)(2,1)S(1)} %collective-permute-done.refs_0_.refs_1_.refs_2_, ...), custom_call_target="tpu_custom_call" | custom-call | tf_op jit(solution)/shard_map/round_0/pallas_call | solution.py:70
  28.9 3.3 %collective-permute-start.1 = (bf16[208,1024]{1,0:T(8,128)(2,1)S(1)}, bf16[208,1024]{1,0:T(8,128)(2,1)S(1)}, u32[]{:S(2)}, u32[]{:S(2)}) collective-permute-start(bf16[208,1024]{1,0:T(8,128)(2,1)S(1)} %get-tuple-element.102), channel_id=1, source_target_pairs={{0,8},{24,16},{1,9},{25,17},{2,10},{26,18},{3,11},{27,19},{4,12},{... | collective-permute-start | bytes 1277960 | tf_op jit(solution)/shard_map/ppermute | solution.py:322
  33.0 8.9 %grad_2.1 = (bf16[8,512,1024]{2,1,0:T(8,128)(2,1)}, f32[1,2048,256]{2,1,0:T(8,128)S(1)}, f32[1,2048,256]{2,1,0:T(8,128)S(1)}, f32[8,128]{1,0:T(8,128)S(1)}) custom-call(s32[3]{0:T(128)S(1)} %pad_add_fusion.s, bf16[1024,4096]{1,0:T(8,128)(2,1)} %refs_0_.9, bf16[1024,1024]{1,0:T(8,128)(2,1)} %refs_1_.5, ...), custom_call_target="tpu_custom_call", output_to_operand_aliasing={{0}: (3, {})} | custom-call | tf_op jit(solution)/shard_map/grad_2/pallas_call | solution.py:70
  42.5 4.3 %collective-permute-start.6 = (bf16[208,1024]{1,0:T(8,128)(2,1)S(1)}, bf16[208,1024]{1,0:T(8,128)(2,1)S(1)}, u32[]{:S(2)}, u32[]{:S(2)}) collective-permute-start(bf16[208,1024]{1,0:T(8,128)(2,1)S(1)} %get-tuple-element.114), channel_id=1, source_target_pairs={{0,8},{24,16},{1,9},{25,17},{2,10},{26,18},{3,11},{27,19},{4,12},{... | collective-permute-start | bytes 1277960 | tf_op jit(solution)/shard_map/ppermute | solution.py:322
  47.5 2.0 %round_2.1 = (bf16[208,1024]{1,0:T(8,128)(2,1)}, bf16[208,1024]{1,0:T(8,128)(2,1)}, bf16[2048,1024]{1,0:T(8,128)(2,1)}, f32[2,2048,256]{2,1,0:T(8,128)}, f32[2,2048,256]{2,1,0:T(8,128)}, /*index=5*/f32[8,128]{1,0:T(8,128)S(1)}) custom-call(s32[3]{0:T(128)S(1)} %pad_add_fusion.s, ...), custom_call_target="tpu_custom_call" | custom-call | tf_op jit(solution)/shard_map/round_2/pallas_call | solution.py:70
  52.3 7.6 %grad_5.1 = (bf16[8,512,1024]{2,1,0:T(8,128)(2,1)}, f32[8,128]{1,0:T(8,128)S(1)}) custom-call(s32[3]{0:T(128)S(1)} %pad_add_fusion.s, bf16[1024,4096]{1,0:T(8,128)(2,1)} %refs_0_.9, bf16[1024,1024]{1,0:T(8,128)(2,1)} %refs_1_.5, bf16[8,512,1024]{2,1,0:T(8,128)(2,1)} %get-tuple-element.119.refs_2_, ...), custom_call_target="tpu_custom_call", output_to_operand_aliasing={{0}: (3, {})} | custom-call | tf_op jit(solution)/shard_map/grad_5/pallas_call | solution.py:70
  60.0 2.0 %round_3.1 = (bf16[208,1024]{1,0:T(8,128)(2,1)}, bf16[208,1024]{1,0:T(8,128)(2,1)}, bf16[2048,1024]{1,0:T(8,128)(2,1)}, f32[2,2048,256]{2,1,0:T(8,128)}, f32[2,2048,256]{2,1,0:T(8,128)}, /*index=5*/f32[8,128]{1,0:T(8,128)S(1)}) custom-call(s32[3]{0:T(128)S(1)} %pad_add_fusion.s, ...), custom_call_target="tpu_custom_call", output_to_operand_aliasing={{2}: (10, {}), {3}: (11, {}), {4}: (12, {})} | custom-call | tf_op jit(solution)/shard_map/round_3/pallas_call | solution.py:70
  62.0 2.4 %collective-permute-start.10 = (bf16[208,1024]{1,0:T(8,128)(2,1)}, bf16[208,1024]{1,0:T(8,128)(2,1)S(1)}, u32[]{:S(2)}, u32[]{:S(2)}) collective-permute-start(bf16[208,1024]{1,0:T(8,128)(2,1)} %get-tuple-element.128), channel_id=1, source_target_pairs={{0,8},{8,0},{16,24},{24,16},{1,9},{9,1},{17,25},{25,17},{2,10},{10... | collective-permute-start | bytes 1277960 | tf_op jit(solution)/shard_map/ppermute | solution.py:322
  65.8 2.2 %copy-done.1 = bf16[1,2048,1024]{2,1,0:T(8,128)(2,1)S(1)} copy-done((bf16[1,2048,1024]{2,1,0:T(8,128)(2,1)S(1)}, bf16[1,2048,1024]{2,1,0:T(8,128)(2,1)}, u32[]{:S(2)}) %copy-start.1) | copy-done | bytes 4194328
  69.6 2.7 %round_4.1 = (bf16[208,1024]{1,0:T(8,128)(2,1)S(1)}, bf16[208,1024]{1,0:T(8,128)(2,1)S(1)}, bf16[2048,1024]{1,0:T(8,128)(2,1)}, f32[2,2048,256]{2,1,0:T(8,128)},...) custom-call(s32[3]{0:T(128)S(1)} %pad_add_fusion.s, ...), custom_call_target="tpu_custom_call", output_to_operand_aliasing={{2}: (10, {}), {3}: (11, {}), {4}: (12, {})} | custom-call | tf_op jit(solution)/shard_map/round_4/pallas_call | solution.py:70
  72.3 2.0 %collective-permute-start.8 = (bf16[208,1024]{1,0:T(8,128)(2,1)S(1)}, bf16[208,1024]{1,0:T(8,128)(2,1)S(1)}, u32[]{:S(2)}, u32[]{:S(2)}) collective-permute-start(bf16[208,1024]{1,0:T(8,128)(2,1)S(1)} %get-tuple-element.126), channel_id=1, source_target_pairs={{0,8},{8,0},{16,24},{24,16},{1,9},{9,1},{17,25},{25,17},{2,10},{10... | collective-permute-start | bytes 1277960 | tf_op jit(solution)/shard_map/ppermute | solution.py:322
  75.0 3.2 %round_5.1 = (bf16[208,1024]{1,0:T(8,128)(2,1)}, bf16[208,1024]{1,0:T(8,128)(2,1)}, bf16[2048,1024]{1,0:T(8,128)(2,1)}, f32[2,2048,256]{2,1,0:T(8,128)}, f32[2,2048,256]{2,1,0:T(8,128)}, /*index=5*/f32[8,128]{1,0:T(8,128)S(1)}) custom-call(s32[3]{0:T(128)S(1)} %pad_add_fusion.s, ...), custom_call_target="tpu_custom_call", output_to_operand_aliasing={{2}: (10, {}), {3}: (11, {}), {4}: (12, {})} | custom-call | tf_op jit(solution)/shard_map/round_5/pallas_call | solution.py:70
  78.3 2.5 %collective-permute-start.14 = (bf16[208,1024]{1,0:T(8,128)(2,1)}, bf16[208,1024]{1,0:T(8,128)(2,1)S(1)}, u32[]{:S(2)}, u32[]{:S(2)}) collective-permute-start(bf16[208,1024]{1,0:T(8,128)(2,1)} %get-tuple-element.142), channel_id=1, source_target_pairs={{0,8},{8,0},{16,24},{24,16},{1,9},{9,1},{17,25},{25,17},{2,10},{10... | collective-permute-start | bytes 1277960 | tf_op jit(solution)/shard_map/ppermute | solution.py:322
  82.2 2.4 %collective-permute-done.8.refs_0_.refs_2_ = bf16[208,1024]{1,0:T(8,128)(2,1)S(1)} collective-permute-done((bf16[208,1024]{1,0:T(8,128)(2,1)S(1)}, bf16[208,1024]{1,0:T(8,128)(2,1)S(1)}, u32[]{:S(2)}, u32[]{:S(2)}) %collective-permute-start.8) | collective-permute-done | bytes 426016 | tf_op jit(solution)/shard_map/ppermute | solution.py:322
  84.6 2.0 %round_6.1 = (bf16[208,1024]{1,0:T(8,128)(2,1)}, bf16[208,1024]{1,0:T(8,128)(2,1)}, bf16[2048,1024]{1,0:T(8,128)(2,1)}, f32[2,2048,256]{2,1,0:T(8,128)}, f32[2,2048,256]{2,1,0:T(8,128)}, /*index=5*/f32[8,128]{1,0:T(8,128)S(1)}) custom-call(s32[3]{0:T(128)S(1)} %pad_add_fusion.s, ...), custom_call_target="tpu_custom_call", output_to_operand_aliasing={{2}: (10, {}), {3}: (11, {}), {4}: (12, {})} | custom-call | tf_op jit(solution)/shard_map/round_6/pallas_call | solution.py:70
  86.6 3.6 %collective-permute-start.12 = (bf16[208,1024]{1,0:T(8,128)(2,1)}, bf16[208,1024]{1,0:T(8,128)(2,1)S(1)}, u32[]{:S(2)}, u32[]{:S(2)}) collective-permute-start(bf16[208,1024]{1,0:T(8,128)(2,1)} %get-tuple-element.140), channel_id=1, source_target_pairs={{0,8},{8,0},{16,24},{24,16},{1,9},{9,1},{17,25},{25,17},{2,10},{10... | collective-permute-start | bytes 1277960 | tf_op jit(solution)/shard_map/ppermute | solution.py:322
  91.6 8.3 %project_0.1 = (f32[1024,1024]{1,0:T(8,128)S(1)}, f32[8,128]{1,0:T(8,128)S(1)}) custom-call(s32[3]{0:T(128)S(1)} %pad_add_fusion.s, bf16[1024,4096]{1,0:T(8,128)(2,1)} %refs_0_.9, bf16[4096,1024]{1,0:T(8,128)(2,1)} %bitcast.37, f32[8,128]{1,0:T(8,128)S(1)} %get-tuple-element.138.refs_2_), custom_call_target="tpu_custom_call" | custom-call | tf_op jit(solution)/shard_map/project_0/pallas_call | solution.py:70
  100.0 2.8 %round_7.1 = (bf16[208,1024]{1,0:T(8,128)(2,1)S(1)}, bf16[208,1024]{1,0:T(8,128)(2,1)S(1)}, bf16[2048,1024]{1,0:T(8,128)(2,1)}, f32[2,2048,256]{2,1,0:T(8,128)},...) custom-call(s32[3]{0:T(128)S(1)} %pad_add_fusion.s, ...), custom_call_target="tpu_custom_call", output_to_operand_aliasing={{2}: (10, {}), {3}: (11, {}), {4}: (12, {})} | custom-call | tf_op jit(solution)/shard_map/round_7/pallas_call | solution.py:70
  104.9 2.8 %round_8.1 = (bf16[208,1024]{1,0:T(8,128)(2,1)S(1)}, bf16[208,1024]{1,0:T(8,128)(2,1)S(1)}, bf16[2048,1024]{1,0:T(8,128)(2,1)}, f32[2,2048,256]{2,1,0:T(8,128)},...) custom-call(s32[3]{0:T(128)S(1)} %pad_add_fusion.s, ...), custom_call_target="tpu_custom_call", output_to_operand_aliasing={{2}: (10, {}), {3}: (11, {}), {4}: (12, {})} | custom-call | tf_op jit(solution)/shard_map/round_8/pallas_call | solution.py:70
  109.6 5.4 %idle.1 = (f32[2,2048,256]{2,1,0:T(8,128)}, f32[2,2048,256]{2,1,0:T(8,128)}, f32[8,128]{1,0:T(8,128)S(1)}) custom-call(s32[3]{0:T(128)S(1)} %pad_add_fusion.s, f32[2,2048,256]{2,1,0:T(8,128)} %bitcast.29, f32[2,2048,256]{2,1,0:T(8,128)} %bitcast.35, f32[2,2048,256]{2,1,0:T(8,128)} %get-tuple-element.157.refs_2_, ...), custom_call_target="tpu_custom_call", output_to_operand_aliasing={{0}: (3, {}), {1}: (4, {})} | custom-call | tf_op jit(solution)/shard_map/idle/pallas_call | solution.py:70
  118.9 3.2 %collective-permute-done.16.refs_0_.refs_2_ = bf16[208,1024]{1,0:T(8,128)(2,1)S(1)} collective-permute-done((bf16[208,1024]{1,0:T(8,128)(2,1)S(1)}, bf16[208,1024]{1,0:T(8,128)(2,1)S(1)}, u32[]{:S(2)}, u32[]{:S(2)}) %collective-permute-start.16) | collective-permute-done | bytes 426016 | tf_op jit(solution)/shard_map/ppermute | solution.py:322
  125.3 9.8 %project_1.1 = (bf16[1024,1024]{1,0:T(8,128)(2,1)}, f32[8,128]{1,0:T(8,128)S(1)}) custom-call(s32[3]{0:T(128)S(1)} %pad_add_fusion.s, bf16[1024,4096]{1,0:T(8,128)(2,1)} %refs_0_.9, bf16[4096,1024]{1,0:T(8,128)(2,1)} %bitcast.38, f32[1024,1024]{1,0:T(8,128)S(1)} %get-tuple-element.139.refs_2_, f32[8,128]{1,0:T(8,128)S(1)} %get-tuple-element.167.refs_3_), custom_call_target="tpu_custom_call" | custom-call | tf_op jit(solution)/shard_map/project_1/pallas_call | solution.py:70
  135.1 1.8 %round_11.1 = (bf16[208,1024]{1,0:T(8,128)(2,1)S(1)}, bf16[2048,1024]{1,0:T(8,128)(2,1)}, f32[2,2048,256]{2,1,0:T(8,128)}, f32[2,2048,256]{2,1,0:T(8,128)}, f32[8,128]{1,0:T(8,128)S(1)}) custom-call(s32[3]{0:T(128)S(1)} %pad_add_fusion.s, ...), custom_call_target="tpu_custom_call", output_to_operand_aliasing={{1}: (10, {}), {2}: (11, {}), {3}: (12, {})} | custom-call | tf_op jit(solution)/shard_map/round_11/pallas_call | solution.py:70
  138.1 2.0 %collective-permute-done.23.refs_0_.refs_1_ = bf16[208,1024]{1,0:T(8,128)(2,1)S(1)} collective-permute-done((bf16[208,1024]{1,0:T(8,128)(2,1)S(1)}, bf16[208,1024]{1,0:T(8,128)(2,1)S(1)}, u32[]{:S(2)}, u32[]{:S(2)}) %collective-permute-start.23) | collective-permute-done | bytes 426016 | tf_op jit(solution)/shard_map/ppermute | solution.py:322
  140.1 2.9 %round_12.1 = (bf16[2048,1024]{1,0:T(8,128)(2,1)}, f32[2,2048,256]{2,1,0:T(8,128)}, f32[2,2048,256]{2,1,0:T(8,128)}, f32[8,128]{1,0:T(8,128)S(1)}) custom-call(s32[3]{0:T(128)S(1)} %pad_add_fusion.s, bf16[208,1024]{1,0:T(8,128)(2,1)S(1)} %collective-permute-done.23.refs_0_.refs_1_, ...), custom_call_target="tpu_custom_call", output_to_operand_aliasing={{0}: (10, {}), {1}: (11, {}), {2}: (12, {})} | custom-call | tf_op jit(solution)/shard_map/round_12/pallas_call | solution.py:70
  143.0 5.1 %collective-permute-done.22.refs_0_.refs_1_ = bf16[208,1024]{1,0:T(8,128)(2,1)S(1)} collective-permute-done((bf16[208,1024]{1,0:T(8,128)(2,1)S(1)}, bf16[208,1024]{1,0:T(8,128)(2,1)S(1)}, u32[]{:S(2)}, u32[]{:S(2)}) %collective-permute-start.22) | collective-permute-done | bytes 426016 | tf_op jit(solution)/shard_map/ppermute | solution.py:322
  148.1 2.8 %round_13.1 = (bf16[2048,1024]{1,0:T(8,128)(2,1)}, f32[2,2048,256]{2,1,0:T(8,128)}, f32[2,2048,256]{2,1,0:T(8,128)}, f32[8,128]{1,0:T(8,128)S(1)}) custom-call(s32[3]{0:T(128)S(1)} %pad_add_fusion.s, bf16[208,1024]{1,0:T(8,128)(2,1)S(1)} %collective-permute-done.22.refs_0_.refs_1_, ...), custom_call_target="tpu_custom_call", output_to_operand_aliasing={{0}: (10, {}), {1}: (11, {}), {2}: (12, {})} | custom-call | flops 115999997952 | tf_op jit(solution)/shard_map/round_13/pallas_call | solution.py:70
  151.0 3.0 %widen.1 = (f32[512,1024]{1,0:T(8,128)}, f32[8,128]{1,0:T(8,128)}) custom-call(s32[3]{0:T(128)S(1)} %pad_add_fusion.s, bf16[512,1024]{1,0:T(8,128)(2,1)} %reduce-scatter.2.cloned.1.call-done.refs_0_, f32[8,128]{1,0:T(8,128)S(1)} %get-tuple-element.186.refs_1_), custom_call_target="tpu_custom_call" | custom-call | tf_op jit(solution)/shard_map/widen/pallas_call | solution.py:70
  (66 shorter events, 26.0 us)
Async XLA Ops:
  7.2 84.4 %all-gather.3.cloned.1.call-start = ((), (), s32[]{:S(2)}) async-start(), calls=%async_computation.2 | async-start | bytes 9437184 | tf_op jit(solution)/shard_map/all_gather | solution.py:96
  7.9 143.1 %reduce-scatter.2.cloned.1.call-start = ((), (), s32[]{:S(2)}) async-start(), calls=%async_computation.1 | async-start | bytes 9437184 | tf_op jit(solution)/shard_map/reduce_scatter | solution.py:148
  10.5 15.4 %collective-permute-start = (bf16[208,1024]{1,0:T(8,128)(2,1)S(1)}, bf16[208,1024]{1,0:T(8,128)(2,1)S(1)}, u32[]{:S(2)}, u32[]{:S(2)}) collective-permute-start(bf16[208,1024]{1,0:T(8,128)(2,1)S(1)} %get-tuple-element.98), channel_id=1, source_target_pairs={{0,8},{24,16},{1,9},{25,17},{2,10},{26,18},{3,11},{27,19},{4,12},{... | collective-permute-start | bytes 1277960 | tf_op jit(solution)/shard_map/ppermute | solution.py:322
  17.2 24.7 %collective-permute-start.3 = (bf16[208,1024]{1,0:T(8,128)(2,1)S(1)}, bf16[208,1024]{1,0:T(8,128)(2,1)S(1)}, u32[]{:S(2)}, u32[]{:S(2)}) collective-permute-start(bf16[208,1024]{1,0:T(8,128)(2,1)S(1)} %get-tuple-element.109), channel_id=1, source_target_pairs={{0,8},{24,16},{1,9},{25,17},{2,10},{26,18},{3,11},{27,19},{4,12},{... | collective-permute-start | bytes 1277960 | tf_op jit(solution)/shard_map/ppermute | solution.py:322
  25.9 34.0 %copy-start = (bf16[1,2048,1024]{2,1,0:T(8,128)(2,1)}, bf16[1,2048,1024]{2,1,0:T(8,128)(2,1)S(1)}, u32[]{:S(2)}) copy-start(bf16[1,2048,1024]{2,1,0:T(8,128)(2,1)S(1)} %get-tuple-element.104.refs_2_.refs_5_.refs_3_.refs_6_) | copy-start | bytes 12582916
  28.9 18.6 %collective-permute-start.1 = (bf16[208,1024]{1,0:T(8,128)(2,1)S(1)}, bf16[208,1024]{1,0:T(8,128)(2,1)S(1)}, u32[]{:S(2)}, u32[]{:S(2)}) collective-permute-start(bf16[208,1024]{1,0:T(8,128)(2,1)S(1)} %get-tuple-element.102), channel_id=1, source_target_pairs={{0,8},{24,16},{1,9},{25,17},{2,10},{26,18},{3,11},{27,19},{4,12},{... | collective-permute-start | bytes 1277960 | tf_op jit(solution)/shard_map/ppermute | solution.py:322
  32.3 15.2 %collective-permute-start.2 = (bf16[208,1024]{1,0:T(8,128)(2,1)S(1)}, bf16[208,1024]{1,0:T(8,128)(2,1)S(1)}, u32[]{:S(2)}, u32[]{:S(2)}) collective-permute-start(bf16[208,1024]{1,0:T(8,128)(2,1)S(1)} %get-tuple-element.103), channel_id=1, source_target_pairs={{8,16},{16,8},{9,17},{17,9},{10,18},{18,10},{11,19},{19,11},{12,20... | collective-permute-start | bytes 1277960 | tf_op jit(solution)/shard_map/ppermute | solution.py:322
  41.8 18.1 %copy-start.3 = (f32[1,2048,256]{2,1,0:T(8,128)}, f32[1,2048,256]{2,1,0:T(8,128)S(1)}, u32[]{:S(2)}) copy-start(f32[1,2048,256]{2,1,0:T(8,128)S(1)} %get-tuple-element.108.refs_4_.refs_7_.refs_5_.refs_8_) | copy-start | bytes 6291460
  42.5 17.4 %collective-permute-start.6 = (bf16[208,1024]{1,0:T(8,128)(2,1)S(1)}, bf16[208,1024]{1,0:T(8,128)(2,1)S(1)}, u32[]{:S(2)}, u32[]{:S(2)}) collective-permute-start(bf16[208,1024]{1,0:T(8,128)(2,1)S(1)} %get-tuple-element.114), channel_id=1, source_target_pairs={{0,8},{24,16},{1,9},{25,17},{2,10},{26,18},{3,11},{27,19},{4,12},{... | collective-permute-start | bytes 1277960 | tf_op jit(solution)/shard_map/ppermute | solution.py:322
  46.8 13.2 %collective-permute-start.7 = (bf16[208,1024]{1,0:T(8,128)(2,1)S(1)}, bf16[208,1024]{1,0:T(8,128)(2,1)S(1)}, u32[]{:S(2)}, u32[]{:S(2)}) collective-permute-start(bf16[208,1024]{1,0:T(8,128)(2,1)S(1)} %get-tuple-element.115), channel_id=1, source_target_pairs={{8,16},{16,8},{9,17},{17,9},{10,18},{18,10},{11,19},{19,11},{12,20... | collective-permute-start | bytes 1277960 | tf_op jit(solution)/shard_map/ppermute | solution.py:322
  49.5 16.2 %collective-permute-start.4 = (bf16[208,1024]{1,0:T(8,128)(2,1)}, bf16[208,1024]{1,0:T(8,128)(2,1)S(1)}, u32[]{:S(2)}, u32[]{:S(2)}) collective-permute-start(bf16[208,1024]{1,0:T(8,128)(2,1)} %get-tuple-element.112), channel_id=1, source_target_pairs={{0,8},{8,0},{16,24},{24,16},{1,9},{9,1},{17,25},{25,17},{2,10},{10... | collective-permute-start | bytes 1277960 | tf_op jit(solution)/shard_map/ppermute | solution.py:322
  50.9 14.9 %collective-permute-start.5 = (bf16[208,1024]{1,0:T(8,128)(2,1)}, bf16[208,1024]{1,0:T(8,128)(2,1)}, u32[]{:S(2)}, u32[]{:S(2)}) collective-permute-start(bf16[208,1024]{1,0:T(8,128)(2,1)} %get-tuple-element.113), channel_id=1, source_target_pairs={{8,16},{16,8},{9,17},{17,9},{10,18},{18,10},{11,19},{19,11},{12,20... | collective-permute-start | bytes 1277960 | tf_op jit(solution)/shard_map/ppermute | solution.py:322
  62.0 13.0 %collective-permute-start.10 = (bf16[208,1024]{1,0:T(8,128)(2,1)}, bf16[208,1024]{1,0:T(8,128)(2,1)S(1)}, u32[]{:S(2)}, u32[]{:S(2)}) collective-permute-start(bf16[208,1024]{1,0:T(8,128)(2,1)} %get-tuple-element.128), channel_id=1, source_target_pairs={{0,8},{8,0},{16,24},{24,16},{1,9},{9,1},{17,25},{25,17},{2,10},{10... | collective-permute-start | bytes 1277960 | tf_op jit(solution)/shard_map/ppermute | solution.py:322
  64.4 10.7 %collective-permute-start.11 = (bf16[208,1024]{1,0:T(8,128)(2,1)}, bf16[208,1024]{1,0:T(8,128)(2,1)}, u32[]{:S(2)}, u32[]{:S(2)}) collective-permute-start(bf16[208,1024]{1,0:T(8,128)(2,1)} %get-tuple-element.129), channel_id=1, source_target_pairs={{8,16},{16,8},{9,17},{17,9},{10,18},{18,10},{11,19},{19,11},{12,20... | collective-permute-start | bytes 1277960 | tf_op jit(solution)/shard_map/ppermute | solution.py:322
  69.6 5.5 %copy-start.7 = (bf16[208,1024]{1,0:T(8,128)(2,1)S(1)}, bf16[208,1024]{1,0:T(8,128)(2,1)}, u32[]{:S(2)}) copy-start(bf16[208,1024]{1,0:T(8,128)(2,1)} %copy-done.6) | copy-start | bytes 1277956
  72.3 12.3 %collective-permute-start.8 = (bf16[208,1024]{1,0:T(8,128)(2,1)S(1)}, bf16[208,1024]{1,0:T(8,128)(2,1)S(1)}, u32[]{:S(2)}, u32[]{:S(2)}) collective-permute-start(bf16[208,1024]{1,0:T(8,128)(2,1)S(1)} %get-tuple-element.126), channel_id=1, source_target_pairs={{0,8},{8,0},{16,24},{24,16},{1,9},{9,1},{17,25},{25,17},{2,10},{10... | collective-permute-start | bytes 1277960 | tf_op jit(solution)/shard_map/ppermute | solution.py:322
  74.3 10.3 %collective-permute-start.9 = (bf16[208,1024]{1,0:T(8,128)(2,1)S(1)}, bf16[208,1024]{1,0:T(8,128)(2,1)S(1)}, u32[]{:S(2)}, u32[]{:S(2)}) collective-permute-start(bf16[208,1024]{1,0:T(8,128)(2,1)S(1)} %get-tuple-element.127), channel_id=1, source_target_pairs={{8,16},{16,8},{9,17},{17,9},{10,18},{18,10},{11,19},{19,11},{12,20... | collective-permute-start | bytes 1277960 | tf_op jit(solution)/shard_map/ppermute | solution.py:322
  78.3 21.7 %collective-permute-start.14 = (bf16[208,1024]{1,0:T(8,128)(2,1)}, bf16[208,1024]{1,0:T(8,128)(2,1)S(1)}, u32[]{:S(2)}, u32[]{:S(2)}) collective-permute-start(bf16[208,1024]{1,0:T(8,128)(2,1)} %get-tuple-element.142), channel_id=1, source_target_pairs={{0,8},{8,0},{16,24},{24,16},{1,9},{9,1},{17,25},{25,17},{2,10},{10... | collective-permute-start | bytes 1277960 | tf_op jit(solution)/shard_map/ppermute | solution.py:322
  80.8 19.2 %collective-permute-start.15 = (bf16[208,1024]{1,0:T(8,128)(2,1)}, bf16[208,1024]{1,0:T(8,128)(2,1)}, u32[]{:S(2)}, u32[]{:S(2)}) collective-permute-start(bf16[208,1024]{1,0:T(8,128)(2,1)} %get-tuple-element.143), channel_id=1, source_target_pairs={{8,16},{16,8},{9,17},{17,9},{10,18},{18,10},{11,19},{19,11},{12,20... | collective-permute-start | bytes 1277960 | tf_op jit(solution)/shard_map/ppermute | solution.py:322
  86.6 18.2 %collective-permute-start.12 = (bf16[208,1024]{1,0:T(8,128)(2,1)}, bf16[208,1024]{1,0:T(8,128)(2,1)S(1)}, u32[]{:S(2)}, u32[]{:S(2)}) collective-permute-start(bf16[208,1024]{1,0:T(8,128)(2,1)} %get-tuple-element.140), channel_id=1, source_target_pairs={{0,8},{8,0},{16,24},{24,16},{1,9},{9,1},{17,25},{25,17},{2,10},{10... | collective-permute-start | bytes 1277960 | tf_op jit(solution)/shard_map/ppermute | solution.py:322
  90.2 14.7 %collective-permute-start.13 = (bf16[208,1024]{1,0:T(8,128)(2,1)}, bf16[208,1024]{1,0:T(8,128)(2,1)}, u32[]{:S(2)}, u32[]{:S(2)}) collective-permute-start(bf16[208,1024]{1,0:T(8,128)(2,1)} %get-tuple-element.141), channel_id=1, source_target_pairs={{8,16},{16,8},{9,17},{17,9},{10,18},{18,10},{11,19},{19,11},{12,20... | collective-permute-start | bytes 1277960 | tf_op jit(solution)/shard_map/ppermute | solution.py:322
  91.6 8.4 %copy-start.2 = (bf16[1,2048,1024]{2,1,0:T(8,128)(2,1)S(1)}, bf16[1,2048,1024]{2,1,0:T(8,128)(2,1)}, u32[]{:S(2)}) copy-start(bf16[1,2048,1024]{2,1,0:T(8,128)(2,1)} %copy-done) | copy-start | bytes 12582916
  91.6 8.4 %copy-start.5 = (f32[1,2048,256]{2,1,0:T(8,128)S(1)}, f32[1,2048,256]{2,1,0:T(8,128)}, u32[]{:S(2)}) copy-start(f32[1,2048,256]{2,1,0:T(8,128)} %copy-done.3) | copy-start | bytes 6291460
  100.0 4.9 %copy-start.9 = (bf16[208,1024]{1,0:T(8,128)(2,1)S(1)}, bf16[208,1024]{1,0:T(8,128)(2,1)}, u32[]{:S(2)}) copy-start(bf16[208,1024]{1,0:T(8,128)(2,1)} %copy-done.8) | copy-start | bytes 1277956
  102.7 12.4 %collective-permute-start.18 = (bf16[208,1024]{1,0:T(8,128)(2,1)S(1)}, bf16[208,1024]{1,0:T(8,128)(2,1)S(1)}, u32[]{:S(2)}, u32[]{:S(2)}) collective-permute-start(bf16[208,1024]{1,0:T(8,128)(2,1)S(1)} %get-tuple-element.154), channel_id=1, source_target_pairs={{0,8},{8,0},{16,24},{24,16},{1,9},{9,1},{17,25},{25,17},{2,10},{10... | collective-permute-start | bytes 1277960 | tf_op jit(solution)/shard_map/ppermute | solution.py:322
  104.2 11.0 %collective-permute-start.19 = (bf16[208,1024]{1,0:T(8,128)(2,1)S(1)}, bf16[208,1024]{1,0:T(8,128)(2,1)S(1)}, u32[]{:S(2)}, u32[]{:S(2)}) collective-permute-start(bf16[208,1024]{1,0:T(8,128)(2,1)S(1)} %get-tuple-element.155), channel_id=1, source_target_pairs={{8,16},{16,8},{9,17},{17,9},{10,18},{18,10},{11,19},{19,11},{12,20... | collective-permute-start | bytes 1277960 | tf_op jit(solution)/shard_map/ppermute | solution.py:322
  107.6 14.4 %collective-permute-start.16 = (bf16[208,1024]{1,0:T(8,128)(2,1)S(1)}, bf16[208,1024]{1,0:T(8,128)(2,1)S(1)}, u32[]{:S(2)}, u32[]{:S(2)}) collective-permute-start(bf16[208,1024]{1,0:T(8,128)(2,1)S(1)} %get-tuple-element.152), channel_id=1, source_target_pairs={{8,0},{16,24},{9,1},{17,25},{10,2},{18,26},{11,3},{19,27},{12,4},{... | collective-permute-start | bytes 1277960 | tf_op jit(solution)/shard_map/ppermute | solution.py:322
  108.9 13.1 %collective-permute-start.17 = (bf16[208,1024]{1,0:T(8,128)(2,1)S(1)}, bf16[208,1024]{1,0:T(8,128)(2,1)S(1)}, u32[]{:S(2)}, u32[]{:S(2)}) collective-permute-start(bf16[208,1024]{1,0:T(8,128)(2,1)S(1)} %get-tuple-element.153), channel_id=1, source_target_pairs={{8,16},{16,8},{9,17},{17,9},{10,18},{18,10},{11,19},{19,11},{12,20... | collective-permute-start | bytes 1277960 | tf_op jit(solution)/shard_map/ppermute | solution.py:322
  116.9 18.2 %collective-permute-start.20 = (bf16[208,1024]{1,0:T(8,128)(2,1)S(1)}, bf16[208,1024]{1,0:T(8,128)(2,1)S(1)}, u32[]{:S(2)}, u32[]{:S(2)}) collective-permute-start(bf16[208,1024]{1,0:T(8,128)(2,1)S(1)} %get-tuple-element.170), channel_id=1, source_target_pairs={{8,0},{16,24},{9,1},{17,25},{10,2},{18,26},{11,3},{19,27},{12,4},{... | collective-permute-start | bytes 1277960 | tf_op jit(solution)/shard_map/ppermute | solution.py:322
  118.2 16.9 %collective-permute-start.21 = (bf16[208,1024]{1,0:T(8,128)(2,1)S(1)}, bf16[208,1024]{1,0:T(8,128)(2,1)S(1)}, u32[]{:S(2)}, u32[]{:S(2)}) collective-permute-start(bf16[208,1024]{1,0:T(8,128)(2,1)S(1)} %get-tuple-element.171), channel_id=1, source_target_pairs={{8,16},{16,8},{9,17},{17,9},{10,18},{18,10},{11,19},{19,11},{12,20... | collective-permute-start | bytes 1277960 | tf_op jit(solution)/shard_map/ppermute | solution.py:322
  123.8 16.3 %collective-permute-start.23 = (bf16[208,1024]{1,0:T(8,128)(2,1)S(1)}, bf16[208,1024]{1,0:T(8,128)(2,1)S(1)}, u32[]{:S(2)}, u32[]{:S(2)}) collective-permute-start(bf16[208,1024]{1,0:T(8,128)(2,1)S(1)} %get-tuple-element.177), channel_id=1, source_target_pairs={{8,0},{16,24},{9,1},{17,25},{10,2},{18,26},{11,3},{19,27},{12,4},{... | collective-permute-start | bytes 1277960 | tf_op jit(solution)/shard_map/ppermute | solution.py:322
  136.8 11.3 %collective-permute-start.22 = (bf16[208,1024]{1,0:T(8,128)(2,1)S(1)}, bf16[208,1024]{1,0:T(8,128)(2,1)S(1)}, u32[]{:S(2)}, u32[]{:S(2)}) collective-permute-start(bf16[208,1024]{1,0:T(8,128)(2,1)S(1)} %get-tuple-element.176), channel_id=1, source_target_pairs={{8,0},{16,24},{9,1},{17,25},{10,2},{18,26},{11,3},{19,27},{12,4},{... | collective-permute-start | bytes 1277960 | tf_op jit(solution)/shard_map/ppermute | solution.py:322
  (4 other events, 7.8 us)
Sparse Core Ops, SparseCore 0:
  9.9 57.0 all-gather.2
  70.5 71.2 reduce-scatter.1
